TPU v7x, 32 devices: a whole 2x2x4 slice. The times are simulated.
32 devices in a mesh: seq: 8 (over z, y), ex: 4 (over x, core).
Axes of the slice: x: 2, y: 2, z: 4, core: 2. Of those that a mesh axis runs over, the one named last changes fastest.
Arguments:
- block_input: float32 [16, 1024, 768], P('ex', 'seq'), may hold values from -6 to 6
- segment_ids: int32 [16, 1024], P('ex'), may hold values from 0 to 1, as said below
- expert_ids: int32 [16, 1024, 1], P('ex', 'seq'), may hold values from 0 to 3; in each aligned block of 128 rows (0 to 127, 128 to 255, ..., all dimensions but the last counted through in order) at most 48 rows name the same one
- ln1_gain: float32 [768], replicated, may hold values from 0.5 to 1.5
- ln1_bias: float32 [768], replicated, may hold values from -1 to 1
- ln2_gain: float32 [768], replicated, may hold values from 0.5 to 1.5
- ln2_bias: float32 [768], replicated, may hold values from -1 to 1
- w_qkv: bfloat16 [768, 2304], replicated, may hold values from -0.3125 to 0.3125
- w_attn_out: bfloat16 [768, 768], replicated, may hold values from -1.75 to 1.75
- w_in: bfloat16 [4, 768, 3072], P('ex'), may hold values from -0.21875 to 0.21875
- w_down: bfloat16 [4, 3072, 768], P('ex'), may hold values from -0.15625 to 0.15625
- grad_out: float32 [16, 1024, 768], P('ex', 'seq'), may hold values from -6 to 6
Outputs:
- block_output: float32 [16, 1024, 768], P('ex', 'seq')
- grad_input: float32 [16, 1024, 768], P('ex', 'seq')
- grad_w_qkv: float32 [768, 2304], replicated
- grad_w_attn_out: float32 [768, 768], replicated
- grad_ln1_gain: float32 [768], replicated
- grad_ln1_bias: float32 [768], replicated
- grad_ln2_gain: float32 [768], replicated
- grad_ln2_bias: float32 [768], replicated
- grad_w_in: float32 [4, 768, 3072], P('ex')
- grad_w_down: float32 [4, 3072, 768], P('ex')
- expert_load: float32 [4], replicated
Inputs may be any that keep to these rules, and one draw needn't show every extreme that they name: `segment_ids`: Non-decreasing along each row and starting at 0; in each aligned group of 4 rows one row is a single document. `expert_ids`: in each aligned block of 128 positions of a row (the positions of one device in that row) at most 48 tokens name one expert.
All inputs are finite; a program needn't handle non-finite values.
Results may differ from a plain program's by a relative error of at most 0.04.
Values may be sent and summed in bfloat16 or wider, within the bound.
No kernel may reach another device: no remote copies, remote signals or barrier semaphores. Data moves between devices by JAX's collectives and lax.ppermute only.
A program may use at most 320 MiB of HBM per device.

v0:
```python
import math

import jax
import jax.numpy as jnp
from jax import lax
from jax.sharding import PartitionSpec as P

HEADS = 12
HEAD = 64
MOST = 48


EPSILON = 1e-05
NEGATIVE = -1e30


def layer_norm(value, gain, bias):
    center = value - jnp.mean(value, -1, keepdims=True)
    spread = jnp.mean(center * center, -1, keepdims=True)
    return center * lax.rsqrt(spread + EPSILON) * gain + bias


def permitted(query_pos, query_seg, key_pos, key_seg):
    causal = key_pos[None, None, None, :] <= query_pos[None, None, :, None]
    same = key_seg[:, None, None, :] == query_seg[:, None, :, None]
    return causal & same


def walk(carry, pieces, segments, step):
    length = pieces[0].shape[1]
    block = math.gcd(length, 512)

    def advance(index, state):
        first = index * block
        parts = tuple(
            (lax.dynamic_slice_in_dim(piece, index * block, block, 1) for piece in pieces)
        )
        position = first + jnp.arange(block, dtype=jnp.int32)
        labels = lax.dynamic_slice_in_dim(segments, first, block, 1)
        return step(state, parts, first, position, labels)

    return lax.fori_loop(0, length // block, advance, carry)


def per_device(
    block_input,
    segment_ids,
    expert_ids,
    ln1_gain,
    ln1_bias,
    ln2_gain,
    ln2_bias,
    w_qkv,
    w_attn_out,
    w_in,
    w_down,
    grad_out,
):
    rows, local, width = block_input.shape
    scale = HEAD ** (-0.5)
    experts = lax.axis_size("ex")
    own_pos = lax.axis_index("seq") * local + jnp.arange(local, dtype=jnp.int32)
    own_seg = lax.dynamic_slice_in_dim(segment_ids, lax.axis_index("seq") * local, local, 1)

    def split(value):
        return value.reshape(value.shape[0], value.shape[1], HEADS, HEAD)

    normed_one, norm_one_back = jax.vjp(layer_norm, block_input, ln1_gain, ln1_bias)
    normed_one = normed_one.astype(jnp.bfloat16)
    projected = jnp.einsum(
        "rsd,de->rse", normed_one, w_qkv, preferred_element_type=jnp.float32
    ).astype(jnp.bfloat16)
    queries = projected[..., :width]
    keys = projected[..., width : 2 * width]
    values = projected[..., 2 * width :]
    query_heads = split(queries)
    key_heads = split(keys)
    value_heads = split(values)

    def forward_step(state, parts, first, position, labels):
        high, total, summed = state
        key_part = split(parts[0])
        value_part = split(parts[1])
        scores = (
            jnp.einsum("rqhd,rkhd->rhqk", query_heads, key_part, preferred_element_type=jnp.float32)
            * scale
        )
        allowed = permitted(own_pos, own_seg, position, labels)
        scores = jnp.where(allowed, scores, NEGATIVE)
        new_high = jnp.maximum(high, jnp.max(scores, -1))
        fade = jnp.exp(high - new_high)
        weights = jnp.where(allowed, jnp.exp(scores - new_high[..., None]), 0.0)
        total = total * fade + jnp.sum(weights, -1)
        summed = summed * jnp.swapaxes(fade, 1, 2)[..., None] + jnp.einsum(
            "rhqk,rkhd->rqhd",
            weights.astype(jnp.bfloat16),
            value_part,
            preferred_element_type=jnp.float32,
        )
        return (new_high, total, summed)

    start_state = (
        jnp.full((rows, HEADS, local), NEGATIVE, jnp.float32),
        jnp.zeros((rows, HEADS, local), jnp.float32),
        jnp.zeros((rows, local, HEADS, HEAD), jnp.float32),
    )
    high, total, summed = walk(
        start_state,
        (
            lax.all_gather(keys, "seq", axis=1, tiled=True),
            lax.all_gather(values, "seq", axis=1, tiled=True),
        ),
        segment_ids,
        forward_step,
    )
    log_total = high + jnp.log(total)
    attended = (summed / jnp.swapaxes(total, 1, 2)[..., None]).reshape(rows, local, width)
    attended_low = attended.astype(jnp.bfloat16)
    branch = jnp.einsum("rsd,de->rse", attended_low, w_attn_out, preferred_element_type=jnp.float32)
    middle = block_input + branch
    normed_two, norm_two_back = jax.vjp(layer_norm, middle, ln2_gain, ln2_bias)
    normed_two = normed_two.astype(jnp.bfloat16)
    chosen = expert_ids[..., 0]
    onehot = (chosen[..., None] == jnp.arange(experts, dtype=jnp.int32)).astype(jnp.int32)
    rank = jnp.cumsum(onehot, 1) - onehot
    target = chosen * MOST + jnp.sum(rank * onehot, -1)
    route = (
        (target[:, None, :] == jnp.arange(experts * MOST, dtype=jnp.int32)[None, :, None])
        .astype(jnp.bfloat16)
        .reshape(rows, experts, MOST, local)
    )
    outgoing = (
        jnp.einsum("remt,rtd->ermd", route, normed_two, preferred_element_type=jnp.float32)
        .astype(jnp.bfloat16)
        .reshape(experts, rows * MOST, width)
    )
    counts = jnp.sum(onehot.astype(jnp.float32), (0, 1))
    inner_weight = w_in[0]
    outer_weight = w_down[0]
    arrived = lax.all_to_all(outgoing, "ex", split_axis=0, concat_axis=0, tiled=True)
    flat = arrived.reshape(-1, width)
    inner = jnp.dot(flat, inner_weight, preferred_element_type=jnp.float32)
    active = jax.nn.gelu(inner).astype(jnp.bfloat16)
    result = jnp.dot(active, outer_weight, preferred_element_type=jnp.float32).astype(jnp.bfloat16)
    produced, inner_kept, arrived = (
        result.reshape(arrived.shape),
        inner.reshape(arrived.shape[0], arrived.shape[1], -1),
        arrived,
    )
    returned = lax.all_to_all(produced, "ex", split_axis=0, concat_axis=0, tiled=True)
    expert_part = jnp.einsum(
        "remt,ermd->rtd",
        route,
        returned.reshape(experts, rows, MOST, width),
        preferred_element_type=jnp.float32,
    )
    block_output = middle + expert_part
    out_low = grad_out.astype(jnp.bfloat16)
    grad_send = (
        jnp.einsum("remt,rtd->ermd", route, out_low, preferred_element_type=jnp.float32)
        .astype(jnp.bfloat16)
        .reshape(experts, rows * MOST, width)
    )
    grad_arrived = lax.all_to_all(grad_send, "ex", split_axis=0, concat_axis=0, tiled=True).reshape(
        -1, width
    )
    inner_flat = inner_kept.reshape(-1, inner_kept.shape[-1])
    active, gelu_back = jax.vjp(jax.nn.gelu, inner_flat)
    active = active.astype(jnp.bfloat16)
    grad_down = jnp.einsum("nf,nd->fd", active, grad_arrived, preferred_element_type=jnp.float32)
    grad_active = jnp.einsum(
        "nd,fd->nf", grad_arrived, outer_weight, preferred_element_type=jnp.float32
    )
    grad_inner = gelu_back(grad_active)[0].astype(jnp.bfloat16)
    grad_up = jnp.einsum(
        "nd,nf->df", arrived.reshape(-1, width), grad_inner, preferred_element_type=jnp.float32
    )
    grad_rows = (
        jnp.einsum("nf,df->nd", grad_inner, inner_weight, preferred_element_type=jnp.float32)
        .astype(jnp.bfloat16)
        .reshape(arrived.shape)
    )
    grad_back = lax.all_to_all(grad_rows, "ex", split_axis=0, concat_axis=0, tiled=True)
    grad_normed_two = jnp.einsum(
        "remt,ermd->rtd",
        route,
        grad_back.reshape(experts, rows, MOST, width),
        preferred_element_type=jnp.float32,
    )
    grad_middle, grad_gain_two, grad_bias_two = norm_two_back(grad_normed_two)
    grad_middle = grad_middle + grad_out
    grad_branch = grad_middle.astype(jnp.bfloat16)
    grad_attn_out = jnp.einsum(
        "rsd,rse->de", attended_low, grad_branch, preferred_element_type=jnp.float32
    )
    grad_attended = jnp.einsum(
        "rse,de->rsd", grad_branch, w_attn_out, preferred_element_type=jnp.float32
    ).astype(jnp.bfloat16)
    grad_heads = split(grad_attended)
    delta = jnp.swapaxes(jnp.sum(grad_heads.astype(jnp.float32) * split(attended), -1), 1, 2)

    def query_step(state, parts, first, position, labels):
        key_part = split(parts[0])
        value_part = split(parts[1])
        scores = (
            jnp.einsum("rqhd,rkhd->rhqk", query_heads, key_part, preferred_element_type=jnp.float32)
            * scale
        )
        allowed = permitted(own_pos, own_seg, position, labels)
        probs = jnp.where(allowed, jnp.exp(scores - log_total[..., None]), 0.0)
        grad_probs = jnp.einsum(
            "rqhd,rkhd->rhqk", grad_heads, value_part, preferred_element_type=jnp.float32
        )
        grad_scores = (probs * (grad_probs - delta[..., None])).astype(jnp.bfloat16)
        return (
            state
            + jnp.einsum(
                "rhqk,rkhd->rqhd", grad_scores, key_part, preferred_element_type=jnp.float32
            )
            * scale
        )

    zero_heads = jnp.zeros((rows, local, HEADS, HEAD), jnp.float32)
    grad_queries = walk(
        zero_heads,
        (
            lax.all_gather(keys, "seq", axis=1, tiled=True),
            lax.all_gather(values, "seq", axis=1, tiled=True),
        ),
        segment_ids,
        query_step,
    )
    log_all, delta_all = (
        lax.all_gather(log_total.astype(jnp.bfloat16), "seq", axis=2, tiled=True).astype(
            log_total.dtype
        ),
        lax.all_gather(delta.astype(jnp.bfloat16), "seq", axis=2, tiled=True).astype(delta.dtype),
    )

    def key_step(state, parts, first, position, labels):
        grad_keys, grad_values = state
        query_part = split(parts[0])
        grad_part = split(parts[1])
        block = parts[0].shape[1]
        log_part = lax.dynamic_slice_in_dim(log_all, first, block, 2)
        delta_part = lax.dynamic_slice_in_dim(delta_all, first, block, 2)
        scores = (
            jnp.einsum("rqhd,rkhd->rhqk", query_part, key_heads, preferred_element_type=jnp.float32)
            * scale
        )
        allowed = permitted(position, labels, own_pos, own_seg)
        probs = jnp.where(allowed, jnp.exp(scores - log_part[..., None]), 0.0)
        grad_values = grad_values + jnp.einsum(
            "rhqk,rqhd->rkhd",
            probs.astype(jnp.bfloat16),
            grad_part,
            preferred_element_type=jnp.float32,
        )
        grad_probs = jnp.einsum(
            "rqhd,rkhd->rhqk", grad_part, value_heads, preferred_element_type=jnp.float32
        )
        grad_scores = (probs * (grad_probs - delta_part[..., None])).astype(jnp.bfloat16)
        grad_keys = (
            grad_keys
            + jnp.einsum(
                "rhqk,rqhd->rkhd", grad_scores, query_part, preferred_element_type=jnp.float32
            )
            * scale
        )
        return (grad_keys, grad_values)

    grad_keys, grad_values = walk(
        (zero_heads, zero_heads),
        (
            lax.all_gather(queries, "seq", axis=1, tiled=True),
            lax.all_gather(grad_attended, "seq", axis=1, tiled=True),
        ),
        segment_ids,
        key_step,
    )
    grad_projected = jnp.concatenate(
        [
            grad_queries.reshape(rows, local, width),
            grad_keys.reshape(rows, local, width),
            grad_values.reshape(rows, local, width),
        ],
        -1,
    ).astype(jnp.bfloat16)
    grad_qkv = jnp.einsum(
        "rsd,rse->de", normed_one, grad_projected, preferred_element_type=jnp.float32
    )
    grad_normed_one = jnp.einsum(
        "rse,de->rsd", grad_projected, w_qkv, preferred_element_type=jnp.float32
    )
    grad_total, grad_gain_one, grad_bias_one = norm_one_back(grad_normed_one)
    grad_total = grad_total + grad_middle
    summed_grads = lax.psum(
        (
            grad_qkv,
            grad_attn_out,
            grad_gain_one,
            grad_bias_one,
            grad_gain_two,
            grad_bias_two,
            counts,
        ),
        ("seq", "ex"),
    )
    expert_grads = (
        lax.psum(grad_up.astype(jnp.bfloat16), "seq").astype(jnp.float32),
        lax.psum(grad_down.astype(jnp.bfloat16), "seq").astype(jnp.float32),
    )
    tokens_all = rows * local * lax.axis_size("seq") * experts
    load = summed_grads[6] * (experts / tokens_all)
    return (
        block_output,
        grad_total,
        summed_grads[0],
        summed_grads[1],
        summed_grads[2],
        summed_grads[3],
        summed_grads[4],
        summed_grads[5],
        expert_grads[0][None],
        expert_grads[1][None],
        load,
    )


def solution(mesh):
    return jax.shard_map(
        per_device,
        mesh=mesh,
        in_specs=(
            P("ex", "seq", None),
            P("ex", None),
            P("ex", "seq", None),
            P(),
            P(),
            P(),
            P(),
            P(),
            P(),
            P("ex", None, None),
            P("ex", None, None),
            P("ex", "seq", None),
        ),
        out_specs=(
            P("ex", "seq", None),
            P("ex", "seq", None),
            P(),
            P(),
            P(),
            P(),
            P(),
            P(),
            P("ex", None, None),
            P("ex", None, None),
            P(),
        ),
        check_vma=False,
    )
```

profile of v0, /device:TPU:0, one launch (start us, length us, event | category | flops | bytes accessed | tf_op | source)
XLA Modules:
  0.0 964.4 jit_solution(8683646888571612052)
XLA Ops:
  11.3 3.5 convolution_convert_fusion.2
  27.3 91.0 %all-gather.7.cloned.1.call-done = bf16[4,1024,768]{2,1,0:T(8,128)(2,1)} async-done(((bf16[4,128,768]{2,1,0:T(8,128)(2,1)}), bf16[4,1024,768]{2,1,0:T(8,128)(2,1)}) %all-gather.7.cloned.1.call-update) | async-done | bytes 6291472 | tf_op jit(solution)/shard_map/all_gather | solution.py:111
  118.3 8.6 copy.41
  126.9 90.8 %all-gather.5.cloned.1.call-done = bf16[4,1024,768]{2,1,0:T(8,128)(2,1)} async-done(((bf16[4,128,768]{2,1,0:T(8,128)(2,1)}), bf16[4,1024,768]{2,1,0:T(8,128)(2,1)}) %all-gather.5.cloned.1.call-update) | async-done | bytes 6291472 | tf_op jit(solution)/shard_map/all_gather | solution.py:110
  217.7 8.6 copy.40
  226.4 30.7 %while.48 = (s32[]{:T(128)}, f32[4,12,128]{2,1,0:T(8,128)}, f32[4,12,128]{2,1,0:T(8,128)}, f32[4,128,12,64]{1,3,2,0:T(8,128)}, s32[4,1024]{1,0:T(4,128)S(1)}, /*...) while((s32[]{:T(128)}, f32[4,12,128]{2,1,0:T(8,128)}, ...), condition=%wide.region_5.6_spmd.clone, body=%wide.region_2.5_spmd.clone.sunk | while | flops 848007808 | bytes 78183808 | solution.py:42
  227.6 3.6 constant_dynamic-slice_fusion.20
  231.2 2.6 fusion.174
  233.9 3.9 bitcast_add_fusion.9
  237.8 3.2 fusion.176
  242.9 3.6 constant_dynamic-slice_fusion.20
  246.6 2.6 fusion.174
  249.3 3.9 bitcast_add_fusion.9
  253.2 3.2 fusion.176
  264.2 4.3 all-to-all-start
  271.6 12.9 %all-to-all-done = bf16[4,192,768]{2,1,0:T(8,128)(2,1)} async-done(((bf16[4,192,768]{2,1,0:T(8,128)(2,1)}), bf16[4,192,768]{2,1,0:T(8,128)(2,1)}, u32[]{:S(2)}, u32[]{:S(2)}) %all-to-all-start) | async-done | bytes 1179680 | tf_op jit(solution)/shard_map/all_to_all | solution.py:140
  284.4 4.3 all-to-all-start.2
  289.0 10.3 %fusion.69 = f32[768,3072]{1,0:T(8,128)} fusion(bf16[768,768]{1,0:T(8,128)(2,1)} %bitcast.10, bf16[1,768,3072]{2,1,0:T(8,128)(2,1)} %param.27), kind=kOutput, calls=%fused_computation.92 | convolution fusion | flops 3623878656 | bytes 15335424 | tf_op jit(solution)/shard_map/dot_general | solution.py:142
  299.3 5.4 all-to-all-done.2
  304.6 12.0 %fusion.62 = bf16[768,3072]{1,0:T(8,128)(2,1)S(1)} fusion(f32[768,3072]{1,0:T(8,128)} %fusion.69, bf16[768,768]{1,0:T(8,128)(2,1)} %bitcast.21, bf16[1,3072,768]{2,1,0:T(8,128)(2,1)} %param.28), kind=kOutput, calls=%fused_computation.81 | convolution fusion | flops 3671064576 | bytes 20054016 | tf_op jit(solution)/shard_map/nd,fd->nf/dot_general | solution.py:171
  316.7 7.9 fusion.79
  324.7 18.4 %all_to_all.20 = bf16[4,192,768]{2,1,0:T(8,128)(2,1)S(1)} all-to-all(bf16[4,192,768]{2,1,0:T(8,128)(2,1)S(1)} %bitcast.230), channel_id=1, replica_groups=mesh['seq'=8,'ex'=4] {'ex'}, dimensions={0} | all-to-all | bytes 2359296 | tf_op jit(solution)/shard_map/all_to_all | solution.py:183
  354.0 3.5 copy.49
  357.5 3.4 copy.56
  362.3 27.0 %all_gather.23 = bf16[4,12,1024]{2,1,0:T(8,128)(2,1)S(1)} all-gather(bf16[4,12,128]{2,1,0:T(8,128)(2,1)S(1)} %get-tuple-element.841), channel_id=1, replica_groups=mesh['seq'=8,'ex'=4] {'seq'}, dimensions={2}, use_global_device_ids=true | all-gather | bytes 110592 | tf_op jit(solution)/shard_map/all_gather | solution.py:234
  390.0 9.5 fusion.71
  399.5 9.7 %fusion.72 = bf16[1,3072,768]{2,1,0:T(8,128)(2,1)} fusion(bf16[768,768]{1,0:T(8,128)(2,1)} %bitcast.21, f32[768,3072]{1,0:T(8,128)} %fusion.69), kind=kOutput, calls=%fused_computation.95 | convolution fusion | flops 3647471616 | bytes 15335424 | tf_op jit(solution)/shard_map/nf,nd->fd/dot_general | solution.py:170
  409.4 3.6 convolution_bitcast_fusion.1
  415.2 2.6 multiply_reduce_fusion.2
  417.8 3.4 copy.51
  422.6 53.4 %while.49 = (s32[]{:T(128)}, f32[4,128,12,64]{1,3,2,0:T(8,128)}, bf16[4,1024,768]{1,2,0:T(8,128)(2,1)}, s32[4,1024]{1,0:T(4,128)S(1)}, s32[4,128]{1,0:T(4,128)},...) while((s32[]{:T(128)}, f32[4,128,12,64]{1,3,2,0:T(8,128)}, ...), condition=%wide.region_14.15_spmd.clone, body=%wide.region_13.14_spmd.clone.sunk | while | flops 1228604032 | bytes 68369680 | solution.py:42
  424.4 5.4 constant_dynamic-slice_fusion.21
  431.4 6.3 fusion.184
  437.7 11.4 %bitcast_add_fusion.10 = f32[4,128,12,64]{1,3,2,0:T(8,128)} fusion(f32[4,128,12,64]{1,3,2,0:T(8,128)} %get-tuple-element.1191, bf16[4,512,12,64]{1,3,2,0:T(8,128)(2,1)} %bitcast.209, f32[4,12,512,128]{2,3,1,0:T(8,128)} %fusion.184, f32[4,12,128]{2,1,0:T(8,128)} %get-tuple-element.1214, f32[4,12,128]{2,1,0:T(8,128)} %get-tuple-element.1211, ...), kind=kOutput, calls=%fused_computation.33.clone.1 | convolution fusion | flops 825360384 | bytes 23117824 | tf_op jit(solution)/shard_map/while/body/eval_jaxpr/rhqk,rkhd->rqhd/dot_general | solution.py:217
  450.9 5.4 constant_dynamic-slice_fusion.21
  457.9 6.3 fusion.184
  464.2 11.8 %bitcast_add_fusion.10 = f32[4,128,12,64]{1,3,2,0:T(8,128)} fusion(f32[4,128,12,64]{1,3,2,0:T(8,128)} %get-tuple-element.1191, bf16[4,512,12,64]{1,3,2,0:T(8,128)(2,1)} %bitcast.209, f32[4,12,512,128]{2,3,1,0:T(8,128)} %fusion.184, f32[4,12,128]{2,1,0:T(8,128)} %get-tuple-element.1214, f32[4,12,128]{2,1,0:T(8,128)} %get-tuple-element.1211, ...), kind=kOutput, calls=%fused_computation.33.clone.1 | convolution fusion | flops 825360384 | bytes 23117824 | tf_op jit(solution)/shard_map/while/body/eval_jaxpr/rhqk,rkhd->rqhd/dot_general | solution.py:217
  476.0 28.9 %all_gather.25 = bf16[4,12,1024]{2,1,0:T(8,128)(2,1)S(1)} all-gather(bf16[4,12,128]{2,1,0:T(8,128)(2,1)} %bitcast_convert_fusion), channel_id=1, replica_groups=mesh['seq'=8,'ex'=4] {'seq'}, dimensions={2}, use_global_device_ids=true | all-gather | bytes 110592 | tf_op jit(solution)/shard_map/all_gather | solution.py:237
  510.4 102.4 %while.50 = (s32[]{:T(128)}, f32[4,128,12,64]{1,3,2,0:T(8,128)}, f32[4,128,12,64]{1,3,2,0:T(8,128)}, bf16[4,1024,768]{2,1,0:T(8,128)(2,1)}, s32[4,128]{1,0:T(4,1...) while((s32[]{:T(128)}, f32[4,128,12,64]{1,3,2,0:T(8,128)}, ...), condition=%wide.region_16.17_spmd.clone, body=%wide.region_15.16_spmd.clone.sunk | while | flops 1644626560 | bytes 84999400 | solution.py:42
  513.9 6.0 constant_dynamic-slice_fusion.23
  519.9 4.7 copy.99
  524.6 4.7 copy.100
  529.3 8.5 fusion.192
  537.7 13.9 %bitcast_add_fusion.11 = f32[4,128,12,64]{1,3,2,0:T(8,128)} fusion(f32[4,128,12,64]{1,3,2,0:T(8,128)} %get-tuple-element.1144, bf16[4,512,12,64]{1,3,2,0:T(8,128)(2,1)} %bitcast.206, f32[4,12,512,128]{3,2,1,0:T(8,128)} %fusion.192, f32[4,12,512]{2,1,0:T(8,128)} %get-tuple-element.1082, f32[4,12,512]{2,1,0:T(8,128)} %get-tuple-element.1083, ...), kind=kOutput, calls=%fused_computation.58.clone.1 | convolution fusion | flops 825360384 | bytes 23265280 | tf_op jit(solution)/shard_map/while/body/eval_jaxpr/rhqk,rqhd->rkhd/dot_general | solution.py:265
  551.6 8.9 bitcast_add_fusion.12
  564.1 6.2 constant_dynamic-slice_fusion.23
  570.3 4.7 copy.99
  575.0 4.6 copy.100
  579.6 8.5 fusion.192
  588.1 14.4 %bitcast_add_fusion.11 = f32[4,128,12,64]{1,3,2,0:T(8,128)} fusion(f32[4,128,12,64]{1,3,2,0:T(8,128)} %get-tuple-element.1144, bf16[4,512,12,64]{1,3,2,0:T(8,128)(2,1)} %bitcast.206, f32[4,12,512,128]{3,2,1,0:T(8,128)} %fusion.192, f32[4,12,512]{2,1,0:T(8,128)} %get-tuple-element.1082, f32[4,12,512]{2,1,0:T(8,128)} %get-tuple-element.1083, ...), kind=kOutput, calls=%fused_computation.58.clone.1 | convolution fusion | flops 825360384 | bytes 23265280 | tf_op jit(solution)/shard_map/while/body/eval_jaxpr/rhqk,rqhd->rkhd/dot_general | solution.py:265
  602.5 10.0 %bitcast_add_fusion.12 = f32[4,128,12,64]{1,3,2,0:T(8,128)} fusion(f32[4,128,12,64]{1,3,2,0:T(8,128)} %get-tuple-element.1145, bf16[4,512,12,64]{1,3,2,0:T(8,128)(2,1)} %bitcast.211, f32[4,12,512,128]{3,2,1,0:T(8,128)} %fusion.192, f32[4,12,512]{2,1,0:T(8,128)} %get-tuple-element.1083, pred[4,512,128]{2,1,0:T(8,128)(4,1)} %compare_and_fusion.8, ...), kind=kOutput, calls=%fused_computation.57.clone.1 | convolution fusion | flops 416022528 | bytes 19234816 | tf_op jit(solution)/shard_map/while/body/eval_jaxpr/rhqk,rqhd->rkhd/dot_general | solution.py:253
  622.3 7.3 convolution_bitcast_fusion
  629.6 11.6 %fusion.82 = bf16[768,768]{1,0:T(8,128)(2,1)} fusion(bf16[1,3072,768]{2,1,0:T(8,128)(2,1)} %param.28, f32[768,3072]{1,0:T(8,128)} %fusion.69), kind=kOutput, calls=%fused_computation.122 | convolution fusion | flops 3645702144 | bytes 15335424 | tf_op jit(solution)/shard_map/dot_general | solution.py:144
  641.1 4.7 all-to-all-start.1
  647.2 14.6 %all-to-all-done.1 = bf16[4,192,768]{2,1,0:T(8,128)(2,1)} async-done(((bf16[4,192,768]{2,1,0:T(8,128)(2,1)}), bf16[4,192,768]{2,1,0:T(8,128)(2,1)}, u32[]{:S(2)}, u32[]{:S(2)}) %all-to-all-start.1) | async-done | bytes 1179680 | tf_op jit(solution)/shard_map/all_to_all | solution.py:150
  661.8 3.4 bitcast_add_fusion.4
  665.2 86.4 %all-reduce.8.cloned.1.call-done = (bf16[1,768,3072]{2,1,0:T(8,128)(2,1)}, bf16[1,3072,768]{2,1,0:T(8,128)(2,1)}) async-done(((bf16[1,768,3072]{2,1,0:T(8,128)(2,1)}, bf16[1,3072,768]{2,1,0:T(8,128)(2,1)}), (bf16[1,768,3072]{2,1,0:T(8,128)(2,1)}, bf16[1,3072,768]{2,1,0:T(8,128)(2,1)})) %all-reduce.8.cloned.1.call-update) | async-done | bytes 9437200 | tf_op jit(solution)/shard_map/psum | solution.py:310
  751.6 7.5 broadcast_in_dim.187
  759.1 5.7 broadcast_in_dim.189
  764.8 2.7 fusion.120
  768.9 41.0 %all-reduce = (f32[768]{0:T(1024)}, f32[768]{0:T(1024)}, f32[768]{0:T(1024)}, f32[768]{0:T(1024)}, f32[4]{0:T(128)}) all-reduce(f32[768]{0:T(1024)} %get-tuple-element.755, f32[768]{0:T(1024)} %get-tuple-element.760, f32[768]{0:T(1024)} %get-tuple-element.757, ...), channel_id=1, replica_groups=mesh['seq'=8,'ex'=4] {'seq','ex'}, use_global_device_ids=true, to_apply=%region_22.23 | all-reduce | flops 3076 | bytes 24608 | tf_op jit(solution)/shard_map/psum | solution.py:297
  811.7 4.6 add_add_fusion.2
  816.3 132.9 %all-reduce.6.cloned.1.call-done = (f32[768,2304]{1,0:T(8,128)}, f32[768,768]{1,0:T(8,128)}) async-done(((f32[768,2304]{1,0:T(8,128)}, f32[768,768]{1,0:T(8,128)}), (f32[768,2304]{1,0:T(8,128)}, f32[768,768]{1,0:T(8,128)})) %all-reduce.6.cloned.1.call-update) | async-done | bytes 9437200 | tf_op jit(solution)/shard_map/psum | solution.py:297
  949.2 6.6 copy.132
  (226 shorter events, 82.4 us)
Async XLA Ops:
  7.2 4.1 copy-start
  7.2 4.1 copy-start.25
  7.2 4.1 copy-start.31
  7.2 111.1 %all-gather.7.cloned.1.call-start = ((), (), s32[]{:S(2)}) async-start(), calls=%async_computation.5 | async-start | bytes 7077888 | tf_op jit(solution)/shard_map/all_gather | solution.py:111
  9.0 5.9 copy-start.27
  11.3 3.6 copy-start.29
  16.4 10.3 %copy-start.24 = (s32[4,1024]{1,0:T(4,128)S(1)}, s32[4,1024]{1,0:T(4,128)}, u32[]{:S(2)}) copy-start(s32[4,1024]{1,0:T(4,128)} %param.19) | copy-start | bytes 49156
  16.4 201.3 %all-gather.5.cloned.1.call-start = ((), (), s32[]{:S(2)}) async-start(), calls=%async_computation.4 | async-start | bytes 7077888 | tf_op jit(solution)/shard_map/all_gather | solution.py:110
  17.1 493.2 %all-gather.9.cloned.1.call-start = ((), (), s32[]{:S(2)}) async-start(), calls=%async_computation.6 | async-start | bytes 7077888 | tf_op jit(solution)/shard_map/all_gather | solution.py:275
  227.6 3.6 copy-start.2
  231.2 2.7 copy-start.15
  231.2 2.7 copy-start.11
  237.8 3.2 copy-start.12
  237.8 3.2 copy-start.21
  242.9 3.7 copy-start.2
  246.5 2.7 copy-start.15
  246.6 2.7 copy-start.11
  253.2 3.2 copy-start.12
  253.2 3.2 copy-start.21
  257.0 1.9 copy-start.3
  258.8 2.5 copy-start.10
  258.9 3.5 copy-start.33
  258.9 3.5 copy-start.36
  258.9 3.5 copy-start.49
  258.9 3.5 copy-start.51
  261.3 2.9 copy-start.6
  261.3 2.9 copy-start.38
  262.5 1.8 copy-start.47
  264.2 20.2 %all-to-all-start = ((bf16[4,192,768]{2,1,0:T(8,128)(2,1)}), bf16[4,192,768]{2,1,0:T(8,128)(2,1)}, u32[]{:S(2)}, u32[]{:S(2)}) async-start(bf16[4,192,768]{2,1,0:T(8,128)(2,1)} %bitcast.221), calls=%async_computation | async-start | bytes 2359296 | tf_op jit(solution)/shard_map/all_to_all | solution.py:140
  284.4 20.2 %all-to-all-start.2 = ((bf16[4,192,768]{2,1,0:T(8,128)(2,1)}), bf16[4,192,768]{2,1,0:T(8,128)(2,1)}, u32[]{:S(2)}, u32[]{:S(2)}) async-start(bf16[4,192,768]{2,1,0:T(8,128)(2,1)} %bitcast.220), calls=%async_computation.2 | async-start | bytes 2359296 | tf_op jit(solution)/shard_map/all_to_all | solution.py:164
  288.7 221.7 %all-gather.11.cloned.1.call-start = ((), (), s32[]{:S(2)}) async-start(), calls=%async_computation.7 | async-start | bytes 7077888 | tf_op jit(solution)/shard_map/all_gather | solution.py:276
  316.7 7.9 copy-start.52
  324.6 18.5 %copy-start.7 = (f32[4,128,768]{2,1,0:T(8,128)S(1)}, f32[4,128,768]{2,1,0:T(8,128)}, u32[]{:S(2)}) copy-start(f32[4,128,768]{2,1,0:T(8,128)} %copy-done.6) | copy-start | bytes 4718596
  324.6 18.5 %copy-start.34 = (s32[4,128]{1,0:T(4,128)S(1)}, s32[4,128]{1,0:T(4,128)}, u32[]{:S(2)}) copy-start(s32[4,128]{1,0:T(4,128)} %multiply_add_fusion.2) | copy-start | bytes 6148
  324.6 18.5 %copy-start.37 = (s32[4,48]{1,0:T(4,128)S(1)}, s32[4,48]{1,0:T(4,128)}, u32[]{:S(2)}) copy-start(s32[4,48]{1,0:T(4,128)} %multiply_add_fusion.1) | copy-start | bytes 2308
  324.6 18.5 %copy-start.39 = (f32[4,128]{1,0:T(4,128)S(1)}, f32[4,128]{1,0:T(4,128)}, u32[]{:S(2)}) copy-start(f32[4,128]{1,0:T(4,128)} %copy-done.38) | copy-start | bytes 6148
  324.6 18.5 %copy-start.48 = (f32[4,128]{1,0:T(4,128)S(1)}, f32[4,128]{1,0:T(4,128)}, u32[]{:S(2)}) copy-start(f32[4,128]{1,0:T(4,128)} %copy-done.47) | copy-start | bytes 6148
  324.7 18.5 %copy-start.50 = (f32[768]{0:T(1024)S(1)}, f32[768]{0:T(1024)}, u32[]{:S(2)}) copy-start(f32[768]{0:T(1024)} %param.23) | copy-start | bytes 9220
  343.1 1.5 copy-start.46
  344.6 1.4 copy-start.8
  345.2 1.2 copy-start.9
  345.2 2.0 copy-start.23
  349.0 402.6 %all-reduce.8.cloned.1.call-start = ((), (), s32[]{:S(2)}) async-start(), calls=%async_computation.9 | async-start | bytes 18874368 | tf_op jit(solution)/shard_map/psum | solution.py:310
  409.2 540.1 %all-reduce.6.cloned.1.call-start = ((), (), s32[]{:S(2)}) async-start(), calls=%async_computation.8 | async-start | bytes 18874368 | tf_op jit(solution)/shard_map/psum | solution.py:297
  424.4 7.0 copy-start.5
  429.7 1.7 copy-start.1
  450.9 7.0 copy-start.5
  456.2 1.7 copy-start.1
  617.5 4.8 copy-start.26
  617.5 4.8 copy-start.28
  617.5 4.8 copy-start.30
  617.5 4.8 copy-start.32
  641.1 20.6 %copy-start.35 = (s32[4,128]{1,0:T(4,128)S(1)}, s32[4,128]{1,0:T(4,128)}, u32[]{:S(2)}) copy-start(s32[4,128]{1,0:T(4,128)} %multiply_add_fusion.2) | copy-start | bytes 6148
  641.1 20.6 %all-to-all-start.1 = ((bf16[4,192,768]{2,1,0:T(8,128)(2,1)}), bf16[4,192,768]{2,1,0:T(8,128)(2,1)}, u32[]{:S(2)}, u32[]{:S(2)}) async-start(bf16[4,192,768]{2,1,0:T(8,128)(2,1)} %bitcast.228), calls=%async_computation.1 | async-start | bytes 2359296 | tf_op jit(solution)/shard_map/all_to_all | solution.py:150
  751.6 7.5 copy-start.14
  759.1 5.7 copy-start.4
  759.1 5.7 copy-start.17
  759.1 5.7 copy-start.18
  759.1 5.7 copy-start.19
  764.8 2.7 copy-start.44
  767.5 1.4 copy-start.13
  767.5 44.2 %copy-start.41 = (f32[4,128]{1,0:T(4,128)S(1)}, f32[4,128]{1,0:T(4,128)}, u32[]{:S(2)}) copy-start(f32[4,128]{1,0:T(4,128)} %copy-done.40) | copy-start | bytes 6148
  767.5 1.4 copy-start.42
  949.2 6.6 copy-start.20
  (6 other events, 4.6 us)
Sparse Core Ops, SparseCore 0:
  16.5 101.7 all-gather.6
  120.5 97.1 all-gather.4
  219.9 97.1 all-gather.8
  349.1 99.2 all-gather.10
  452.2 299.3 all-reduce.7
  757.9 191.2 all-reduce.5
where the time goes:
time: 969 us; the launch traced here: 964 us
  waiting for transfers between devices  435 us (45%)
  matrix products  202 us (21%)
  local copies, waits for them, and re-layouts  116 us (12%)
  blocking collectives  115 us (12%)
  other arithmetic  65.2 us (7%)
  between operations  14.9 us (2%)
  starting transfers between devices  14.5 us (1%)
    psum x1, waiting for transfers between devices, per_device(): lax.psum((grad_qkv, grad_attn_out, grad_gain_one, grad_bias_one, grad_gai...  133 us
    all_gather x1, waiting for transfers between devices, per_device(): lax.all_gather(values, 'seq', axis=1, tiled=True)  91 us
    all_gather x1, waiting for transfers between devices, per_device(): lax.all_gather(keys, 'seq', axis=1, tiled=True)  90.8 us
    psum x1, waiting for transfers between devices, per_device(): lax.psum(grad_up.astype(jnp.bfloat16), 'seq').astype(jnp.float32)  86.4 us
    dynamic_slice x10, local copies, waits for them, and re-layouts, advance(): lax.dynamic_slice_in_dim(piece, index * block, block, 1)  48.8 us
    psum x1, blocking collectives, per_device(): lax.psum((grad_qkv, grad_attn_out, grad_gain_one, grad_bias_one, grad_gai...  41 us
    unnamed x97, local copies, waits for them, and re-layouts  39 us
    all_gather x1, blocking collectives, per_device(): lax.all_gather(delta.astype(jnp.bfloat16), 'seq', axis=2, tiled=True)  28.9 us
  transfers between devices with their start and end apart: 9, of which 7 were waited for; matrix products, arithmetic and copies ran while one was open for 37% of the time, Pallas kernels for 0%

commit v1 on v0

v1 whole, which is shorter than its diff:
```python
import functools
import math

import jax
import jax.numpy as jnp
from jax import lax
from jax.experimental import pallas as pl
from jax.experimental.pallas import tpu as pltpu
from jax.sharding import PartitionSpec as P

HEADS = 12
HEAD = 64
MOST = 48
PAIR = 2 * HEAD
EPSILON = 1e-05
NEGATIVE = -1e30
LOW = jnp.bfloat16
FULL = jnp.float32
VMEM_LIMIT = 60 * 1024 * 1024
NN = (((1,), (0,)), ((), ()))
NT = (((1,), (1,)), ((), ()))
TN = (((0,), (0,)), ((), ()))


def dot(a, b, dims=NN):
    return lax.dot_general(a, b, dims, preferred_element_type=FULL)


def spans(count, unroll, body):
    if unroll:
        for index in range(count):
            body(index)
    else:

        def step(index, carry):
            body(index)
            return carry

        lax.fori_loop(0, count, step, 0)


def chain(first, last, unroll, body, carry):
    if unroll:
        for index in range(first, last):
            carry = body(index, carry)
        return carry
    return lax.fori_loop(first, last, body, carry)


def tile_mask(scores, low_row, key_first, query_first, diagonal):
    key_pos = key_first + lax.broadcasted_iota(jnp.int32, scores.shape, 0)
    allowed = key_pos >= low_row
    if diagonal:
        query_pos = query_first + lax.broadcasted_iota(jnp.int32, scores.shape, 1)
        allowed = allowed & (key_pos <= query_pos)
    return allowed


def head_lanes(value, head):
    lane = lax.broadcasted_iota(jnp.int32, value.shape, 1)
    return jnp.where((lane // HEAD) == head, value, jnp.zeros_like(value))


def attend_kernel(
    block, unroll, own_ref, x_ref, wq_ref, wk_ref, wv_ref, low_ref,
    q_ref, k_ref, v_ref, o_ref, ot_ref, log_ref, vt_ref,
):
    length = x_ref.shape[0]
    count = length // block

    def project(index):
        rows = pl.ds(index * block, block)
        x = x_ref[rows, :]
        q_ref[rows, :] = (dot(x, wq_ref[...]).astype(LOW) * LOW(HEAD**-0.5)).astype(LOW)
        k_ref[rows, :] = dot(x, wk_ref[...]).astype(LOW)
        v = dot(x, wv_ref[...]).astype(LOW)
        v_ref[rows, :] = v
        vt_ref[:, rows] = v.T

    spans(count, unroll, project)

    def one_block(qi):
        rows = pl.ds(qi * block, block)
        low_row = low_ref[:, rows]
        q = q_ref[rows, :]
        done = []
        for head in range(2):
            qm = head_lanes(q, head)
            part = pl.ds(head * HEAD, HEAD)

            def tile(kj, state, diagonal):
                keys = pl.ds(kj * block, block)
                scores = dot(k_ref[keys, :], qm, NT)
                allowed = tile_mask(scores, low_row, kj * block, qi * block, diagonal)
                scores = jnp.where(allowed, scores, NEGATIVE)
                high = jnp.max(scores, 0, keepdims=True)
                if state is not None:
                    high = jnp.maximum(high, state[0])
                weights = jnp.exp(scores - high)
                total = jnp.sum(weights, 0, keepdims=True)
                summed = dot(vt_ref[part, keys], weights.astype(LOW))
                if state is not None:
                    fade = jnp.exp(state[0] - high)
                    total = total + state[1] * fade
                    summed = summed + state[2] * fade
                return high, total, summed

            state = tile(qi, None, True)
            high, total, summed = chain(
                0, qi, unroll, lambda kj, carry: tile(kj, carry, False), state
            )
            log_ref[0, pl.ds(head, 1), rows] = high + jnp.log(total)
            done.append(summed / total)
        both = jnp.concatenate(done, 0)
        ot_ref[:, rows] = both
        o_ref[rows, :] = both.T.astype(LOW)

    spans(count, unroll, one_block)


def attend_back_kernel(
    block, unroll, own_ref, x_ref, wq_ref, wk_ref, wv_ref, low_ref,
    q_ref, k_ref, v_ref, g_ref, ot_ref, log_ref,
    gx_ref, gw_ref, kt_ref, delta_ref, dqt_ref, dk_ref, dv_ref, sum_ref,
):
    length = x_ref.shape[0]
    count = length // block
    width = x_ref.shape[1]
    scale = HEAD**-0.5
    pair = pl.program_id(0)

    def prepare(index):
        rows = pl.ds(index * block, block)
        kt_ref[:, rows] = k_ref[rows, :].T
        product = g_ref[rows, :].astype(FULL).T * ot_ref[:, rows]
        for head in range(2):
            part = product[head * HEAD : (head + 1) * HEAD]
            delta_ref[pl.ds(head, 1), rows] = jnp.sum(part, 0, keepdims=True)
        dqt_ref[:, rows] = jnp.zeros((PAIR, block), FULL)

    spans(count, unroll, prepare)

    def one_block(kj):
        keys = pl.ds(kj * block, block)
        k = k_ref[keys, :]
        v = v_ref[keys, :]

        def tile(qi, carry, diagonal):
            grad_k, grad_v = carry
            rows = pl.ds(qi * block, block)
            q = q_ref[rows, :]
            g = g_ref[rows, :]
            low_row = low_ref[:, rows]
            for head in range(2):
                qm = head_lanes(q, head)
                gm = head_lanes(g, head)
                part = pl.ds(head * HEAD, HEAD)
                scores = dot(k, qm, NT)
                allowed = tile_mask(scores, low_row, kj * block, qi * block, diagonal)
                probs = jnp.exp(scores - log_ref[0, pl.ds(head, 1), rows])
                probs = jnp.where(allowed, probs, 0.0)
                grad_probs = dot(v, gm, NT)
                grad_scores = (probs * (grad_probs - delta_ref[pl.ds(head, 1), rows])).astype(LOW)
                grad_v = grad_v + dot(probs.astype(LOW), gm)
                grad_k = grad_k + dot(grad_scores, qm)
                dqt_ref[part, rows] += dot(kt_ref[part, keys], grad_scores)
            return grad_k, grad_v

        zero = jnp.zeros((block, PAIR), FULL)
        carry = tile(kj, (zero, zero), True)
        grad_k, grad_v = chain(
            kj + 1, count, unroll, lambda qi, carry: tile(qi, carry, False), carry
        )
        dk_ref[keys, :] = grad_k.astype(LOW)
        dv_ref[keys, :] = grad_v.astype(LOW)

    spans(count, unroll, one_block)

    @pl.when(pair == 0)
    def _():
        sum_ref[...] = jnp.zeros_like(sum_ref)

    gw_ref[...] = jnp.zeros_like(gw_ref)

    def spread(index):
        rows = pl.ds(index * block, block)
        dq = (dqt_ref[:, rows] * scale).T.astype(LOW)
        dk = dk_ref[rows, :]
        dv = dv_ref[rows, :]
        total = dot(dq, wq_ref[...], NT) + dot(dk, wk_ref[...], NT) + dot(dv, wv_ref[...], NT)
        sum_ref[rows, :] += total
        x = x_ref[rows, :]
        gw_ref[0] += dot(x, dq, TN)
        gw_ref[1] += dot(x, dk, TN)
        gw_ref[2] += dot(x, dv, TN)

    spans(count, unroll, spread)

    @pl.when(pair == pl.num_programs(0) - 1)
    def _():
        gx_ref[...] = sum_ref[...].astype(LOW)


def attention_specs(length, width, pairs, all_pairs):
    whole = lambda: pl.BlockSpec((length, width), lambda p, own: (0, 0))
    weight = lambda which: pl.BlockSpec(
        (width, PAIR), lambda p, own: (0, which * all_pairs + own[0] * pairs + p)
    )
    low = pl.BlockSpec((1, length), lambda p, own: (0, 0))
    columns = lambda: pl.BlockSpec((length, PAIR), lambda p, own: (0, p))
    across = pl.BlockSpec((PAIR, length), lambda p, own: (p, 0))
    logs = pl.BlockSpec((1, 2, length), lambda p, own: (p, 0, 0))
    return whole, weight, low, columns, across, logs


def attend(own, x, weights, low, pairs, all_pairs):
    length, width = x.shape
    block = math.gcd(length, 256)
    unroll = length // block <= 4
    whole, weight, lows, columns, across, logs = attention_specs(length, width, pairs, all_pairs)
    shape = jax.ShapeDtypeStruct
    return pl.pallas_call(
        functools.partial(attend_kernel, block, unroll),
        grid_spec=pltpu.PrefetchScalarGridSpec(
            num_scalar_prefetch=1,
            grid=(pairs,),
            in_specs=[whole(), weight(0), weight(1), weight(2), lows],
            out_specs=[columns(), columns(), columns(), columns(), across, logs],
            scratch_shapes=[pltpu.VMEM((PAIR, length), LOW)],
        ),
        out_shape=[shape((length, pairs * PAIR), LOW)] * 4
        + [shape((pairs * PAIR, length), FULL), shape((pairs, 2, length), FULL)],
        compiler_params=pltpu.CompilerParams(vmem_limit_bytes=VMEM_LIMIT),
        cost_estimate=pl.CostEstimate(
            flops=2 * length * width * 3 * pairs * PAIR + 8 * length * length * pairs * PAIR,
            bytes_accessed=2 * length * width + 12 * length * pairs * PAIR,
            transcendentals=length * length * pairs,
        ),
        name="attend",
    )(own, x, weights, weights, weights, low)


def attend_back(own, x, weights, low, q, k, v, g, ot, logs_in, pairs, all_pairs):
    length, width = x.shape
    block = math.gcd(length, 256)
    unroll = length // block <= 4
    whole, weight, lows, columns, across, logs = attention_specs(length, width, pairs, all_pairs)
    shape = jax.ShapeDtypeStruct
    return pl.pallas_call(
        functools.partial(attend_back_kernel, block, unroll),
        grid_spec=pltpu.PrefetchScalarGridSpec(
            num_scalar_prefetch=1,
            grid=(pairs,),
            in_specs=[whole(), weight(0), weight(1), weight(2), lows]
            + [columns(), columns(), columns(), columns(), across, logs],
            out_specs=[whole(), pl.BlockSpec((3, width, PAIR), lambda p, own: (0, 0, p))],
            scratch_shapes=[
                pltpu.VMEM((PAIR, length), LOW),
                pltpu.VMEM((2, length), FULL),
                pltpu.VMEM((PAIR, length), FULL),
                pltpu.VMEM((length, PAIR), LOW),
                pltpu.VMEM((length, PAIR), LOW),
                pltpu.VMEM((length, width), FULL),
            ],
        ),
        out_shape=[shape((length, width), LOW), shape((3, width, pairs * PAIR), FULL)],
        compiler_params=pltpu.CompilerParams(vmem_limit_bytes=VMEM_LIMIT),
        cost_estimate=pl.CostEstimate(
            flops=4 * length * width * 3 * pairs * PAIR + 20 * length * length * pairs * PAIR,
            bytes_accessed=4 * length * width + 24 * length * pairs * PAIR,
            transcendentals=length * length * pairs,
        ),
        name="attend_back",
    )(own, x, weights, weights, weights, low, q, k, v, g, ot, logs_in)


GELU_SCALE = math.sqrt(2.0 / math.pi)
GELU_CUBE = 0.044715


def expert_kernel(
    x_ref, g_ref, up_ref, down_ref, y_ref, gx_ref, gup_ref, gdown_ref, y_sum, gx_sum
):
    step = pl.program_id(0)
    x = x_ref[...]
    g = g_ref[...]
    inner = dot(x, up_ref[...])
    square = inner * inner
    curve = jnp.tanh(GELU_SCALE * inner * (1.0 + GELU_CUBE * square))
    half = 0.5 + 0.5 * curve
    active = (inner * half).astype(LOW)
    slope = half + (0.5 * GELU_SCALE) * inner * (1.0 - curve * curve) * (
        1.0 + (3.0 * GELU_CUBE) * square
    )
    grad_inner = (dot(g, down_ref[...], NT) * slope).astype(LOW)
    gdown_ref[...] = dot(active, g, TN).astype(LOW)
    gup_ref[...] = dot(x, grad_inner, TN).astype(LOW)
    y = dot(active, down_ref[...])
    gx = dot(grad_inner, up_ref[...], NT)

    @pl.when(step == 0)
    def _():
        y_sum[...] = y
        gx_sum[...] = gx

    @pl.when(step > 0)
    def _():
        y_sum[...] += y
        gx_sum[...] += gx

    @pl.when(step == pl.num_programs(0) - 1)
    def _():
        y_ref[...] = y_sum[...].astype(LOW)
        gx_ref[...] = gx_sum[...].astype(LOW)


def expert(x, g, up, down):
    slots, width = x.shape
    hidden = up.shape[1]
    block = math.gcd(hidden, 512)
    rows = lambda: pl.BlockSpec((slots, width), lambda f: (0, 0))
    ups = lambda: pl.BlockSpec((width, block), lambda f: (0, f))
    downs = lambda: pl.BlockSpec((block, width), lambda f: (f, 0))
    shape = jax.ShapeDtypeStruct
    return pl.pallas_call(
        expert_kernel,
        grid=(hidden // block,),
        in_specs=[rows(), rows(), ups(), downs()],
        out_specs=[rows(), rows(), ups(), downs()],
        out_shape=[shape((slots, width), LOW)] * 2
        + [shape((width, hidden), LOW), shape((hidden, width), LOW)],
        scratch_shapes=[pltpu.VMEM((slots, width), FULL)] * 2,
        compiler_params=pltpu.CompilerParams(vmem_limit_bytes=VMEM_LIMIT),
        cost_estimate=pl.CostEstimate(
            flops=12 * slots * width * hidden,
            bytes_accessed=8 * width * hidden + 8 * slots * width,
            transcendentals=slots * hidden,
        ),
        name="expert",
    )(x, g, up, down)


def standard(value):
    center = value - jnp.mean(value, -1, keepdims=True)
    spread = jnp.mean(center * center, -1, keepdims=True)
    inverse = lax.rsqrt(spread + EPSILON)
    return center * inverse, inverse


def standard_back(grad, gain, unit, inverse):
    u = grad * gain
    lean = jnp.mean(u * unit, -1, keepdims=True)
    back = (u - jnp.mean(u, -1, keepdims=True) - unit * lean) * inverse
    return back, jnp.sum(grad * unit, 0), jnp.sum(grad, 0)


def per_device(
    block_input, segment_ids, expert_ids, ln1_gain, ln1_bias, ln2_gain, ln2_bias,
    w_qkv, w_attn_out, w_in, w_down, grad_out,
):
    rows, local, width = block_input.shape
    seq = lax.axis_size("seq")
    experts = lax.axis_size("ex")
    team = seq // rows
    length = seq * local
    owned = rows * local
    pairs = -(-HEADS // (2 * team))
    share = pairs * PAIR
    all_pairs = pairs * team
    padded = all_pairs * PAIR
    place = lax.axis_index("seq")
    row, member = place // team, place % team
    across_rows = [[r * team + g for r in range(rows)] for g in range(team)]
    in_row = [[r * team + g for g in range(team)] for r in range(rows)]

    def swap_rows(value):
        return lax.all_to_all(value, "seq", 0, 0, tiled=True, axis_index_groups=across_rows)

    def swap_team(value):
        return lax.all_to_all(value, "seq", 0, 0, tiled=True, axis_index_groups=in_row)

    def swap_experts(value):
        return lax.all_to_all(value, "ex", 0, 0, tiled=True)

    center = block_input - jnp.mean(block_input, -1, keepdims=True)
    residual = swap_rows(center.astype(LOW)).reshape(owned, width).astype(FULL)
    chosen = swap_rows(expert_ids[..., 0])
    grad_low = swap_rows(grad_out.astype(LOW))

    segments = lax.dynamic_slice_in_dim(segment_ids, row, 1, 0)[0]
    lows = jnp.sum((segments[:, None] < segments[None, :]).astype(jnp.int32), 0)[None, :]

    weights = w_qkv
    out_weights = w_attn_out
    if padded != width:
        weights = jnp.pad(
            w_qkv.reshape(width, 3, width), ((0, 0), (0, 0), (0, padded - width))
        ).reshape(width, 3 * padded)

    unit_one, inverse_one = standard(residual)
    normed_one = (unit_one * ln1_gain + ln1_bias).astype(LOW)
    gathered = swap_team(
        jnp.broadcast_to(normed_one[None], (team, owned, width))
    ).reshape(team, rows, local, width)
    full = jnp.swapaxes(gathered, 0, 1).reshape(length, width)

    own = member.reshape(1).astype(jnp.int32)
    q, k, v, o, ot, logs = attend(own, full, weights, lows, pairs, all_pairs)

    def to_owners(value):
        parts = value.reshape(rows, team, local, value.shape[-1])
        parts = jnp.swapaxes(parts, 0, 1)
        return swap_team(parts).reshape(team, owned, value.shape[-1])

    attended = jnp.swapaxes(to_owners(o), 0, 1).reshape(owned, padded)[:, :width]
    branch = dot(attended, out_weights)
    middle = residual + branch
    unit_two, inverse_two = standard(middle)
    normed_two = (unit_two * ln2_gain + ln2_bias).astype(LOW)

    onehot = (chosen[..., None] == jnp.arange(experts, dtype=jnp.int32)).astype(jnp.int32)
    rank = jnp.cumsum(onehot, 1) - onehot
    target = chosen * MOST + jnp.sum(rank * onehot, -1)
    route = (
        (target[:, None, :] == jnp.arange(experts * MOST, dtype=jnp.int32)[None, :, None])
        .astype(LOW)
        .reshape(rows, experts, MOST, local)
    )
    counts = jnp.sum(onehot.astype(FULL), (0, 1))

    def dispatch(value):
        placed = jnp.einsum(
            "remt,rtd->ermd", route, value.reshape(rows, local, width), preferred_element_type=FULL
        )
        return swap_experts(placed.astype(LOW).reshape(experts, rows * MOST, width)).reshape(
            experts * rows * MOST, width
        )

    def collect(value):
        returned = swap_experts(value.reshape(experts, rows * MOST, width))
        return jnp.einsum(
            "remt,ermd->rtd",
            route,
            returned.reshape(experts, rows, MOST, width),
            preferred_element_type=FULL,
        ).reshape(owned, width)

    grad_arrived = dispatch(grad_low)
    arrived = dispatch(normed_two)
    produced, grad_rows, grad_up, grad_down = expert(arrived, grad_arrived, w_in[0], w_down[0])

    grad_normed_two = collect(grad_rows)
    back_two, grad_gain_two, grad_bias_two = standard_back(
        grad_normed_two, ln2_gain, unit_two, inverse_two
    )
    grad_branch = (back_two + grad_low.reshape(owned, width).astype(FULL)).astype(LOW)
    grad_attended = dot(grad_branch, out_weights, NT).astype(LOW)
    if padded != width:
        grad_attended = jnp.pad(grad_attended, ((0, 0), (0, padded - width)))
    parted = jnp.swapaxes(grad_attended.reshape(owned, team, share), 0, 1)
    grad_heads = jnp.swapaxes(swap_team(parted).reshape(team, rows, local, share), 0, 1)
    grad_full, grad_weights = attend_back(
        own, full, weights, lows, q, k, v, grad_heads.reshape(length, share), ot, logs,
        pairs, all_pairs,
    )

    expert_part = collect(produced)
    change = swap_rows((branch + expert_part).astype(LOW).reshape(rows, local, width))
    block_output = block_input + change.astype(FULL)

    grad_attn_out = dot(attended, grad_branch, TN)

    grad_normed_one = jnp.sum(to_owners(grad_full).astype(FULL), 0)
    back_one, grad_gain_one, grad_bias_one = standard_back(
        grad_normed_one, ln1_gain, unit_one, inverse_one
    )
    grad_change = swap_rows((back_two + back_one).astype(LOW).reshape(rows, local, width))
    grad_input = grad_out + grad_change.astype(FULL)

    cut = width // (experts * rows)
    parts = grad_weights.astype(LOW).reshape(3, experts, rows, cut, share)
    parts = jnp.transpose(parts, (1, 2, 0, 3, 4))
    parts = jnp.sum(swap_experts(parts).astype(FULL), 0)
    parts = jnp.sum(swap_rows(parts.astype(LOW)).astype(FULL), 0).astype(LOW)
    parts = swap_rows(jnp.broadcast_to(parts[None], (rows,) + parts.shape))
    parts = swap_team(jnp.broadcast_to(parts[None], (team,) + parts.shape))
    parts = swap_experts(jnp.broadcast_to(parts[None], (experts,) + parts.shape))
    parts = parts.reshape(experts, team, rows, 3, cut, share)
    grad_qkv = jnp.transpose(parts, (0, 2, 4, 3, 1, 5)).reshape(width, 3, padded)[..., :width]
    grad_qkv = grad_qkv.reshape(width, 3 * width).astype(FULL)

    grad_attn_out = lax.psum(grad_attn_out.astype(LOW), ("seq", "ex")).astype(FULL)
    small = jnp.stack([grad_gain_one, grad_bias_one, grad_gain_two, grad_bias_two])
    small, counts = lax.psum((small, counts), ("seq", "ex"))
    expert_grads = (
        lax.psum(grad_up, "seq").astype(FULL),
        lax.psum(grad_down, "seq").astype(FULL),
    )
    load = counts * (experts / (rows * length * experts))
    return (
        block_output, grad_input, grad_qkv, grad_attn_out, small[0], small[1], small[2], small[3],
        expert_grads[0][None], expert_grads[1][None], load,
    )


def solution(mesh):
    tokens = P("ex", "seq", None)
    expert_axis = P("ex", None, None)
    return jax.shard_map(
        per_device,
        mesh=mesh,
        in_specs=(
            tokens, P("ex", None), tokens, P(), P(), P(), P(), P(), P(),
            expert_axis, expert_axis, tokens,
        ),
        out_specs=(
            tokens, tokens, P(), P(), P(), P(), P(), P(), expert_axis, expert_axis, P(),
        ),
        check_vma=False,
    )
```

time: 969 us -> 757 us (0.78)
  matrix products: 202 us -> 10.5 us
  waiting for transfers between devices: 435 us -> 339 us
  Pallas kernels: 0 us -> 83.1 us
  local copies, waits for them, and re-layouts: 116 us -> 40 us
  starting transfers between devices: 14.5 us -> 56.2 us
  blocking collectives: 115 us -> 153 us
  other arithmetic: 65.2 us -> 50.7 us
    dot_general x30 -> x7, matrix products: 202 us -> 10.5 us  [the longest x3 7.06 us: dot(): return lax.dot_general(a, b, dims, preferred_element_type=FULL)]
    all_gather x4 -> x0, waiting for transfers between devices: 182 us -> none  [the longest x1 91 us: per_device(): lax.all_gather(values, 'seq', axis=1, tiled=True)]
    all_to_all x3 -> x14, waiting for transfers between devices: 32.8 us -> 131 us  [the longest x6 58.1 us: swap_rows(): lax.all_to_all(value, 'seq', 0, 0, tiled=True, axis_index_groups=across_r...]
    pallas_call x0 -> x3, Pallas kernels: none -> 83.1 us  [the longest x1 31.3 us: expert(): pl.pallas_call(expert_kernel, grid=(hidden // block,), in_specs=[rows(),...]
    all_to_all x1 -> x4, blocking collectives: 18.4 us -> 80.2 us  [the longest x2 40.1 us: swap_experts(): return lax.all_to_all(value, 'ex', 0, 0, tiled=True)]
    all_gather x2 -> x0, blocking collectives: 55.9 us -> none  [the longest x1 28.9 us: per_device(): lax.all_gather(delta.astype(jnp.bfloat16), 'seq', axis=2, tiled=True)]
    dynamic_slice x19 -> x1, local copies, waits for them, and re-layouts: 52.8 us -> 0.73 us  [per_device(): segments = lax.dynamic_slice_in_dim(segment_ids, row, 1, 0)[0]]
    all_to_all x3 -> x14, starting transfers between devices: 13.3 us -> 56.1 us  [the longest x6 23.5 us: swap_rows(): lax.all_to_all(value, 'seq', 0, 0, tiled=True, axis_index_groups=across_r...]
  transfers between devices with their start and end apart: 9 -> 16, of which waited for: 7 -> 13; matrix products, arithmetic and copies ran while one was open for 37% -> 10% of each run, Pallas kernels for 0% -> 7%
where the time goes in v1:
time: 757 us; the launch traced here: 747 us
  waiting for transfers between devices  339 us (45%)
  blocking collectives  153 us (20%)
  Pallas kernels  83.1 us (11%)
  starting transfers between devices  56.2 us (7%)
  other arithmetic  50.7 us (7%)
  local copies, waits for them, and re-layouts  40 us (5%)
  between operations  14.9 us (2%)
  matrix products  10.5 us (1%)
    psum x1, waiting for transfers between devices, per_device(): lax.psum(grad_up, 'seq').astype(FULL)  206 us
    psum x1, blocking collectives, per_device(): small, counts = lax.psum((small, counts), ('seq', 'ex'))  72.8 us
    all_to_all x6, waiting for transfers between devices, swap_rows(): lax.all_to_all(value, 'seq', 0, 0, tiled=True, axis_index_groups=across_r...  58.1 us
    all_to_all x4, waiting for transfers between devices, swap_team(): lax.all_to_all(value, 'seq', 0, 0, tiled=True, axis_index_groups=in_row)  46.7 us
    all_to_all x2, blocking collectives, swap_experts(): return lax.all_to_all(value, 'ex', 0, 0, tiled=True)  40.1 us
    pallas_call x1, Pallas kernels, expert(): pl.pallas_call(expert_kernel, grid=(hidden // block,), in_specs=[rows(),...  31.3 us
    pallas_call x1, Pallas kernels, attend_back(): pl.pallas_call(functools.partial(attend_back_kernel, block, unroll), grid...  27.6 us
    all_to_all x4, waiting for transfers between devices, swap_experts(): return lax.all_to_all(value, 'ex', 0, 0, tiled=True)  26.3 us
  transfers between devices with their start and end apart: 16, of which 13 were waited for; matrix products, arithmetic and copies ran while one was open for 10% of the time, Pallas kernels for 7%

profile of v1, /device:TPU:0, one launch (start us, length us, event | category | flops | bytes accessed | tf_op | source)
XLA Modules:
  0.0 747.4 jit_solution(6119985059510978764)
XLA Ops:
  7.2 1.7 reduce_sum.181
  9.4 26.2 %all_to_all.94 = bf16[4,128,768]{2,1,0:T(8,128)(2,1)S(1)} all-to-all(bf16[4,128,768]{2,1,0:T(8,128)(2,1)S(1)} %subtract_convert_fusion), channel_id=1, replica_groups={{0,8,16,24},{4,12,20,28},{1,9,17,25},{5,13,21,29},{2,10,18,26},{6,14,22..., dimensions={0} | all-to-all | bytes 1572864 | tf_op jit(solution)/shard_map/all_to_all | solution.py:377
  35.6 3.2 all-to-all-start.3
  40.9 3.4 all-to-all-done.3
  44.2 1.2 broadcast_in_dim.20
  45.5 3.7 all-to-all-start.1
  49.2 2.4 convert_element_type.117
  51.6 14.8 %all-to-all-done.1 = bf16[2,512,768]{2,1,0:T(8,128)(2,1)S(1)} async-done(((bf16[2,512,768]{2,1,0:T(8,128)(2,1)}), bf16[2,512,768]{2,1,0:T(8,128)(2,1)S(1)}, u32[]{:S(2)}, u32[]{:S(2)}) %all-to-all-start.1) | async-done | bytes 1572896 | tf_op jit(solution)/shard_map/all_to_all | solution.py:380
  66.4 1.1 copy-done.8
  67.5 3.5 all-to-all-start.5
  73.5 2.7 copy.60
  76.1 24.2 %attend.1 = (bf16[1024,384]{1,0:T(8,128)(2,1)}, bf16[1024,384]{1,0:T(8,128)(2,1)}, bf16[1024,384]{1,0:T(8,128)(2,1)}, bf16[1024,384]{1,0:T(8,128)(2,1)}, f32[384,1024]{1,0:T(8,128)}, /*index=5*/f32[3,2,1024]{2,1,0:T(2,128)}) custom-call(s32[1]{0:T(128)} %bitcast.own_ref, bf16[1024,768]{1,0:T(8,128)(2,1)} %bitcast.161, bf16[768,2304]{1,0:T(8,128)(2,1)} %wv_ref.3, ...), custom_call_target="tpu_custom_call" | custom-call | flops 5033164800 | bytes 6291456 | tf_op jit(solution)/shard_map/attend/pallas_call | solution.py:222
  100.3 2.1 copy.93
  102.4 3.5 all-to-all-start.2
  106.5 1.1 copy.64
  107.6 6.3 all-to-all-done.2
  113.9 4.3 all-to-all-start.6
  118.2 1.2 copy.62
  119.5 3.1 fusion.43
  125.2 9.0 %all-to-all-done.6 = bf16[4,192,768]{2,1,0:T(8,128)(2,1)} async-done(((bf16[4,192,768]{2,1,0:T(8,128)(2,1)}), bf16[4,192,768]{2,1,0:T(8,128)(2,1)}, u32[]{:S(2)}, u32[]{:S(2)}) %all-to-all-start.6) | async-done | bytes 1179680 | tf_op jit(solution)/shard_map/all_to_all | solution.py:383
  134.2 20.7 %all_to_all.95 = bf16[4,192,768]{2,1,0:T(8,128)(2,1)} all-to-all(bf16[4,192,768]{2,1,0:T(8,128)(2,1)} %bitcast.151), channel_id=1, replica_groups=mesh['seq'=8,'ex'=4] {'ex'}, dimensions={0} | all-to-all | bytes 2359296 | tf_op jit(solution)/shard_map/all_to_all | solution.py:383
  154.9 31.3 %expert.1 = (bf16[768,768]{1,0:T(8,128)(2,1)}, bf16[768,768]{1,0:T(8,128)(2,1)}, bf16[768,3072]{1,0:T(8,128)(2,1)}, bf16[3072,768]{1,0:T(8,128)(2,1)}) custom-call(bf16[768,768]{1,0:T(8,128)(2,1)} %bitcast.165, bf16[768,768]{1,0:T(8,128)(2,1)} %bitcast.28.g_ref, bf16[768,3072]{1,0:T(8,128)(2,1)} %bitcast.182, bf16[3072,768]{1,0:T(8,128)(2,1)} %bitcast.183), custom_call_target="tpu_custom_call" | custom-call | flops 21743271936 | bytes 23592960 | tf_op jit(solution)/shard_map/expert/pallas_call | solution.py:325
  186.2 19.4 %all_to_all.96 = bf16[4,192,768]{2,1,0:T(8,128)(2,1)S(1)} all-to-all(bf16[4,192,768]{2,1,0:T(8,128)(2,1)} %bitcast.166), channel_id=1, replica_groups=mesh['seq'=8,'ex'=4] {'ex'}, dimensions={0} | all-to-all | bytes 2359296 | tf_op jit(solution)/shard_map/all_to_all | solution.py:383
  206.7 1.1 fusion.2
  210.0 13.9 %all_to_all.97 = bf16[2,512,384]{2,1,0:T(8,128)(2,1)} all-to-all(bf16[2,512,384]{2,1,0:T(8,128)(2,1)S(1)} %bitcast.156), channel_id=1, replica_groups={{0,4},{8,12},{16,20},{24,28},{1,5},{9,13},{17,21},{25,29},{2,6},{10,14}..., dimensions={0} | all-to-all | bytes 1572864 | tf_op jit(solution)/shard_map/all_to_all | solution.py:380
  223.9 3.7 all-to-all-start.7
  227.6 2.1 copy.68
  229.7 27.6 %attend_back.1 = (bf16[1024,768]{1,0:T(8,128)(2,1)}, f32[3,768,384]{2,1,0:T(8,128)}) custom-call(s32[1]{0:T(128)} %bitcast.own_ref, bf16[1024,768]{1,0:T(8,128)(2,1)} %bitcast.162, bf16[768,2304]{1,0:T(8,128)(2,1)} %wv_ref.3, bf16[768,2304]{1,0:T(8,128)(2,1)} %wv_ref.3, bf16[768,2304]{1,0:T(8,128)(2,1)} %wv_ref.3, s32[1,1024]{1,0:T(1,128)} %bitcast.181, ...), custom_call_target="tpu_custom_call" | custom-call | flops 11676942336 | bytes 12582912 | tf_op jit(solution)/shard_map/attend_back/pallas_call | solution.py:249
  257.3 2.2 convert_element_type.129
  259.5 1.4 copy.90
  260.9 4.4 all-to-all-start.13
  265.3 3.2 convolution_convert_fusion.2
  269.3 1.3 fusion.25
  271.8 17.3 %all-to-all-done.13 = bf16[4,4,3,48,384]{4,3,1,2,0:T(8,128)(2,1)} async-done(((bf16[4,4,3,48,384]{4,3,1,2,0:T(8,128)(2,1)}), bf16[4,4,3,48,384]{4,3,1,2,0:T(8,128)(2,1)}, u32[]{:S(2)}, u32[]{:S(2)}) %all-to-all-start.13) | async-done | bytes 1769504 | tf_op jit(solution)/shard_map/all_to_all | solution.py:383
  289.1 5.3 all-to-all-start.8
  294.4 2.6 reduce_sum.195
  297.1 1.8 copy.72
  298.9 16.4 %all-to-all-done.8 = bf16[4,128,768]{2,1,0:T(8,128)(2,1)S(1)} async-done(((bf16[4,128,768]{2,1,0:T(8,128)(2,1)}), bf16[4,128,768]{2,1,0:T(8,128)(2,1)S(1)}, u32[]{:S(2)}, u32[]{:S(2)}) %all-to-all-start.8) | async-done | bytes 786464 | tf_op jit(solution)/shard_map/all_to_all | solution.py:377
  315.3 4.1 all-to-all-start.14
  319.4 2.7 copy.91
  322.1 10.8 %all-to-all-done.14 = bf16[4,3,48,384]{3,2,1,0:T(8,128)(2,1)} async-done(((bf16[4,3,48,384]{3,2,1,0:T(8,128)(2,1)}), bf16[4,3,48,384]{3,2,1,0:T(8,128)(2,1)}, u32[]{:S(2)}, u32[]{:S(2)}) %all-to-all-start.14) | async-done | bytes 442400 | tf_op jit(solution)/shard_map/all_to_all | solution.py:377
  332.9 4.6 all-to-all-start.11
  338.6 18.0 %all-to-all-done.11 = bf16[2,4,128,768]{3,2,1,0:T(8,128)(2,1)} async-done(((bf16[2,4,128,768]{3,2,1,0:T(8,128)(2,1)}), bf16[2,4,128,768]{3,2,1,0:T(8,128)(2,1)}, u32[]{:S(2)}, u32[]{:S(2)}) %all-to-all-start.11) | async-done | bytes 1572896 | tf_op jit(solution)/shard_map/all_to_all | solution.py:380
  357.5 3.7 all-to-all-start.15
  361.2 2.9 convert_reduce_fusion.1
  364.1 1.1 copy-done.2
  365.2 1.3 fusion.14
  366.5 6.2 all-to-all-done.15
  373.7 3.6 all-to-all-start.16
  377.4 3.2 fusion.7
  380.5 7.5 %all-to-all-done.16 = bf16[2,4,3,48,384]{4,3,2,1,0:T(8,128)(2,1)S(1)} async-done(((bf16[2,4,3,48,384]{4,3,2,1,0:T(8,128)(2,1)}), bf16[2,4,3,48,384]{4,3,2,1,0:T(8,128)(2,1)S(1)}, u32[]{:S(2)}, u32[]{:S(2)}) %all-to-all-start.16) | async-done | bytes 884768 | tf_op jit(solution)/shard_map/all_to_all | solution.py:380
  388.1 3.6 all-to-all-start.12
  392.6 21.3 %all-to-all-done.12 = bf16[4,128,768]{2,1,0:T(8,128)(2,1)S(1)} async-done(((bf16[4,128,768]{2,1,0:T(8,128)(2,1)}), bf16[4,128,768]{2,1,0:T(8,128)(2,1)S(1)}, u32[]{:S(2)}, u32[]{:S(2)}) %all-to-all-start.12) | async-done | bytes 786464 | tf_op jit(solution)/shard_map/all_to_all | solution.py:377
  413.9 3.6 broadcast_in_dim.24
  417.5 4.9 all-to-all-start.17
  423.4 2.8 convert_element_type.134
  426.3 72.8 %all-reduce = (f32[4,768]{1,0:T(4,128)S(1)}, f32[4]{0:T(128)S(1)}) all-reduce(f32[4,768]{1,0:T(4,128)S(1)} %pad_maximum_fusion, f32[4]{0:T(128)S(1)} %convert_reduce_fusion.4), channel_id=1, replica_groups=mesh['seq'=8,'ex'=4] {'seq','ex'}, use_global_device_ids=true, to_apply=%region_20.21 | all-reduce | flops 3076 | bytes 24608 | tf_op jit(solution)/shard_map/psum | solution.py:494
  500.3 1.3 convert_add_fusion.2
  502.2 1.3 convert_add_fusion.1
  503.6 8.3 %convert_bitcast_fusion = f32[4,4,48,3,2,384]{5,4,3,2,1,0:T(2,128)} fusion(bf16[4,2,4,3,48,384]{5,1,3,4,2,0:T(2,128)(2,1)} %all-to-all-done.17), kind=kLoop, calls=%fused_computation | loop fusion | flops 1769472 | bytes 10616832 | tf_op jit(solution)/shard_map/convert_element_type | solution.py:490
  511.9 9.8 %reshape.322 = f32[768,2304]{1,0:T(8,128)} reshape(f32[4,4,48,3,2,384]{5,4,3,2,1,0:T(2,128)} %convert_bitcast_fusion) | data formatting | bytes 14155776 | tf_op jit(solution)/shard_map/convert_element_type | solution.py:490
  521.8 206.5 %all-reduce.7.cloned.1.call-done = (bf16[1,768,3072]{2,1,0:T(8,128)(2,1)}, bf16[1,3072,768]{2,1,0:T(8,128)(2,1)}) async-done(((bf16[1,768,3072]{2,1,0:T(8,128)(2,1)}, bf16[1,3072,768]{2,1,0:T(8,128)(2,1)}), (bf16[1,768,3072]{2,1,0:T(8,128)(2,1)}, bf16[1,3072,768]{2,1,0:T(8,128)(2,1)})) %all-reduce.7.cloned.1.call-update) | async-done | bytes 9437200 | tf_op jit(solution)/shard_map/psum | solution.py:496
  728.3 7.5 %broadcast_in_dim.26 = f32[1,768,3072]{2,1,0:T(8,128)} convert(bf16[1,768,3072]{2,1,0:T(8,128)(2,1)} %get-tuple-element.50) | non-fusion elementwise | flops 2359296 | bytes 14155776 | tf_op jit(solution)/shard_map/broadcast_in_dim | solution.py:502
  735.8 4.5 broadcast_in_dim.28
  (129 shorter events, 20.0 us)
Async XLA Ops:
  7.2 112.3 %copy-start = (bf16[768,768]{1,0:T(8,128)(2,1)S(1)}, bf16[768,768]{1,0:T(8,128)(2,1)}, u32[]{:S(2)}) copy-start(bf16[768,768]{1,0:T(8,128)(2,1)} %param.20) | copy-start | bytes 3538948
  7.2 2.0 copy-start.3
  9.3 31.2 %copy-start.16 = (f32[768]{0:T(1024)S(1)}, f32[768]{0:T(1024)}, u32[]{:S(2)}) copy-start(f32[768]{0:T(1024)} %param.15) | copy-start | bytes 9220
  9.3 31.2 %copy-start.38 = (f32[768]{0:T(1024)S(1)}, f32[768]{0:T(1024)}, u32[]{:S(2)}) copy-start(f32[768]{0:T(1024)} %param.16) | copy-start | bytes 9220
  35.6 8.7 %all-to-all-start.3 = ((s32[4,1,128]{2,1,0:T(1,128)}), s32[4,1,128]{2,1,0:T(1,128)S(1)}, u32[]{:S(2)}, u32[]{:S(2)}) async-start(s32[4,1,128]{2,1,0:T(1,128)} %bitcast.14), calls=%async_computation.3 | async-start | bytes 4096 | tf_op jit(solution)/shard_map/all_to_all | solution.py:377
  39.0 0.6 copy-start.28
  39.0 6.5 copy-start.24
  40.5 5.0 copy-start.26
  45.5 20.9 %all-to-all-start.1 = ((bf16[2,512,768]{2,1,0:T(8,128)(2,1)}), bf16[2,512,768]{2,1,0:T(8,128)(2,1)S(1)}, u32[]{:S(2)}, u32[]{:S(2)}) async-start(bf16[2,512,768]{2,1,0:T(8,128)(2,1)} %broadcast_in_dim.20), calls=%async_computation.1 | async-start | bytes 3145728 | tf_op jit(solution)/shard_map/all_to_all | solution.py:380
  66.4 1.1 copy-start.8
  67.5 34.9 %all-to-all-start.5 = ((bf16[4,128,768]{2,1,0:T(8,128)(2,1)}), bf16[4,128,768]{2,1,0:T(8,128)(2,1)S(1)}, u32[]{:S(2)}, u32[]{:S(2)}) async-start(bf16[4,128,768]{2,1,0:T(8,128)(2,1)} %convert_element_type.117), calls=%async_computation.5 | async-start | bytes 1572864 | tf_op jit(solution)/shard_map/all_to_all | solution.py:377
  71.0 35.0 %copy-start.21 = (s32[4,48]{1,0:T(4,128)}, s32[4,48]{1,0:T(4,128)S(1)}, u32[]{:S(2)}) copy-start(s32[4,48]{1,0:T(4,128)S(1)} %multiply_add_fusion) | copy-start | bytes 2308
  102.4 4.1 copy-start.6
  102.4 11.5 %all-to-all-start.2 = ((bf16[2,4,128,384]{3,2,1,0:T(8,128)(2,1)}), bf16[2,4,128,384]{3,2,1,0:T(8,128)(2,1)S(1)}, u32[]{:S(2)}, u32[]{:S(2)}) async-start(bf16[2,4,128,384]{3,2,1,0:T(8,128)(2,1)} %bitcast.154), calls=%async_computation.2 | async-start | bytes 1572864 | tf_op jit(solution)/shard_map/all_to_all | solution.py:380
  106.0 1.6 copy-start.18
  113.9 20.2 %all-to-all-start.6 = ((bf16[4,192,768]{2,1,0:T(8,128)(2,1)}), bf16[4,192,768]{2,1,0:T(8,128)(2,1)}, u32[]{:S(2)}, u32[]{:S(2)}) async-start(bf16[4,192,768]{2,1,0:T(8,128)(2,1)} %bitcast.150), calls=%async_computation.6 | async-start | bytes 2359296 | tf_op jit(solution)/shard_map/all_to_all | solution.py:383
  122.6 0.7 copy-start.15
  122.6 0.7 copy-start.39
  122.9 0.7 copy-start.19
  122.9 0.7 copy-start.22
  186.2 19.4 %copy-start.20 = (s32[4,1,128]{2,1,0:T(1,128)S(1)}, s32[4,1,128]{2,1,0:T(1,128)}, u32[]{:S(2)}) copy-start(s32[4,1,128]{2,1,0:T(1,128)} %copy-done.18) | copy-start | bytes 6148
  186.2 19.4 %copy-start.23 = (s32[4,48]{1,0:T(4,128)S(1)}, s32[4,48]{1,0:T(4,128)}, u32[]{:S(2)}) copy-start(s32[4,48]{1,0:T(4,128)} %copy-done.21) | copy-start | bytes 2308
  206.7 1.2 copy-start.5
  206.7 1.2 copy-start.30
  206.7 1.7 copy-start.7
  208.4 0.6 copy-start.32
  209.0 0.9 copy-start.14
  223.9 37.0 %all-to-all-start.7 = ((bf16[4,192,768]{2,1,0:T(8,128)(2,1)}), bf16[4,192,768]{2,1,0:T(8,128)(2,1)S(1)}, u32[]{:S(2)}, u32[]{:S(2)}) async-start(bf16[4,192,768]{2,1,0:T(8,128)(2,1)} %bitcast.164), calls=%async_computation.7 | async-start | bytes 2359296 | tf_op jit(solution)/shard_map/all_to_all | solution.py:383
  260.9 28.2 %all-to-all-start.13 = ((bf16[4,4,3,48,384]{4,3,1,2,0:T(8,128)(2,1)}), bf16[4,4,3,48,384]{4,3,1,2,0:T(8,128)(2,1)}, u32[]{:S(2)}, u32[]{:S(2)}) async-start(bf16[4,4,3,48,384]{4,3,1,2,0:T(8,128)(2,1)} %bitcast.143), calls=%async_computation.13 | async-start | bytes 3538944 | tf_op jit(solution)/shard_map/all_to_all | solution.py:383
  265.3 158.1 %all-reduce.5.cloned.1.call-start = ((), (), s32[]{:S(2)}) async-start(), calls=%async_computation.18 | async-start | bytes 2359296 | tf_op jit(solution)/shard_map/psum | solution.py:492
  268.5 459.7 %all-reduce.7.cloned.1.call-start = ((), (), s32[]{:S(2)}) async-start(), calls=%async_computation.19 | async-start | bytes 18874368 | tf_op jit(solution)/shard_map/psum | solution.py:496
  269.3 1.4 copy-start.10
  289.1 26.2 %all-to-all-start.8 = ((bf16[4,128,768]{2,1,0:T(8,128)(2,1)}), bf16[4,128,768]{2,1,0:T(8,128)(2,1)S(1)}, u32[]{:S(2)}, u32[]{:S(2)}) async-start(bf16[4,128,768]{2,1,0:T(8,128)(2,1)} %bitcast.160), calls=%async_computation.8 | async-start | bytes 1572864 | tf_op jit(solution)/shard_map/all_to_all | solution.py:377
  315.3 6.8 copy-start.12
  315.3 17.6 %all-to-all-start.14 = ((bf16[4,3,48,384]{3,2,1,0:T(8,128)(2,1)}), bf16[4,3,48,384]{3,2,1,0:T(8,128)(2,1)}, u32[]{:S(2)}, u32[]{:S(2)}) async-start(bf16[4,3,48,384]{3,2,1,0:T(8,128)(2,1)} %copy.72), calls=%async_computation.14 | async-start | bytes 884736 | tf_op jit(solution)/shard_map/all_to_all | solution.py:377
  332.9 23.7 %all-to-all-start.11 = ((bf16[2,4,128,768]{3,2,1,0:T(8,128)(2,1)}), bf16[2,4,128,768]{3,2,1,0:T(8,128)(2,1)}, u32[]{:S(2)}, u32[]{:S(2)}) async-start(bf16[2,4,128,768]{3,2,1,0:T(8,128)(2,1)} %bitcast.146), calls=%async_computation.11 | async-start | bytes 3145728 | tf_op jit(solution)/shard_map/all_to_all | solution.py:380
  357.5 15.3 %all-to-all-start.15 = ((bf16[4,3,48,384]{3,2,1,0:T(8,128)(2,1)}), bf16[4,3,48,384]{3,2,1,0:T(8,128)(2,1)S(1)}, u32[]{:S(2)}, u32[]{:S(2)}) async-start(bf16[4,3,48,384]{3,2,1,0:T(8,128)(2,1)} %broadcast_in_dim.22), calls=%async_computation.15 | async-start | bytes 884736 | tf_op jit(solution)/shard_map/all_to_all | solution.py:377
  361.1 4.1 copy-start.17
  361.2 4.1 copy-start.29
  361.2 4.1 copy-start.37
  364.1 1.1 copy-start.2
  366.5 10.8 %copy-start.25 = (f32[512]{0:T(512)S(1)}, f32[512]{0:T(512)}, u32[]{:S(2)}) copy-start(f32[512]{0:T(512)} %copy-done.24) | copy-start | bytes 6148
  366.5 10.8 %copy-start.27 = (f32[512]{0:T(512)S(1)}, f32[512]{0:T(512)}, u32[]{:S(2)}) copy-start(f32[512]{0:T(512)} %copy-done.26) | copy-start | bytes 6148
  366.5 10.8 %copy-start.31 = (f32[512]{0:T(512)S(1)}, f32[512]{0:T(512)}, u32[]{:S(2)}) copy-start(f32[512]{0:T(512)} %copy-done.30) | copy-start | bytes 6148
  366.5 10.8 %copy-start.33 = (f32[512]{0:T(512)S(1)}, f32[512]{0:T(512)}, u32[]{:S(2)}) copy-start(f32[512]{0:T(512)} %copy-done.32) | copy-start | bytes 6148
  373.7 14.3 %all-to-all-start.16 = ((bf16[2,4,3,48,384]{4,3,2,1,0:T(8,128)(2,1)}), bf16[2,4,3,48,384]{4,3,2,1,0:T(8,128)(2,1)S(1)}, u32[]{:S(2)}, u32[]{:S(2)}) async-start(bf16[2,4,3,48,384]{4,3,2,1,0:T(8,128)(2,1)} %broadcast_in_dim.23), calls=%async_computation.16 | async-start | bytes 1769472 | tf_op jit(solution)/shard_map/all_to_all | solution.py:380
  388.1 25.8 %all-to-all-start.12 = ((bf16[4,128,768]{2,1,0:T(8,128)(2,1)}), bf16[4,128,768]{2,1,0:T(8,128)(2,1)S(1)}, u32[]{:S(2)}, u32[]{:S(2)}) async-start(bf16[4,128,768]{2,1,0:T(8,128)(2,1)} %bitcast.152), calls=%async_computation.12 | async-start | bytes 1572864 | tf_op jit(solution)/shard_map/all_to_all | solution.py:377
  417.5 5.0 copy-start.40
  417.5 5.0 copy-start.34
  417.5 86.1 %all-to-all-start.17 = ((bf16[4,2,4,3,48,384]{5,1,3,4,2,0:T(2,128)(2,1)}), bf16[4,2,4,3,48,384]{5,1,3,4,2,0:T(2,128)(2,1)}, u32[]{:S(2)}, u32[]{:S(2)}) async-start(bf16[4,2,4,3,48,384]{5,1,3,4,2,0:T(2,128)(2,1)} %broadcast_in_dim.24), calls=%async_computation.17 | async-start | bytes 7077888 | tf_op jit(solution)/shard_map/all_to_all | solution.py:383
  422.6 3.7 copy-start.35
  422.6 3.7 copy-start.36
  422.6 77.7 %copy-start.4 = (f32[4,128,768]{2,1,0:T(8,128)S(1)}, f32[4,128,768]{2,1,0:T(8,128)}, u32[]{:S(2)}) copy-start(f32[4,128,768]{2,1,0:T(8,128)} %param.12) | copy-start | bytes 4718596
  422.6 77.7 %copy-start.13 = (bf16[4,128,768]{2,1,0:T(8,128)(2,1)S(1)}, bf16[4,128,768]{2,1,0:T(8,128)(2,1)}, u32[]{:S(2)}) copy-start(bf16[4,128,768]{2,1,0:T(8,128)(2,1)} %copy-done.12) | copy-start | bytes 2359300
  500.3 2.0 copy-start.9
  728.3 7.5 %copy-start.11 = (bf16[1,3072,768]{2,1,0:T(8,128)(2,1)S(1)}, bf16[1,3072,768]{2,1,0:T(8,128)(2,1)}, u32[]{:S(2)}) copy-start(bf16[1,3072,768]{2,1,0:T(8,128)(2,1)} %get-tuple-element.51) | copy-start | bytes 14155780
  735.8 4.5 copy-start.1
Sparse Core Ops, SparseCore 0:
  272.1 151.2 all-reduce.4
  428.5 299.7 all-reduce.6

commit v2 on v1

v2 whole, which is shorter than its diff:
```python
import functools
import math

import jax
import jax.numpy as jnp
from jax import lax
from jax.experimental import pallas as pl
from jax.experimental.pallas import tpu as pltpu
from jax.sharding import PartitionSpec as P

HEADS = 12
HEAD = 64
MOST = 48
PAIR = 2 * HEAD
EPSILON = 1e-05
NEGATIVE = -1e30
LOW = jnp.bfloat16
FULL = jnp.float32
VMEM_LIMIT = 60 * 1024 * 1024
NN = (((1,), (0,)), ((), ()))
NT = (((1,), (1,)), ((), ()))
TN = (((0,), (0,)), ((), ()))


def dot(a, b, dims=NN):
    return lax.dot_general(a, b, dims, preferred_element_type=FULL)


def loop(first, last, unroll, body, carry):
    if unroll:
        for index in range(first, last):
            carry = body(index, carry)
        return carry
    return lax.fori_loop(first, last, body, carry)


def each(count, unroll, body):
    def step(index, carry):
        body(index)
        return carry

    loop(0, count, unroll, step, 0)


def tile_mask(shape, low_row, key_first, query_first, diagonal):
    key_pos = key_first + lax.broadcasted_iota(jnp.int32, shape, 0)
    allowed = key_pos >= low_row
    if diagonal:
        query_pos = query_first + lax.broadcasted_iota(jnp.int32, shape, 1)
        allowed = allowed & (key_pos <= query_pos)
    return allowed


def head_lanes(value, head):
    lane = lax.broadcasted_iota(jnp.int32, value.shape, 1)
    return jnp.where((lane // HEAD) == head, value, jnp.zeros_like(value))


def place_of(own_ref, j, k, team, rows, local):
    row = lax.rem(own_ref[0] + (rows - k), rows)
    member = lax.rem(own_ref[1] + (team + j) % team, team)
    return pl.ds(pl.multiple_of((row * team + member) * local, local), local)


def standard(value):
    center = value - jnp.mean(value, -1, keepdims=True)
    spread = jnp.mean(center * center, -1, keepdims=True)
    inverse = lax.rsqrt(spread + EPSILON)
    return center * inverse, inverse


def standard_back(grad, gain, unit, inverse):
    u = grad * gain
    lean = jnp.mean(u * unit, -1, keepdims=True)
    back = (u - jnp.mean(u, -1, keepdims=True) - unit * lean) * inverse
    return back, jnp.sum(grad * unit, 0), jnp.sum(grad, 0)


def attend_kernel(team, rows, local, block, unroll, own_ref, *refs):
    pieces, refs = refs[: team * rows], refs[team * rows :]
    gain_ref, bias_ref, wq_ref, wk_ref, wv_ref, low_ref = refs[:6]
    x_ref, q_ref, k_ref, v_ref, ot_ref, log_ref = refs[6:12]
    o_refs = refs[12 : 12 + team]
    vt_ref, o_ref = refs[12 + team :]
    length = x_ref.shape[0]
    count = length // block

    @pl.when(pl.program_id(0) == 0)
    def _():
        for j in range(team):
            for k in range(rows):
                unit, _ = standard(pieces[j * rows + k][...].astype(FULL))
                normed = unit * gain_ref[...] + bias_ref[...]
                x_ref[place_of(own_ref, -j, k, team, rows, local), :] = normed.astype(LOW)

    def project(index):
        span = pl.ds(index * block, block)
        x = x_ref[span, :]
        q_ref[span, :] = (dot(x, wq_ref[...]).astype(LOW) * LOW(HEAD**-0.5)).astype(LOW)
        k_ref[span, :] = dot(x, wk_ref[...]).astype(LOW)
        v = dot(x, wv_ref[...]).astype(LOW)
        v_ref[span, :] = v
        vt_ref[:, span] = v.T

    each(count, unroll, project)

    def one_block(qi):
        span = pl.ds(qi * block, block)
        low_row = low_ref[:, span]
        q = q_ref[span, :]
        masked = [head_lanes(q, head) for head in range(2)]

        def tile(kj, state, diagonal):
            keys = pl.ds(kj * block, block)
            k = k_ref[keys, :]
            allowed = tile_mask((block, block), low_row, kj * block, qi * block, diagonal)
            after = []
            for head in range(2):
                scores = jnp.where(allowed, dot(k, masked[head], NT), NEGATIVE)
                high = jnp.max(scores, 0, keepdims=True)
                if state is not None:
                    high = jnp.maximum(high, state[head][0])
                weights = jnp.exp(scores - high)
                total = jnp.sum(weights, 0, keepdims=True)
                summed = dot(vt_ref[pl.ds(head * HEAD, HEAD), keys], weights.astype(LOW))
                if state is not None:
                    fade = jnp.exp(state[head][0] - high)
                    total = total + state[head][1] * fade
                    summed = summed + state[head][2] * fade
                after.append((high, total, summed))
            return tuple(after)

        state = loop(
            0, qi, unroll, lambda kj, carry: tile(kj, carry, False), tile(qi, None, True)
        )
        done = []
        for head in range(2):
            high, total, summed = state[head]
            log_ref[0, pl.ds(head, 1), span] = high + jnp.log(total)
            done.append(summed / total)
        both = jnp.concatenate(done, 0)
        ot_ref[:, span] = both
        o_ref[span, :] = both.T.astype(LOW)

    each(count, unroll, one_block)
    for j in range(team):
        for k in range(rows):
            o_refs[j][k] = o_ref[place_of(own_ref, j, k, team, rows, local), :]


def attend_back_kernel(team, rows, local, block, unroll, own_ref, *refs):
    pieces, refs = refs[:team], refs[team:]
    x_ref, wq_ref, wk_ref, wv_ref, wo_ref, low_ref = refs[:6]
    q_ref, k_ref, v_ref, ot_ref, log_ref, gw_ref = refs[6:12]
    gx_refs = refs[12 : 12 + team]
    b_ref, g_ref, kt_ref, delta_ref, dqt_ref, d_ref, sum_ref = refs[12 + team :]
    length, width = x_ref.shape
    count = length // block
    scale = HEAD**-0.5
    pair = pl.program_id(0)

    @pl.when(pair == 0)
    def _():
        for j in range(team):
            for k in range(rows):
                b_ref[place_of(own_ref, -j, k, team, rows, local), :] = pieces[j][k]
        sum_ref[...] = jnp.zeros_like(sum_ref)

    def prepare(index):
        span = pl.ds(index * block, block)
        kt_ref[:, span] = k_ref[span, :].T
        g = dot(b_ref[span, :], wo_ref[...], NT).astype(LOW)
        g_ref[span, :] = g
        product = g.astype(FULL).T * ot_ref[:, span]
        for head in range(2):
            part = product[head * HEAD : (head + 1) * HEAD]
            delta_ref[pl.ds(head, 1), span] = jnp.sum(part, 0, keepdims=True)
        dqt_ref[:, span] = jnp.zeros((PAIR, block), FULL)

    each(count, unroll, prepare)

    def one_block(kj):
        keys = pl.ds(kj * block, block)
        k = k_ref[keys, :]
        v = v_ref[keys, :]

        def tile(qi, carry, diagonal):
            grad_k, grad_v = carry
            span = pl.ds(qi * block, block)
            q = q_ref[span, :]
            g = g_ref[span, :]
            allowed = tile_mask(
                (block, block), low_ref[:, span], kj * block, qi * block, diagonal
            )
            for head in range(2):
                qm = head_lanes(q, head)
                gm = head_lanes(g, head)
                part = pl.ds(head * HEAD, HEAD)
                probs = jnp.exp(dot(k, qm, NT) - log_ref[0, pl.ds(head, 1), span])
                probs = jnp.where(allowed, probs, 0.0)
                grad_probs = dot(v, gm, NT)
                grad_scores = (probs * (grad_probs - delta_ref[pl.ds(head, 1), span])).astype(LOW)
                grad_v = grad_v + dot(probs.astype(LOW), gm)
                grad_k = grad_k + dot(grad_scores, qm)
                dqt_ref[part, span] += dot(kt_ref[part, keys], grad_scores)
            return grad_k, grad_v

        zero = jnp.zeros((block, PAIR), FULL)
        grad_k, grad_v = loop(
            kj + 1,
            count,
            unroll,
            lambda qi, carry: tile(qi, carry, False),
            tile(kj, (zero, zero), True),
        )
        d_ref[keys, PAIR : 2 * PAIR] = grad_k.astype(LOW)
        d_ref[keys, 2 * PAIR :] = grad_v.astype(LOW)

    each(count, unroll, one_block)

    weight = jnp.concatenate([wq_ref[...], wk_ref[...], wv_ref[...]], 1)

    def spread(index):
        span = pl.ds(index * block, block)
        d_ref[span, :PAIR] = (dqt_ref[:, span] * scale).T.astype(LOW)
        sum_ref[span, :] += dot(d_ref[span, :], weight, NT)

    each(count, unroll, spread)

    grads = dot(x_ref[...], d_ref[...], TN)
    for which in range(3):
        gw_ref[which] = grads[:, which * PAIR : (which + 1) * PAIR].astype(LOW)
    gw_ref[3] = dot(ot_ref[...].astype(LOW), b_ref[...]).T.astype(LOW)

    @pl.when(pair == pl.num_programs(0) - 1)
    def _():
        for j in range(team):
            for k in range(rows):
                gx_refs[j][k] = sum_ref[place_of(own_ref, j, k, team, rows, local), :].astype(LOW)


def fixed(*shape):
    return pl.BlockSpec(shape, lambda p, own: (0,) * len(shape), pipeline_mode=pl.Buffered(1))


def attention_specs(length, width, pairs, all_pairs):
    weight = lambda which: pl.BlockSpec(
        (width, PAIR), lambda p, own: (0, which * all_pairs + own[1] * pairs + p)
    )
    columns = lambda: pl.BlockSpec((length, PAIR), lambda p, own: (0, p))
    across = pl.BlockSpec((PAIR, length), lambda p, own: (p, 0))
    logs = pl.BlockSpec((1, 2, length), lambda p, own: (p, 0, 0))
    return weight, columns, across, logs


def attend(own, pieces, gain, bias, weights, low, team, rows, pairs):
    local, width = pieces[0].shape
    length = team * rows * local
    share = pairs * PAIR
    block = math.gcd(length, 256)
    unroll = length // block <= 4
    weight, columns, across, logs = attention_specs(length, width, pairs, pairs * team)
    shape = jax.ShapeDtypeStruct
    return pl.pallas_call(
        functools.partial(attend_kernel, team, rows, local, block, unroll),
        grid_spec=pltpu.PrefetchScalarGridSpec(
            num_scalar_prefetch=1,
            grid=(pairs,),
            in_specs=[fixed(local, width)] * len(pieces)
            + [fixed(1, width)] * 2
            + [weight(0), weight(1), weight(2), fixed(1, length)],
            out_specs=[pl.BlockSpec((length, width), lambda p, own: (0, 0))]
            + [columns(), columns(), columns(), across, logs]
            + [pl.BlockSpec((rows, local, PAIR), lambda p, own: (0, 0, p))] * team,
            scratch_shapes=[pltpu.VMEM((PAIR, length), LOW), pltpu.VMEM((length, PAIR), LOW)],
        ),
        out_shape=[shape((length, width), LOW)]
        + [shape((length, share), LOW)] * 3
        + [shape((share, length), FULL), shape((pairs, 2, length), FULL)]
        + [shape((rows, local, share), LOW)] * team,
        compiler_params=pltpu.CompilerParams(vmem_limit_bytes=VMEM_LIMIT),
        cost_estimate=pl.CostEstimate(
            flops=2 * length * width * 3 * share + 8 * length * length * share,
            bytes_accessed=4 * length * width + 12 * length * share,
            transcendentals=length * length * pairs,
        ),
        name="attend",
    )(own, *pieces, gain[None], bias[None], weights, weights, weights, low)


def attend_back(own, pieces, x, weights, out_weights, low, q, k, v, ot, logs_in, team, rows, pairs):
    length, width = x.shape
    local = length // (team * rows)
    share = pairs * PAIR
    block = math.gcd(length, 256)
    unroll = length // block <= 4
    weight, columns, across, logs = attention_specs(length, width, pairs, pairs * team)
    shape = jax.ShapeDtypeStruct
    out = pl.BlockSpec((rows, local, width), lambda p, own: (0, 0, 0))
    results = pl.pallas_call(
        functools.partial(attend_back_kernel, team, rows, local, block, unroll),
        grid_spec=pltpu.PrefetchScalarGridSpec(
            num_scalar_prefetch=1,
            grid=(pairs,),
            in_specs=[fixed(rows, local, width)] * team
            + [fixed(length, width), weight(0), weight(1), weight(2)]
            + [pl.BlockSpec((PAIR, width), lambda p, own: (own[1] * pairs + p, 0))]
            + [fixed(1, length), columns(), columns(), columns(), across, logs],
            out_specs=[pl.BlockSpec((4, width, PAIR), lambda p, own: (0, 0, p))] + [out] * team,
            scratch_shapes=[
                pltpu.VMEM((length, width), LOW),
                pltpu.VMEM((length, PAIR), LOW),
                pltpu.VMEM((PAIR, length), LOW),
                pltpu.VMEM((2, length), FULL),
                pltpu.VMEM((PAIR, length), FULL),
                pltpu.VMEM((length, 3 * PAIR), LOW),
                pltpu.VMEM((length, width), FULL),
            ],
        ),
        out_shape=[shape((4, width, share), LOW)] + [shape((rows, local, width), LOW)] * team,
        compiler_params=pltpu.CompilerParams(vmem_limit_bytes=VMEM_LIMIT),
        cost_estimate=pl.CostEstimate(
            flops=4 * length * width * 4 * share + 20 * length * length * share,
            bytes_accessed=6 * length * width + 24 * length * share,
            transcendentals=length * length * pairs,
        ),
        name="attend_back",
    )(own, *pieces, x, weights, weights, weights, out_weights, low, q, k, v, ot, logs_in)
    return results[0], results[1:]


GELU_SCALE = math.sqrt(2.0 / math.pi)
GELU_CUBE = 0.044715


def expert_kernel(count, first, last, *refs):
    x_refs, refs = refs[:count], refs[count:]
    g_refs, refs = refs[:count], refs[count:]
    up_ref, down_ref, refs = refs[0], refs[1], refs[2:]
    if not first:
        y_in, gx_in, refs = refs[0], refs[1], refs[2:]
    gup_ref, gdown_ref, refs = refs[0], refs[1], refs[2:]
    if last:
        y_outs, refs = refs[:count], refs[count:]
        gx_outs, refs = refs[:count], refs[count:]
        y_sum, gx_sum, refs = refs[0], refs[1], refs[2:]
    else:
        y_sum, gx_sum, refs = refs[0], refs[1], refs[2:]
    x_ref, g_ref = refs
    step = pl.program_id(0)
    size = x_refs[0].shape[0]

    @pl.when(step == 0)
    def _():
        for index in range(count):
            span = pl.ds(index * size, size)
            x_ref[span, :] = x_refs[index][...]
            g_ref[span, :] = g_refs[index][...]
        if first:
            y_sum[...] = jnp.zeros_like(y_sum)
            gx_sum[...] = jnp.zeros_like(gx_sum)
        else:
            y_sum[...] = y_in[...]
            gx_sum[...] = gx_in[...]

    x = x_ref[...]
    g = g_ref[...]
    inner = dot(x, up_ref[...])
    square = inner * inner
    curve = jnp.tanh(GELU_SCALE * inner * (1.0 + GELU_CUBE * square))
    half = 0.5 + 0.5 * curve
    active = (inner * half).astype(LOW)
    slope = half + (0.5 * GELU_SCALE) * inner * (1.0 - curve * curve) * (
        1.0 + (3.0 * GELU_CUBE) * square
    )
    grad_inner = (dot(g, down_ref[...], NT) * slope).astype(LOW)
    gdown_ref[...] = dot(active, g, TN).astype(LOW)
    gup_ref[...] = dot(x, grad_inner, TN).astype(LOW)
    y_sum[...] += dot(active, down_ref[...])
    gx_sum[...] += dot(grad_inner, up_ref[...], NT)

    if last:

        @pl.when(step == pl.num_programs(0) - 1)
        def _():
            for index in range(count):
                span = pl.ds(index * size, size)
                y_outs[index][...] = y_sum[span, :].astype(LOW)
                gx_outs[index][...] = gx_sum[span, :].astype(LOW)


def expert(xs, gs, up, down, part, parts, sums):
    count = len(xs)
    size, width = xs[0].shape
    hidden = up.shape[1] // parts
    block = math.gcd(hidden, 512)
    steps = hidden // block
    first, last = part == 0, part == parts - 1
    rows = pl.BlockSpec((size, width), lambda f: (0, 0))
    whole = pl.BlockSpec((count * size, width), lambda f: (0, 0))
    shape = jax.ShapeDtypeStruct
    sum_shape = shape((count * size, width), FULL)
    in_specs = [rows] * (2 * count) + [
        pl.BlockSpec((width, block), lambda f: (0, f + part * steps)),
        pl.BlockSpec((block, width), lambda f: (f + part * steps, 0)),
    ]
    out_specs = [
        pl.BlockSpec((width, block), lambda f: (0, f)),
        pl.BlockSpec((block, width), lambda f: (f, 0)),
    ]
    out_shape = [shape((width, hidden), LOW), shape((hidden, width), LOW)]
    scratch = []
    if not first:
        in_specs += [whole] * 2
    if last:
        out_specs += [rows] * (2 * count)
        out_shape += [shape((size, width), LOW)] * (2 * count)
        scratch += [pltpu.VMEM(sum_shape.shape, FULL)] * 2
    else:
        out_specs += [whole] * 2
        out_shape += [sum_shape] * 2
    results = pl.pallas_call(
        functools.partial(expert_kernel, count, first, last),
        grid=(steps,),
        in_specs=in_specs,
        out_specs=out_specs,
        out_shape=out_shape,
        scratch_shapes=scratch + [pltpu.VMEM((count * size, width), LOW)] * 2,
        compiler_params=pltpu.CompilerParams(vmem_limit_bytes=VMEM_LIMIT),
        cost_estimate=pl.CostEstimate(
            flops=12 * count * size * width * hidden,
            bytes_accessed=8 * width * hidden + 8 * count * size * width,
            transcendentals=count * size * hidden,
        ),
        name="expert",
    )(*xs, *gs, up, down, *sums)
    return results[0], results[1], results[2:]


def add_low(a, b):
    return (a.astype(FULL) + b.astype(FULL)).astype(LOW)


def pick(value, index):
    return lax.dynamic_index_in_dim(value, index, 0, keepdims=False)


def ring_scatter(value, size, place, send):
    total = pick(value, (place + size - 1) % size)
    for step in range(size - 1):
        total = add_low(send(total), pick(value, (place + 2 * size - 2 - step) % size))
    return total


def ring_gather(value, size, place, send):
    out = jnp.zeros((size,) + value.shape, value.dtype)
    out = lax.dynamic_update_index_in_dim(out, value, place, 0)
    for step in range(size - 1):
        value = send(value)
        out = lax.dynamic_update_index_in_dim(out, value, (place + size - 1 - step) % size, 0)
    return out


def per_device(
    block_input, segment_ids, expert_ids, ln1_gain, ln1_bias, ln2_gain, ln2_bias,
    w_qkv, w_attn_out, w_in, w_down, grad_out,
):
    rows, local, width = block_input.shape
    seq = lax.axis_size("seq")
    experts = lax.axis_size("ex")
    team = seq // rows
    length = seq * local
    owned = rows * local
    pairs = -(-HEADS // (2 * team))
    share = pairs * PAIR
    padded = share * team
    place = lax.axis_index("seq")
    mine = lax.axis_index("ex")
    row, member = place // team, place % team
    slots = rows * MOST

    def row_send(value, k):
        if k % rows == 0:
            return value
        pattern = [(a * team + b, (a + k) % rows * team + b) for a in range(rows) for b in range(team)]
        return lax.ppermute(value, "seq", pattern)

    def team_send(value, j):
        if j % team == 0:
            return value
        pattern = [(a * team + b, a * team + (b + j) % team) for a in range(rows) for b in range(team)]
        return lax.ppermute(value, "seq", pattern)

    def swap(value, axis, m):
        if m == 0:
            return value
        return lax.ppermute(value, axis, [(a, a ^ m) for a in range(lax.axis_size(axis))])

    def home(pieces):
        stacked = jnp.stack([row_send(piece, rows - k) for k, piece in enumerate(pieces)])
        twice = jnp.concatenate([stacked, stacked], 0)
        return lax.dynamic_slice_in_dim(twice, (rows - row) % rows, rows, 0)

    center = (block_input - jnp.mean(block_input, -1, keepdims=True)).astype(LOW)
    owned_x = [row_send(pick(center, (row + k) % rows), k) for k in range(rows)]
    pieces = [team_send(piece, j) for j in range(team) for piece in owned_x]

    labels = jnp.pad(expert_ids.reshape(rows, 1, local), ((0, 0), (0, 15), (0, width - local)))
    carried = jnp.concatenate([grad_out.astype(LOW), labels.astype(LOW)], 1)
    carried, pieces = lax.optimization_barrier((carried, pieces))
    owned_g = jnp.stack([row_send(pick(carried, (row + k) % rows), k) for k in range(rows)])
    grad_low = owned_g[:, :local]
    chosen = owned_g[:, local, :local].astype(jnp.int32)

    segments = lax.dynamic_slice_in_dim(segment_ids, row, 1, 0)[0]
    lows = jnp.sum((segments[:, None] < segments[None, :]).astype(jnp.int32), 0)[None, :]

    weights, out_weights = w_qkv, w_attn_out
    if padded != width:
        extra = padded - width
        weights = jnp.pad(w_qkv.reshape(width, 3, width), ((0, 0), (0, 0), (0, extra)))
        weights = weights.reshape(width, 3 * padded)
        out_weights = jnp.pad(w_attn_out, ((0, extra), (0, 0)))

    own = jnp.stack([row, member]).astype(jnp.int32)
    results = attend(own, pieces, ln1_gain, ln1_bias, weights, lows, team, rows, pairs)
    full, q, k, v, ot, logs = results[:6]
    branch = 0.0
    for j, part in enumerate(results[6:]):
        first = (member + team - j) % team * share
        weight = lax.dynamic_slice_in_dim(out_weights, first, share, 0)
        branch = branch + dot(team_send(part, j).reshape(owned, share), weight)

    residual = jnp.concatenate(owned_x, 0).astype(FULL)
    middle = residual + branch
    unit_two, inverse_two = standard(middle)
    normed_two = (unit_two * ln2_gain + ln2_bias).astype(LOW)

    relative = chosen ^ mine
    onehot = (relative[..., None] == jnp.arange(experts, dtype=jnp.int32)).astype(jnp.int32)
    rank = jnp.cumsum(onehot, 1) - onehot
    target = relative * MOST + jnp.sum(rank * onehot, -1)
    route = (
        (target[:, None, :] == jnp.arange(experts * MOST, dtype=jnp.int32)[None, :, None])
        .astype(LOW)
        .reshape(rows, experts, MOST, local)
    )
    named = (chosen[..., None] == jnp.arange(experts, dtype=jnp.int32)).astype(FULL)
    counts = jnp.sum(named, (0, 1))

    def dispatch(value):
        placed = jnp.einsum(
            "remt,rtd->ermd", route, value.reshape(rows, local, width), preferred_element_type=FULL
        )
        placed = placed.astype(LOW).reshape(experts, slots, width)
        return [swap(placed[m], "ex", m) for m in range(experts)]

    def collect(parts):
        returned = jnp.stack([swap(part, "ex", m) for m, part in enumerate(parts)])
        return jnp.einsum(
            "remt,ermd->rtd",
            route,
            returned.reshape(experts, rows, MOST, width),
            preferred_element_type=FULL,
        ).reshape(owned, width)

    grad_arrived = dispatch(grad_low)
    arrived = dispatch(normed_two)

    def shared_sum(value, rows_first):
        along_team = lambda v: team_send(v, 1)
        along_rows = lambda v: row_send(v, 1)
        cut = value.shape[0] // (team * rows)
        if rows_first:
            value = value.reshape((rows, team, cut) + value.shape[1:])
            value = ring_scatter(value, rows, row, along_rows)
            value = ring_scatter(value, team, member, along_team)
            value = ring_gather(value, team, member, along_team)
            value = ring_gather(value, rows, row, along_rows)
        else:
            value = value.reshape((team, rows, cut) + value.shape[1:])
            value = ring_scatter(value, team, member, along_team)
            value = ring_scatter(value, rows, row, along_rows)
            value = ring_gather(value, rows, row, along_rows)
            value = ring_gather(value, team, member, along_team)
        return value.reshape((-1,) + value.shape[3:]).astype(FULL)

    up_low, down_low, sums = expert(arrived, grad_arrived, w_in[0], w_down[0], 0, 2, ())
    up_high, down_high, sums = expert(arrived, grad_arrived, w_in[0], w_down[0], 1, 2, sums)
    produced, grad_rows = sums[:experts], sums[experts:]
    grad_up = jnp.concatenate([shared_sum(up_low, False), shared_sum(up_high, False)], 1)
    grad_down = jnp.concatenate([shared_sum(down_low, False), shared_sum(down_high, True)], 0)

    back_two, grad_gain_two, grad_bias_two = standard_back(
        collect(grad_rows), ln2_gain, unit_two, inverse_two
    )
    grad_branch = (back_two + grad_low.reshape(owned, width).astype(FULL)).astype(LOW)
    grad_branch = grad_branch.reshape(rows, local, width)
    grad_weights, grad_full = attend_back(
        own, [team_send(grad_branch, j) for j in range(team)], full, weights, out_weights, lows,
        q, k, v, ot, logs, team, rows, pairs,
    )

    change = (branch + collect(produced)).astype(LOW).reshape(rows, local, width)
    block_output = block_input + home(list(change)).astype(FULL)

    unit_one, inverse_one = standard(residual)
    grad_normed_one = sum(
        team_send(part, j).astype(FULL) for j, part in enumerate(grad_full)
    ).reshape(owned, width)
    back_one, grad_gain_one, grad_bias_one = standard_back(
        grad_normed_one, ln1_gain, unit_one, inverse_one
    )
    grad_change = (back_two + back_one).astype(LOW).reshape(rows, local, width)
    grad_input = grad_out + home(list(grad_change)).astype(FULL)

    cut = width // (experts * rows)
    bits = [1 << b for b in range(experts.bit_length() - 1)]
    value = grad_weights.reshape(4, experts, rows, cut, share).swapaxes(0, 1)
    for bit in bits:
        halves = value.reshape((value.shape[0] // 2, 2) + value.shape[1:])
        on = (mine // bit) % 2
        keep = lax.dynamic_index_in_dim(halves, on, 1, keepdims=False)
        give = lax.dynamic_index_in_dim(halves, 1 - on, 1, keepdims=False)
        value = add_low(keep, swap(give, "ex", bit))
    value = value[0].swapaxes(0, 1)
    value = sum(row_send(pick(value, (row + k) % rows), k).astype(FULL) for k in range(rows)).astype(LOW)
    out = jnp.zeros((rows,) + value.shape, LOW)
    for k in range(rows):
        out = lax.dynamic_update_index_in_dim(out, row_send(value, k), (row + rows - k) % rows, 0)
    value = ring_gather(out, team, member, lambda v: team_send(v, 1))[None]
    for bit in reversed(bits):
        on = (mine // bit) % 2
        other = swap(value, "ex", bit)
        pair = jnp.where(on == 0, jnp.stack([value, other], 1), jnp.stack([other, value], 1))
        value = pair.reshape((-1,) + pair.shape[2:])
    value = value.reshape(experts, team, rows, 4, cut, share)
    grad_qkv = jnp.transpose(value[:, :, :, :3], (0, 2, 4, 3, 1, 5)).reshape(width, 3, padded)
    grad_qkv = grad_qkv[..., :width].reshape(width, 3 * width).astype(FULL)
    grad_attn_out = jnp.transpose(value[:, :, :, 3], (1, 4, 0, 2, 3)).reshape(padded, width)
    grad_attn_out = grad_attn_out[:width].astype(FULL)

    small = jnp.stack(
        [
            grad_gain_one, grad_bias_one, grad_gain_two, grad_bias_two,
            jnp.pad(counts, (0, width - experts)),
        ]
    )
    for axis, size in (("ex", experts), ("seq", seq)):
        for b in range(size.bit_length() - 1):
            small = small + swap(small, axis, 1 << b)
    load = small[4, :experts] * (experts / (rows * length * experts))
    return (
        block_output, grad_input, grad_qkv, grad_attn_out, small[0], small[1], small[2], small[3],
        grad_up[None], grad_down[None], load,
    )


def solution(mesh):
    tokens = P("ex", "seq", None)
    expert_axis = P("ex", None, None)
    return jax.shard_map(
        per_device,
        mesh=mesh,
        in_specs=(
            tokens, P("ex", None), tokens, P(), P(), P(), P(), P(), P(),
            expert_axis, expert_axis, tokens,
        ),
        out_specs=(
            tokens, tokens, P(), P(), P(), P(), P(), P(), expert_axis, expert_axis, P(),
        ),
        check_vma=False,
    )
```

time: 757 us -> 650 us (0.86)
  blocking collectives: 153 us -> 0 us
  starting transfers between devices: 56.2 us -> 88.2 us
  local copies, waits for them, and re-layouts: 40 us -> 55.2 us
  between operations: 14.9 us -> 2.29 us
  other arithmetic: 50.7 us -> 60.1 us
    ppermute x0 -> x79, waiting for transfers between devices: none -> 339 us  [the longest x42 184 us: row_send(): return lax.ppermute(value, 'seq', pattern)]
    psum x2 -> x0, waiting for transfers between devices: 207 us -> none  [the longest x1 206 us: per_device(): lax.psum(grad_up, 'seq').astype(FULL)]
    all_to_all x14 -> x0, waiting for transfers between devices: 131 us -> none  [the longest x6 58.1 us: swap_rows(): lax.all_to_all(value, 'seq', 0, 0, tiled=True, axis_index_groups=across_r...]
    ppermute x0 -> x79, starting transfers between devices: none -> 88.2 us  [the longest x42 51.2 us: row_send(): return lax.ppermute(value, 'seq', pattern)]
    all_to_all x4 -> x0, blocking collectives: 80.2 us -> none  [the longest x2 40.1 us: swap_experts(): return lax.all_to_all(value, 'ex', 0, 0, tiled=True)]
    psum x1 -> x0, blocking collectives: 72.8 us -> none  [per_device(): small, counts = lax.psum((small, counts), ('seq', 'ex'))]
    all_to_all x14 -> x0, starting transfers between devices: 56.1 us -> none  [the longest x6 23.5 us: swap_rows(): lax.all_to_all(value, 'seq', 0, 0, tiled=True, axis_index_groups=across_r...]
    convert_element_type x3, local copies, waits for them, and re-layouts: 12 us -> 22.9 us  [the longest x2 21.1 us: per_device(): grad_qkv = grad_qkv[..., :width].reshape(width, 3 * width).astype(FULL)]
  transfers between devices with their start and end apart: 16 -> 79, of which waited for: 13 -> 38; matrix products, arithmetic and copies ran while one was open for 10% -> 12% of each run, Pallas kernels for 7% -> 4%
where the time goes in v2:
time: 650 us; the launch traced here: 642 us
  waiting for transfers between devices  339 us (52%)
  Pallas kernels  90 us (14%)
  starting transfers between devices  88.2 us (14%)
  other arithmetic  60.1 us (9%)
  local copies, waits for them, and re-layouts  55.2 us (8%)
  matrix products  6.83 us (1%)
    ppermute x42, waiting for transfers between devices, row_send(): return lax.ppermute(value, 'seq', pattern)  184 us
    ppermute x16, waiting for transfers between devices, team_send(): return lax.ppermute(value, 'seq', pattern)  92.9 us
    ppermute x21, waiting for transfers between devices, swap(): lax.ppermute(value, axis, [(a, a ^ m) for a in range(lax.axis_size(axis))])  63.1 us
    ppermute x42, starting transfers between devices, row_send(): return lax.ppermute(value, 'seq', pattern)  51.2 us
    pallas_call x2, Pallas kernels, expert(): pl.pallas_call(functools.partial(expert_kernel, count, first, last), grid...  35.3 us
    pallas_call x1, Pallas kernels, attend_back(): pl.pallas_call(functools.partial(attend_back_kernel, team, rows, local, b...  28 us
    pallas_call x1, Pallas kernels, attend(): pl.pallas_call(functools.partial(attend_kernel, team, rows, local, block,...  26.7 us
    convert_element_type x2, local copies, waits for them, and re-layouts, per_device(): grad_qkv = grad_qkv[..., :width].reshape(width, 3 * width).astype(FULL)  21.1 us
  transfers between devices with their start and end apart: 79, of which 38 were waited for; matrix products, arithmetic and copies ran while one was open for 12% of the time, Pallas kernels for 4%

profile of v2, /device:TPU:0, one launch (start us, length us, event | category | flops | bytes accessed | tf_op | source)
XLA Modules:
  0.0 642.1 jit_solution(301933521539016028)
XLA Ops:
  3.6 2.0 dynamic-slice_bitcast_fusion.12
  5.6 5.0 collective-permute-start.2
  20.1 4.4 collective-permute-done.refs_1_
  31.0 2.3 fusion.80
  35.7 3.2 collective-permute-done.6.refs_7_
  39.6 26.7 %attend.1 = (bf16[1024,768]{1,0:T(8,128)(2,1)}, bf16[1024,384]{1,0:T(8,128)(2,1)}, bf16[1024,384]{1,0:T(8,128)(2,1)}, bf16[1024,384]{1,0:T(8,128)(2,1)}, f32[384...) custom-call(s32[2]{0:T(128)} %pad_add_fusion.own_ref, ...), custom_call_target="tpu_custom_call" | custom-call | flops 5033164800 | bytes 7864320 | tf_op jit(solution)/shard_map/attend/pallas_call | solution.py:264
  69.2 5.1 collective-permute-start.9
  74.3 2.1 collective-permute-start.8
  78.1 13.9 %collective-permute-done.9 = bf16[144,768]{1,0:T(8,128)(2,1)S(1)} collective-permute-done((bf16[144,768]{1,0:T(8,128)(2,1)S(1)}, bf16[144,768]{1,0:T(8,128)(2,1)S(1)}, u32[]{:S(2)}, u32[]{:S(2)}) %collective-permute-start.9) | collective-permute-done | bytes 221216 | tf_op jit(solution)/shard_map/ppermute | solution.py:486
  96.1 3.0 fusion.86
  104.7 4.9 collective-permute-done.16.refs_7_
  109.6 7.1 %collective-permute-done.12.refs_2_ = bf16[192,768]{1,0:T(8,128)(2,1)S(1)} collective-permute-done((bf16[192,768]{1,0:T(8,128)(2,1)S(1)}, bf16[192,768]{1,0:T(8,128)(2,1)S(1)}, u32[]{:S(2)}, u32[]{:S(2)}) %collective-permute-start.12) | collective-permute-done | bytes 294944 | tf_op jit(solution)/shard_map/ppermute | solution.py:497
  116.7 5.5 collective-permute-done.13.refs_3_
  122.9 16.8 %expert.2 = (bf16[768,1536]{1,0:T(8,128)(2,1)}, bf16[1536,768]{1,0:T(8,128)(2,1)}, f32[768,768]{1,0:T(8,128)}, f32[768,768]{1,0:T(8,128)}) custom-call(bf16[192,768]{1,0:T(8,128)(2,1)} %bitcast.390, bf16[192,768]{1,0:T(8,128)(2,1)} %copy-done.49, bf16[192,768]{1,0:T(8,128)(2,1)} %copy-done.50, bf16[192,768]{1,0:T(8,128)(2,1)} %copy-done.51, ...), custom_call_target="tpu_custom_call" | custom-call | flops 10871635968 | bytes 14155776 | tf_op jit(solution)/shard_map/expert/pallas_call | solution.py:422
  139.7 18.5 %expert.3 = (bf16[768,1536]{1,0:T(8,128)(2,1)}, bf16[1536,768]{1,0:T(8,128)(2,1)}, bf16[192,768]{1,0:T(8,128)(2,1)}, bf16[192,768]{1,0:T(8,128)(2,1)}, bf16[192,...) custom-call(bf16[192,768]{1,0:T(8,128)(2,1)} %bitcast.391, ...), custom_call_target="tpu_custom_call" | custom-call | flops 10871635968 | bytes 14155776 | tf_op jit(solution)/shard_map/expert/pallas_call | solution.py:422
  162.3 2.4 dynamic-slice_bitcast_fusion.1
  168.2 6.3 collective-permute-done.18
  178.2 2.0 collective-permute-done.25
  180.2 6.6 %collective-permute-done.24 = bf16[192,768]{1,0:T(8,128)(2,1)S(1)} collective-permute-done((bf16[192,768]{1,0:T(8,128)(2,1)}, bf16[192,768]{1,0:T(8,128)(2,1)S(1)}, u32[]{:S(2)}, u32[]{:S(2)}) %collective-permute-start.24) | collective-permute-done | bytes 294944 | tf_op jit(solution)/shard_map/ppermute | solution.py:497
  190.9 11.5 %collective-permute-done.20 = bf16[128,768]{1,0:T(8,128)(2,1)S(1)} collective-permute-done((bf16[128,768]{1,0:T(8,128)(2,1)S(1)}, bf16[128,768]{1,0:T(8,128)(2,1)S(1)}, u32[]{:S(2)}, u32[]{:S(2)}) %collective-permute-start.20) | collective-permute-done | bytes 196640 | tf_op jit(solution)/shard_map/ppermute | solution.py:486
  202.9 11.4 %collective-permute-done.21 = bf16[128,768]{1,0:T(8,128)(2,1)S(1)} collective-permute-done((bf16[128,768]{1,0:T(8,128)(2,1)S(1)}, bf16[128,768]{1,0:T(8,128)(2,1)S(1)}, u32[]{:S(2)}, u32[]{:S(2)}) %collective-permute-start.21) | collective-permute-done | bytes 196640 | tf_op jit(solution)/shard_map/ppermute | solution.py:486
  214.3 8.6 %collective-permute-done.22 = bf16[128,768]{1,0:T(8,128)(2,1)S(1)} collective-permute-done((bf16[128,768]{1,0:T(8,128)(2,1)S(1)}, bf16[128,768]{1,0:T(8,128)(2,1)S(1)}, u32[]{:S(2)}, u32[]{:S(2)}) %collective-permute-start.22) | collective-permute-done | bytes 196640 | tf_op jit(solution)/shard_map/ppermute | solution.py:486
  224.9 2.0 fusion.36
  227.0 42.5 %collective-permute-done.26.refs_1_ = bf16[4,128,768]{2,1,0:T(8,128)(2,1)S(1)} collective-permute-done((bf16[4,128,768]{2,1,0:T(8,128)(2,1)S(1)}, bf16[4,128,768]{2,1,0:T(8,128)(2,1)S(1)}, u32[]{:S(2)}, u32[]{:S(2)}) %collective-permute-start.26) | collective-permute-done | bytes 786464 | tf_op jit(solution)/shard_map/ppermute | solution.py:492
  270.4 28.0 %attend_back.1 = (bf16[4,768,384]{2,1,0:T(8,128)(2,1)}, bf16[4,128,768]{2,1,0:T(8,128)(2,1)}, bf16[4,128,768]{2,1,0:T(8,128)(2,1)}) custom-call(s32[2]{0:T(128)} %pad_add_fusion.own_ref, bf16[4,128,768]{2,1,0:T(8,128)(2,1)} %bitcast.385, bf16[4,128,768]{2,1,0:T(8,128)(2,1)} %copy-done.44, bf16[1024,768]{1,0:T(8,128)(2,1)} %get-tuple-element.66.refs_2_, ...), custom_call_target="tpu_custom_call" | custom-call | flops 12884901888 | bytes 14155776 | tf_op jit(solution)/shard_map/attend_back/pallas_call | solution.py:300
  299.0 1.9 copy.121
  305.6 2.0 fusion.4
  307.9 1.8 fusion.35
  311.6 5.7 collective-permute-done.56
  317.4 6.2 collective-permute-done.48
  323.9 18.7 %collective-permute-done.64 = bf16[192,768]{1,0:T(8,128)(2,1)S(1)} collective-permute-done((bf16[192,768]{1,0:T(8,128)(2,1)S(1)}, bf16[192,768]{1,0:T(8,128)(2,1)S(1)}, u32[]{:S(2)}, u32[]{:S(2)}) %collective-permute-start.64) | collective-permute-done | bytes 294944 | tf_op jit(solution)/shard_map/ppermute | solution.py:486
  342.7 6.2 collective-permute-done.57
  349.7 5.5 collective-permute-done.49
  356.0 5.5 collective-permute-done.65
  363.4 3.3 multiply_reduce_fusion
  376.7 2.8 fusion.14
  380.4 3.1 collective-permute-done.45
  383.5 4.4 collective-permute-start.46
  387.9 1.8 collective-permute-done.46
  391.7 2.4 collective-permute-start.28
  397.2 2.1 collective-permute-start.30
  401.6 18.8 %collective-permute-start.51 = (bf16[96,1536]{1,0:T(8,128)(2,1)S(1)}, bf16[96,1536]{1,0:T(8,128)(2,1)S(1)}, u32[]{:S(2)}, u32[]{:S(2)}) collective-permute-start(bf16[96,1536]{1,0:T(8,128)(2,1)S(1)} %get-tuple-element.162), channel_id=1, source_target_pairs={{0,8},{4,12},{8,16},{12,20},{16,24},{20,28},{24,0},{28,4},{1,9},{5... | collective-permute-start | bytes 884744 | tf_op jit(solution)/shard_map/ppermute | solution.py:486
  429.4 4.8 collective-permute-start.52
  434.9 18.8 %collective-permute-done.60 = bf16[96,1536]{1,0:T(8,128)(2,1)S(1)} collective-permute-done((bf16[96,1536]{1,0:T(8,128)(2,1)S(1)}, bf16[96,1536]{1,0:T(8,128)(2,1)S(1)}, u32[]{:S(2)}, u32[]{:S(2)}) %collective-permute-start.60) | collective-permute-done | bytes 294944 | tf_op jit(solution)/shard_map/ppermute | solution.py:486
  453.6 6.3 collective-permute-done.52
  460.0 6.4 %collective-permute-done.68 = bf16[192,768]{1,0:T(8,128)(2,1)S(1)} collective-permute-done((bf16[192,768]{1,0:T(8,128)(2,1)S(1)}, bf16[192,768]{1,0:T(8,128)(2,1)S(1)}, u32[]{:S(2)}, u32[]{:S(2)}) %collective-permute-start.68) | collective-permute-done | bytes 294944 | tf_op jit(solution)/shard_map/ppermute | solution.py:486
  466.7 3.9 collective-permute-start.35
  470.6 2.1 collective-permute-done.61
  472.8 6.2 collective-permute-done.53
  479.0 6.9 %collective-permute-done.35 = bf16[4,48,384]{2,1,0:T(8,128)(2,1)S(1)} collective-permute-done((bf16[4,48,384]{2,1,0:T(8,128)(2,1)S(1)}, bf16[4,48,384]{2,1,0:T(8,128)(2,1)S(1)}, u32[]{:S(2)}, u32[]{:S(2)}) %collective-permute-start.35) | collective-permute-done | bytes 147488 | tf_op jit(solution)/shard_map/ppermute | solution.py:486
  485.9 2.3 collective-permute-start.62
  488.2 18.3 %collective-permute-done.34 = bf16[4,48,384]{2,1,0:T(8,128)(2,1)S(1)} collective-permute-done((bf16[4,48,384]{2,1,0:T(8,128)(2,1)S(1)}, bf16[4,48,384]{2,1,0:T(8,128)(2,1)S(1)}, u32[]{:S(2)}, u32[]{:S(2)}) %collective-permute-start.34) | collective-permute-done | bytes 147488 | tf_op jit(solution)/shard_map/ppermute | solution.py:486
  508.9 6.5 %collective-permute-done.36 = bf16[4,48,384]{2,1,0:T(8,128)(2,1)S(1)} collective-permute-done((bf16[4,48,384]{2,1,0:T(8,128)(2,1)S(1)}, bf16[4,48,384]{2,1,0:T(8,128)(2,1)S(1)}, u32[]{:S(2)}, u32[]{:S(2)}) %collective-permute-start.36) | collective-permute-done | bytes 147488 | tf_op jit(solution)/shard_map/ppermute | solution.py:486
  515.4 7.1 %collective-permute-done.37 = bf16[4,48,384]{2,1,0:T(8,128)(2,1)S(1)} collective-permute-done((bf16[4,48,384]{2,1,0:T(8,128)(2,1)S(1)}, bf16[4,48,384]{2,1,0:T(8,128)(2,1)S(1)}, u32[]{:S(2)}, u32[]{:S(2)}) %collective-permute-start.37) | collective-permute-done | bytes 147488 | tf_op jit(solution)/shard_map/ppermute | solution.py:486
  523.6 4.0 collective-permute-done.38
  529.1 45.3 %collective-permute-done.39 = bf16[4,4,48,384]{3,2,1,0:T(8,128)(2,1)S(1)} collective-permute-done((bf16[4,4,48,384]{3,2,1,0:T(8,128)(2,1)S(1)}, bf16[4,4,48,384]{3,2,1,0:T(8,128)(2,1)S(1)}, u32[]{:S(2)}, u32[]{:S(2)}) %collective-permute-start.39) | collective-permute-done | bytes 589856 | tf_op jit(solution)/shard_map/ppermute | solution.py:492
  576.9 23.6 %collective-permute-done.40 = bf16[1,2,4,4,48,384]{5,4,3,2,1,0:T(8,128)(2,1)S(1)} collective-permute-done((bf16[1,2,4,4,48,384]{5,4,3,2,1,0:T(8,128)(2,1)S(1)}, bf16[1,2,4,4,48,384]{5,4,3,2,1,0:T(8,128)(2,1)S(1)}, u32[]{:S(2)}, u32[]{:S(2)}) %collective-permute-start.40) | collective-permute-done | bytes 1179680 | tf_op jit(solution)/shard_map/ppermute | solution.py:497
  601.3 5.0 fusion
  606.3 4.5 fusion.1
  612.9 3.7 convert_bitcast_fusion
  616.8 11.3 %copy.123 = f32[4,4,48,3,2,384]{5,4,3,2,1,0:T(2,128)} copy(f32[4,4,48,3,2,384]{5,2,3,1,4,0:T(8,128)} %convert_bitcast_fusion) | data formatting | bytes 14155776 | tf_op jit(solution)/shard_map/convert_element_type | solution.py:639
  628.1 9.8 %reshape.430 = f32[768,2304]{1,0:T(8,128)} reshape(f32[4,4,48,3,2,384]{5,4,3,2,1,0:T(2,128)} %copy.123) | data formatting | bytes 14155776 | tf_op jit(solution)/shard_map/convert_element_type | solution.py:639
  637.9 1.8 copy.124
  639.9 2.0 copy.125
  (371 shorter events, 104.7 us)
Async XLA Ops:
  5.6 23.6 %collective-permute-start.2 = (bf16[128,768]{1,0:T(8,128)(2,1)}, bf16[128,768]{1,0:T(8,128)(2,1)S(1)}, u32[]{:S(2)}, u32[]{:S(2)}) collective-permute-start(bf16[128,768]{1,0:T(8,128)(2,1)} %get-tuple-element.189), channel_id=1, source_target_pairs={{0,24},{4,28},{8,0},{12,4},{16,8},{20,12},{24,16},{28,20},{1,25},{... | collective-permute-start | bytes 589832 | tf_op jit(solution)/shard_map/ppermute | solution.py:486
  10.7 17.0 %collective-permute-start.1 = (bf16[128,768]{1,0:T(8,128)(2,1)}, bf16[128,768]{1,0:T(8,128)(2,1)}, u32[]{:S(2)}, u32[]{:S(2)}) collective-permute-start(bf16[128,768]{1,0:T(8,128)(2,1)} %get-tuple-element.190), channel_id=1, source_target_pairs={{0,16},{4,20},{8,24},{12,28},{16,0},{20,4},{24,8},{28,12},{1,17},{... | collective-permute-start | bytes 589832 | tf_op jit(solution)/shard_map/ppermute | solution.py:486
  10.7 13.9 %collective-permute-start = (bf16[128,768]{1,0:T(8,128)(2,1)}, bf16[128,768]{1,0:T(8,128)(2,1)}, u32[]{:S(2)}, u32[]{:S(2)}) collective-permute-start(bf16[128,768]{1,0:T(8,128)(2,1)} %get-tuple-element.191), channel_id=1, source_target_pairs={{0,8},{4,12},{8,16},{12,20},{16,24},{20,28},{24,0},{28,4},{1,9},{5... | collective-permute-start | bytes 589832 | tf_op jit(solution)/shard_map/ppermute | solution.py:486
  11.7 22.2 %collective-permute-start.3 = (bf16[128,768]{1,0:T(8,128)(2,1)S(1)}, bf16[128,768]{1,0:T(8,128)(2,1)}, u32[]{:S(2)}, u32[]{:S(2)}) collective-permute-start(bf16[128,768]{1,0:T(8,128)(2,1)S(1)} %get-tuple-element.45.refs_0_), channel_id=1, source_target_pairs={{0,4},{4,0},{8,12},{12,8},{16,20},{20,16},{24,28},{28,24},{1,5},{5... | collective-permute-start | bytes 589832 | tf_op jit(solution)/shard_map/ppermute | solution.py:492
  66.3 29.8 %collective-permute-start.7 = (bf16[4,128,384]{2,1,0:T(8,128)(2,1)}, bf16[4,128,384]{2,1,0:T(8,128)(2,1)}, u32[]{:S(2)}, u32[]{:S(2)}) collective-permute-start(bf16[4,128,384]{2,1,0:T(8,128)(2,1)} %get-tuple-element.54), channel_id=1, source_target_pairs={{0,4},{4,0},{8,12},{12,8},{16,20},{20,16},{24,28},{28,24},{1,5},{5... | collective-permute-start | bytes 1179656 | tf_op jit(solution)/shard_map/ppermute | solution.py:492
  67.9 10.2 %collective-permute-start.10 = (bf16[144,768]{1,0:T(8,128)(2,1)S(1)}, bf16[144,768]{1,0:T(8,128)(2,1)S(1)}, u32[]{:S(2)}, u32[]{:S(2)}) collective-permute-start(bf16[144,768]{1,0:T(8,128)(2,1)S(1)} %get-tuple-element.179), channel_id=1, source_target_pairs={{0,24},{4,28},{8,0},{12,4},{16,8},{20,12},{24,16},{28,20},{1,25},{... | collective-permute-start | bytes 663560 | tf_op jit(solution)/shard_map/ppermute | solution.py:486
  69.2 22.9 %collective-permute-start.9 = (bf16[144,768]{1,0:T(8,128)(2,1)S(1)}, bf16[144,768]{1,0:T(8,128)(2,1)S(1)}, u32[]{:S(2)}, u32[]{:S(2)}) collective-permute-start(bf16[144,768]{1,0:T(8,128)(2,1)S(1)} %get-tuple-element.180), channel_id=1, source_target_pairs={{0,16},{4,20},{8,24},{12,28},{16,0},{20,4},{24,8},{28,12},{1,17},{... | collective-permute-start | bytes 663560 | tf_op jit(solution)/shard_map/ppermute | solution.py:486
  74.3 17.8 %collective-permute-start.8 = (bf16[144,768]{1,0:T(8,128)(2,1)S(1)}, bf16[144,768]{1,0:T(8,128)(2,1)S(1)}, u32[]{:S(2)}, u32[]{:S(2)}) collective-permute-start(bf16[144,768]{1,0:T(8,128)(2,1)S(1)} %get-tuple-element.181), channel_id=1, source_target_pairs={{0,8},{4,12},{8,16},{12,20},{16,24},{20,28},{24,0},{28,4},{1,9},{5... | collective-permute-start | bytes 663560 | tf_op jit(solution)/shard_map/ppermute | solution.py:486
  94.2 10.4 %collective-permute-start.15 = (bf16[192,768]{1,0:T(8,128)(2,1)S(1)}, bf16[192,768]{1,0:T(8,128)(2,1)S(1)}, u32[]{:S(2)}, u32[]{:S(2)}) collective-permute-start(bf16[192,768]{1,0:T(8,128)(2,1)S(1)} %bitcast.392), channel_id=1, source_target_pairs={{0,2},{1,3},{2,0},{3,1},{4,6},{5,7},{6,4},{7,5},{8,10},{9,11},{10,... | collective-permute-start | bytes 884744 | tf_op jit(solution)/shard_map/ppermute | solution.py:497
  95.7 13.9 %collective-permute-start.16 = (bf16[192,768]{1,0:T(8,128)(2,1)S(1)}, bf16[192,768]{1,0:T(8,128)(2,1)S(1)}, u32[]{:S(2)}, u32[]{:S(2)}) collective-permute-start(bf16[192,768]{1,0:T(8,128)(2,1)S(1)} %bitcast.389), channel_id=1, source_target_pairs={{0,3},{1,2},{2,1},{3,0},{4,7},{5,6},{6,5},{7,4},{8,11},{9,10},{10,... | collective-permute-start | bytes 884744 | tf_op jit(solution)/shard_map/ppermute | solution.py:497
  101.7 14.9 %collective-permute-start.12 = (bf16[192,768]{1,0:T(8,128)(2,1)S(1)}, bf16[192,768]{1,0:T(8,128)(2,1)S(1)}, u32[]{:S(2)}, u32[]{:S(2)}) collective-permute-start(bf16[192,768]{1,0:T(8,128)(2,1)S(1)} %bitcast.395), channel_id=1, source_target_pairs={{0,2},{1,3},{2,0},{3,1},{4,6},{5,7},{6,4},{7,5},{8,10},{9,11},{10,... | collective-permute-start | bytes 884744 | tf_op jit(solution)/shard_map/ppermute | solution.py:497
  103.2 19.0 %collective-permute-start.13 = (bf16[192,768]{1,0:T(8,128)(2,1)S(1)}, bf16[192,768]{1,0:T(8,128)(2,1)S(1)}, u32[]{:S(2)}, u32[]{:S(2)}) collective-permute-start(bf16[192,768]{1,0:T(8,128)(2,1)S(1)} %bitcast.394), channel_id=1, source_target_pairs={{0,3},{1,2},{2,1},{3,0},{4,7},{5,6},{6,5},{7,4},{8,11},{9,10},{10,... | collective-permute-start | bytes 884744 | tf_op jit(solution)/shard_map/ppermute | solution.py:497
  158.3 9.9 %collective-permute-start.19 = (bf16[192,768]{1,0:T(8,128)(2,1)}, bf16[192,768]{1,0:T(8,128)(2,1)S(1)}, u32[]{:S(2)}, u32[]{:S(2)}) collective-permute-start(bf16[192,768]{1,0:T(8,128)(2,1)} %get-tuple-element.61), channel_id=1, source_target_pairs={{0,3},{1,2},{2,1},{3,0},{4,7},{5,6},{6,5},{7,4},{8,11},{9,10},{10,... | collective-permute-start | bytes 884744 | tf_op jit(solution)/shard_map/ppermute | solution.py:497
  159.7 14.8 %collective-permute-start.18 = (bf16[192,768]{1,0:T(8,128)(2,1)}, bf16[192,768]{1,0:T(8,128)(2,1)S(1)}, u32[]{:S(2)}, u32[]{:S(2)}) collective-permute-start(bf16[192,768]{1,0:T(8,128)(2,1)} %get-tuple-element.60), channel_id=1, source_target_pairs={{0,2},{1,3},{2,0},{3,1},{4,6},{5,7},{6,4},{7,5},{8,10},{9,11},{10,... | collective-permute-start | bytes 884744 | tf_op jit(solution)/shard_map/ppermute | solution.py:497
  160.2 14.8 %collective-permute-start.17 = (bf16[192,768]{1,0:T(8,128)(2,1)}, bf16[192,768]{1,0:T(8,128)(2,1)S(1)}, u32[]{:S(2)}, u32[]{:S(2)}) collective-permute-start(bf16[192,768]{1,0:T(8,128)(2,1)} %get-tuple-element.59), channel_id=1, source_target_pairs={{0,1},{1,0},{2,3},{3,2},{4,5},{5,4},{6,7},{7,6},{8,9},{9,8},{10,11... | collective-permute-start | bytes 884744 | tf_op jit(solution)/shard_map/ppermute | solution.py:497
  160.2 20.0 %collective-permute-start.25 = (bf16[192,768]{1,0:T(8,128)(2,1)}, bf16[192,768]{1,0:T(8,128)(2,1)S(1)}, u32[]{:S(2)}, u32[]{:S(2)}) collective-permute-start(bf16[192,768]{1,0:T(8,128)(2,1)} %get-tuple-element.65), channel_id=1, source_target_pairs={{0,3},{1,2},{2,1},{3,0},{4,7},{5,6},{6,5},{7,4},{8,11},{9,10},{10,... | collective-permute-start | bytes 884744 | tf_op jit(solution)/shard_map/ppermute | solution.py:497
  161.8 25.0 %collective-permute-start.24 = (bf16[192,768]{1,0:T(8,128)(2,1)}, bf16[192,768]{1,0:T(8,128)(2,1)S(1)}, u32[]{:S(2)}, u32[]{:S(2)}) collective-permute-start(bf16[192,768]{1,0:T(8,128)(2,1)} %get-tuple-element.64), channel_id=1, source_target_pairs={{0,2},{1,3},{2,0},{3,1},{4,6},{5,7},{6,4},{7,5},{8,10},{9,11},{10,... | collective-permute-start | bytes 884744 | tf_op jit(solution)/shard_map/ppermute | solution.py:497
  168.2 19.2 %collective-permute-start.23 = (bf16[192,768]{1,0:T(8,128)(2,1)S(1)}, bf16[192,768]{1,0:T(8,128)(2,1)S(1)}, u32[]{:S(2)}, u32[]{:S(2)}) collective-permute-start(bf16[192,768]{1,0:T(8,128)(2,1)S(1)} %copy-done.48), channel_id=1, source_target_pairs={{0,1},{1,0},{2,3},{3,2},{4,5},{5,4},{6,7},{7,6},{8,9},{9,8},{10,11... | collective-permute-start | bytes 884744 | tf_op jit(solution)/shard_map/ppermute | solution.py:497
  174.5 127.7 %collective-permute-start.55 = (bf16[4,96,1536]{2,1,0:T(8,128)(2,1)}, bf16[4,96,1536]{2,1,0:T(8,128)(2,1)}, u32[]{:S(2)}, u32[]{:S(2)}) collective-permute-start(bf16[4,96,1536]{2,1,0:T(8,128)(2,1)} %dynamic-slice_bitcast_fusion.1), channel_id=1, source_target_pairs={{0,4},{4,0},{8,12},{12,8},{16,20},{20,16},{24,28},{28,24},{1,5},{5... | collective-permute-start | bytes 3538952 | tf_op jit(solution)/shard_map/ppermute | solution.py:492
  175.0 130.5 %collective-permute-start.47 = (bf16[4,96,1536]{2,1,0:T(8,128)(2,1)}, bf16[4,96,1536]{2,1,0:T(8,128)(2,1)}, u32[]{:S(2)}, u32[]{:S(2)}) collective-permute-start(bf16[4,96,1536]{2,1,0:T(8,128)(2,1)} %dynamic-slice_bitcast_fusion.2), channel_id=1, source_target_pairs={{0,4},{4,0},{8,12},{12,8},{16,20},{20,16},{24,28},{28,24},{1,5},{5... | collective-permute-start | bytes 3538952 | tf_op jit(solution)/shard_map/ppermute | solution.py:492
  180.2 44.7 %collective-permute-start.71 = (bf16[2,192,768]{2,1,0:T(8,128)(2,1)S(1)}, bf16[2,192,768]{2,1,0:T(8,128)(2,1)S(1)}, u32[]{:S(2)}, u32[]{:S(2)}) collective-permute-start(bf16[2,192,768]{2,1,0:T(8,128)(2,1)S(1)} %dynamic-slice_bitcast_fusion.4), channel_id=1, source_target_pairs={{0,8},{4,12},{8,16},{12,20},{16,24},{20,28},{24,0},{28,4},{1,9},{5... | collective-permute-start | bytes 1769480 | tf_op jit(solution)/shard_map/ppermute | solution.py:486
  186.8 122.9 %collective-permute-start.63 = (bf16[4,192,768]{2,1,0:T(8,128)(2,1)}, bf16[4,192,768]{2,1,0:T(8,128)(2,1)}, u32[]{:S(2)}, u32[]{:S(2)}) collective-permute-start(bf16[4,192,768]{2,1,0:T(8,128)(2,1)} %dynamic-slice_bitcast_fusion), channel_id=1, source_target_pairs={{0,4},{4,0},{8,12},{12,8},{16,20},{20,16},{24,28},{28,24},{1,5},{5... | collective-permute-start | bytes 3538952 | tf_op jit(solution)/shard_map/ppermute | solution.py:492
  187.3 15.0 %collective-permute-start.20 = (bf16[128,768]{1,0:T(8,128)(2,1)S(1)}, bf16[128,768]{1,0:T(8,128)(2,1)S(1)}, u32[]{:S(2)}, u32[]{:S(2)}) collective-permute-start(bf16[128,768]{1,0:T(8,128)(2,1)S(1)} %get-tuple-element.188), channel_id=1, source_target_pairs={{0,24},{4,28},{8,0},{12,4},{16,8},{20,12},{24,16},{28,20},{1,25},{... | collective-permute-start | bytes 589832 | tf_op jit(solution)/shard_map/ppermute | solution.py:486
  202.4 11.9 %collective-permute-start.21 = (bf16[128,768]{1,0:T(8,128)(2,1)S(1)}, bf16[128,768]{1,0:T(8,128)(2,1)S(1)}, u32[]{:S(2)}, u32[]{:S(2)}) collective-permute-start(bf16[128,768]{1,0:T(8,128)(2,1)S(1)} %get-tuple-element.187), channel_id=1, source_target_pairs={{0,16},{4,20},{8,24},{12,28},{16,0},{20,4},{24,8},{28,12},{1,17},{... | collective-permute-start | bytes 589832 | tf_op jit(solution)/shard_map/ppermute | solution.py:486
  223.0 46.5 %collective-permute-start.26 = (bf16[4,128,768]{2,1,0:T(8,128)(2,1)S(1)}, bf16[4,128,768]{2,1,0:T(8,128)(2,1)S(1)}, u32[]{:S(2)}, u32[]{:S(2)}) collective-permute-start(bf16[4,128,768]{2,1,0:T(8,128)(2,1)S(1)} %bitcast.384), channel_id=1, source_target_pairs={{0,4},{4,0},{8,12},{12,8},{16,20},{20,16},{24,28},{28,24},{1,5},{5... | collective-permute-start | bytes 2359304 | tf_op jit(solution)/shard_map/ppermute | solution.py:492
  227.0 80.7 %collective-permute-start.72 = (bf16[2,192,768]{2,1,0:T(8,128)(2,1)}, bf16[2,192,768]{2,1,0:T(8,128)(2,1)}, u32[]{:S(2)}, u32[]{:S(2)}) collective-permute-start(bf16[2,192,768]{2,1,0:T(8,128)(2,1)} %fusion.36), channel_id=1, source_target_pairs={{0,8},{4,12},{8,16},{12,20},{16,24},{20,28},{24,0},{28,4},{1,9},{5... | collective-permute-start | bytes 1769480 | tf_op jit(solution)/shard_map/ppermute | solution.py:486
  298.4 64.9 %collective-permute-start.27 = (bf16[4,128,768]{2,1,0:T(8,128)(2,1)}, bf16[4,128,768]{2,1,0:T(8,128)(2,1)S(1)}, u32[]{:S(2)}, u32[]{:S(2)}) collective-permute-start(bf16[4,128,768]{2,1,0:T(8,128)(2,1)} %get-tuple-element.73), channel_id=1, source_target_pairs={{0,4},{4,0},{8,12},{12,8},{16,20},{20,16},{24,28},{28,24},{1,5},{5... | collective-permute-start | bytes 2359304 | tf_op jit(solution)/shard_map/ppermute | solution.py:492
  302.2 122.8 %collective-permute-start.31 = (bf16[2,4,4,48,384]{4,3,2,1,0:T(8,128)(2,1)}, bf16[2,4,4,48,384]{4,3,2,1,0:T(8,128)(2,1)}, u32[]{:S(2)}, u32[]{:S(2)}) collective-permute-start(bf16[2,4,4,48,384]{4,3,2,1,0:T(8,128)(2,1)} %dynamic-slice_bitcast_fusion.3), channel_id=1, source_target_pairs={{0,1},{1,0},{2,3},{3,2},{4,5},{5,4},{6,7},{7,6},{8,9},{9,8},{10,11... | collective-permute-start | bytes 3538952 | tf_op jit(solution)/shard_map/ppermute | solution.py:497
  305.5 11.8 %collective-permute-start.56 = (bf16[96,1536]{1,0:T(8,128)(2,1)S(1)}, bf16[96,1536]{1,0:T(8,128)(2,1)S(1)}, u32[]{:S(2)}, u32[]{:S(2)}) collective-permute-start(bf16[96,1536]{1,0:T(8,128)(2,1)S(1)} %dynamic-slice_bitcast_fusion.7), channel_id=1, source_target_pairs={{0,8},{4,12},{8,16},{12,20},{16,24},{20,28},{24,0},{28,4},{1,9},{5... | collective-permute-start | bytes 884744 | tf_op jit(solution)/shard_map/ppermute | solution.py:486
  307.7 15.9 %collective-permute-start.48 = (bf16[96,1536]{1,0:T(8,128)(2,1)S(1)}, bf16[96,1536]{1,0:T(8,128)(2,1)S(1)}, u32[]{:S(2)}, u32[]{:S(2)}) collective-permute-start(bf16[96,1536]{1,0:T(8,128)(2,1)S(1)} %dynamic-slice_bitcast_fusion.8), channel_id=1, source_target_pairs={{0,8},{4,12},{8,16},{12,20},{16,24},{20,28},{24,0},{28,4},{1,9},{5... | collective-permute-start | bytes 884744 | tf_op jit(solution)/shard_map/ppermute | solution.py:486
  309.7 52.6 %collective-permute-start.73 = (bf16[2,192,768]{2,1,0:T(8,128)(2,1)S(1)}, bf16[2,192,768]{2,1,0:T(8,128)(2,1)S(1)}, u32[]{:S(2)}, u32[]{:S(2)}) collective-permute-start(bf16[2,192,768]{2,1,0:T(8,128)(2,1)S(1)} %fusion.35), channel_id=1, source_target_pairs={{0,8},{4,12},{8,16},{12,20},{16,24},{20,28},{24,0},{28,4},{1,9},{5... | collective-permute-start | bytes 1769480 | tf_op jit(solution)/shard_map/ppermute | solution.py:486
  317.3 25.3 %collective-permute-start.64 = (bf16[192,768]{1,0:T(8,128)(2,1)S(1)}, bf16[192,768]{1,0:T(8,128)(2,1)S(1)}, u32[]{:S(2)}, u32[]{:S(2)}) collective-permute-start(bf16[192,768]{1,0:T(8,128)(2,1)S(1)} %dynamic-slice_bitcast_fusion.6), channel_id=1, source_target_pairs={{0,8},{4,12},{8,16},{12,20},{16,24},{20,28},{24,0},{28,4},{1,9},{5... | collective-permute-start | bytes 884744 | tf_op jit(solution)/shard_map/ppermute | solution.py:486
  323.6 25.3 %collective-permute-start.57 = (bf16[96,1536]{1,0:T(8,128)(2,1)S(1)}, bf16[96,1536]{1,0:T(8,128)(2,1)S(1)}, u32[]{:S(2)}, u32[]{:S(2)}) collective-permute-start(bf16[96,1536]{1,0:T(8,128)(2,1)S(1)} %fusion.49), channel_id=1, source_target_pairs={{0,8},{4,12},{8,16},{12,20},{16,24},{20,28},{24,0},{28,4},{1,9},{5... | collective-permute-start | bytes 884744 | tf_op jit(solution)/shard_map/ppermute | solution.py:486
  342.6 12.6 %collective-permute-start.49 = (bf16[96,1536]{1,0:T(8,128)(2,1)S(1)}, bf16[96,1536]{1,0:T(8,128)(2,1)S(1)}, u32[]{:S(2)}, u32[]{:S(2)}) collective-permute-start(bf16[96,1536]{1,0:T(8,128)(2,1)S(1)} %fusion.52), channel_id=1, source_target_pairs={{0,8},{4,12},{8,16},{12,20},{16,24},{20,28},{24,0},{28,4},{1,9},{5... | collective-permute-start | bytes 884744 | tf_op jit(solution)/shard_map/ppermute | solution.py:486
  348.9 12.6 %collective-permute-start.65 = (bf16[192,768]{1,0:T(8,128)(2,1)S(1)}, bf16[192,768]{1,0:T(8,128)(2,1)S(1)}, u32[]{:S(2)}, u32[]{:S(2)}) collective-permute-start(bf16[192,768]{1,0:T(8,128)(2,1)S(1)} %fusion.46), channel_id=1, source_target_pairs={{0,8},{4,12},{8,16},{12,20},{16,24},{20,28},{24,0},{28,4},{1,9},{5... | collective-permute-start | bytes 884744 | tf_op jit(solution)/shard_map/ppermute | solution.py:486
  355.2 36.5 %collective-permute-start.58 = (bf16[96,1536]{1,0:T(8,128)(2,1)}, bf16[96,1536]{1,0:T(8,128)(2,1)}, u32[]{:S(2)}, u32[]{:S(2)}) collective-permute-start(bf16[96,1536]{1,0:T(8,128)(2,1)} %fusion.48), channel_id=1, source_target_pairs={{0,8},{4,12},{8,16},{12,20},{16,24},{20,28},{24,0},{28,4},{1,9},{5... | collective-permute-start | bytes 884744 | tf_op jit(solution)/shard_map/ppermute | solution.py:486
  361.6 33.8 %collective-permute-start.50 = (bf16[96,1536]{1,0:T(8,128)(2,1)}, bf16[96,1536]{1,0:T(8,128)(2,1)}, u32[]{:S(2)}, u32[]{:S(2)}) collective-permute-start(bf16[96,1536]{1,0:T(8,128)(2,1)} %fusion.51), channel_id=1, source_target_pairs={{0,8},{4,12},{8,16},{12,20},{16,24},{20,28},{24,0},{28,4},{1,9},{5... | collective-permute-start | bytes 884744 | tf_op jit(solution)/shard_map/ppermute | solution.py:486
  362.3 34.9 %collective-permute-start.66 = (bf16[192,768]{1,0:T(8,128)(2,1)}, bf16[192,768]{1,0:T(8,128)(2,1)}, u32[]{:S(2)}, u32[]{:S(2)}) collective-permute-start(bf16[192,768]{1,0:T(8,128)(2,1)} %fusion.45), channel_id=1, source_target_pairs={{0,8},{4,12},{8,16},{12,20},{16,24},{20,28},{24,0},{28,4},{1,9},{5... | collective-permute-start | bytes 884744 | tf_op jit(solution)/shard_map/ppermute | solution.py:486
  389.7 10.8 %collective-permute-start.74 = (bf16[192,768]{1,0:T(8,128)(2,1)S(1)}, bf16[192,768]{1,0:T(8,128)(2,1)S(1)}, u32[]{:S(2)}, u32[]{:S(2)}) collective-permute-start(bf16[192,768]{1,0:T(8,128)(2,1)S(1)} %dynamic-slice_bitcast_fusion.5), channel_id=1, source_target_pairs={{0,4},{4,0},{8,12},{12,8},{16,20},{20,16},{24,28},{28,24},{1,5},{5... | collective-permute-start | bytes 884744 | tf_op jit(solution)/shard_map/ppermute | solution.py:492
  391.7 9.9 %collective-permute-start.28 = (bf16[128,768]{1,0:T(8,128)(2,1)S(1)}, bf16[128,768]{1,0:T(8,128)(2,1)S(1)}, u32[]{:S(2)}, u32[]{:S(2)}) collective-permute-start(bf16[128,768]{1,0:T(8,128)(2,1)S(1)} %get-tuple-element.184), channel_id=1, source_target_pairs={{0,24},{4,28},{8,0},{12,4},{16,8},{20,12},{24,16},{28,20},{1,25},{... | collective-permute-start | bytes 589832 | tf_op jit(solution)/shard_map/ppermute | solution.py:486
  395.3 26.6 %collective-permute-start.29 = (bf16[128,768]{1,0:T(8,128)(2,1)S(1)}, bf16[128,768]{1,0:T(8,128)(2,1)S(1)}, u32[]{:S(2)}, u32[]{:S(2)}) collective-permute-start(bf16[128,768]{1,0:T(8,128)(2,1)S(1)} %get-tuple-element.183), channel_id=1, source_target_pairs={{0,16},{4,20},{8,24},{12,28},{16,0},{20,4},{24,8},{28,12},{1,17},{... | collective-permute-start | bytes 589832 | tf_op jit(solution)/shard_map/ppermute | solution.py:486
  397.2 24.8 %collective-permute-start.30 = (bf16[128,768]{1,0:T(8,128)(2,1)S(1)}, bf16[128,768]{1,0:T(8,128)(2,1)S(1)}, u32[]{:S(2)}, u32[]{:S(2)}) collective-permute-start(bf16[128,768]{1,0:T(8,128)(2,1)S(1)} %get-tuple-element.182), channel_id=1, source_target_pairs={{0,8},{4,12},{8,16},{12,20},{16,24},{20,28},{24,0},{28,4},{1,9},{5... | collective-permute-start | bytes 589832 | tf_op jit(solution)/shard_map/ppermute | solution.py:486
  400.5 28.8 %collective-permute-start.59 = (bf16[96,1536]{1,0:T(8,128)(2,1)S(1)}, bf16[96,1536]{1,0:T(8,128)(2,1)S(1)}, u32[]{:S(2)}, u32[]{:S(2)}) collective-permute-start(bf16[96,1536]{1,0:T(8,128)(2,1)S(1)} %get-tuple-element.164), channel_id=1, source_target_pairs={{0,8},{4,12},{8,16},{12,20},{16,24},{20,28},{24,0},{28,4},{1,9},{5... | collective-permute-start | bytes 884744 | tf_op jit(solution)/shard_map/ppermute | solution.py:486
  401.6 27.8 %collective-permute-start.51 = (bf16[96,1536]{1,0:T(8,128)(2,1)S(1)}, bf16[96,1536]{1,0:T(8,128)(2,1)S(1)}, u32[]{:S(2)}, u32[]{:S(2)}) collective-permute-start(bf16[96,1536]{1,0:T(8,128)(2,1)S(1)} %get-tuple-element.162), channel_id=1, source_target_pairs={{0,8},{4,12},{8,16},{12,20},{16,24},{20,28},{24,0},{28,4},{1,9},{5... | collective-permute-start | bytes 884744 | tf_op jit(solution)/shard_map/ppermute | solution.py:486
  421.9 12.3 %collective-permute-start.67 = (bf16[192,768]{1,0:T(8,128)(2,1)S(1)}, bf16[192,768]{1,0:T(8,128)(2,1)S(1)}, u32[]{:S(2)}, u32[]{:S(2)}) collective-permute-start(bf16[192,768]{1,0:T(8,128)(2,1)S(1)} %get-tuple-element.158), channel_id=1, source_target_pairs={{0,8},{4,12},{8,16},{12,20},{16,24},{20,28},{24,0},{28,4},{1,9},{5... | collective-permute-start | bytes 884744 | tf_op jit(solution)/shard_map/ppermute | solution.py:486
  427.6 38.9 %collective-permute-start.32 = (bf16[1,4,4,48,384]{4,3,2,1,0:T(8,128)(2,1)S(1)}, bf16[1,4,4,48,384]{4,3,2,1,0:T(8,128)(2,1)S(1)}, u32[]{:S(2)}, u32[]{:S(2)}) collective-permute-start(bf16[1,4,4,48,384]{4,3,2,1,0:T(8,128)(2,1)S(1)} %constant_dynamic-slice_fusion), channel_id=1, source_target_pairs={{0,2},{1,3},{2,0},{3,1},{4,6},{5,7},{6,4},{7,5},{8,10},{9,11},{10,... | collective-permute-start | bytes 1769480 | tf_op jit(solution)/shard_map/ppermute | solution.py:497
  429.2 41.4 %collective-permute-start.76 = (bf16[2,192,768]{2,1,0:T(8,128)(2,1)S(1)}, bf16[2,192,768]{2,1,0:T(8,128)(2,1)S(1)}, u32[]{:S(2)}, u32[]{:S(2)}) collective-permute-start(bf16[2,192,768]{2,1,0:T(8,128)(2,1)S(1)} %bitcast_dynamic-update-slice_fusion.12), channel_id=1, source_target_pairs={{0,8},{4,12},{8,16},{12,20},{16,24},{20,28},{24,0},{28,4},{1,9},{5... | collective-permute-start | bytes 1769480 | tf_op jit(solution)/shard_map/ppermute | solution.py:486
  429.3 24.3 %collective-permute-start.60 = (bf16[96,1536]{1,0:T(8,128)(2,1)S(1)}, bf16[96,1536]{1,0:T(8,128)(2,1)S(1)}, u32[]{:S(2)}, u32[]{:S(2)}) collective-permute-start(bf16[96,1536]{1,0:T(8,128)(2,1)S(1)} %collective-permute-done.59), channel_id=1, source_target_pairs={{0,8},{4,12},{8,16},{12,20},{16,24},{20,28},{24,0},{28,4},{1,9},{5... | collective-permute-start | bytes 884744 | tf_op jit(solution)/shard_map/ppermute | solution.py:486
  429.4 30.5 %collective-permute-start.52 = (bf16[96,1536]{1,0:T(8,128)(2,1)S(1)}, bf16[96,1536]{1,0:T(8,128)(2,1)S(1)}, u32[]{:S(2)}, u32[]{:S(2)}) collective-permute-start(bf16[96,1536]{1,0:T(8,128)(2,1)S(1)} %collective-permute-done.51), channel_id=1, source_target_pairs={{0,8},{4,12},{8,16},{12,20},{16,24},{20,28},{24,0},{28,4},{1,9},{5... | collective-permute-start | bytes 884744 | tf_op jit(solution)/shard_map/ppermute | solution.py:486
  434.3 32.1 %collective-permute-start.68 = (bf16[192,768]{1,0:T(8,128)(2,1)S(1)}, bf16[192,768]{1,0:T(8,128)(2,1)S(1)}, u32[]{:S(2)}, u32[]{:S(2)}) collective-permute-start(bf16[192,768]{1,0:T(8,128)(2,1)S(1)} %collective-permute-done.67), channel_id=1, source_target_pairs={{0,8},{4,12},{8,16},{12,20},{16,24},{20,28},{24,0},{28,4},{1,9},{5... | collective-permute-start | bytes 884744 | tf_op jit(solution)/shard_map/ppermute | solution.py:486
  453.6 19.1 %collective-permute-start.61 = (bf16[96,1536]{1,0:T(8,128)(2,1)S(1)}, bf16[96,1536]{1,0:T(8,128)(2,1)S(1)}, u32[]{:S(2)}, u32[]{:S(2)}) collective-permute-start(bf16[96,1536]{1,0:T(8,128)(2,1)S(1)} %collective-permute-done.60), channel_id=1, source_target_pairs={{0,8},{4,12},{8,16},{12,20},{16,24},{20,28},{24,0},{28,4},{1,9},{5... | collective-permute-start | bytes 884744 | tf_op jit(solution)/shard_map/ppermute | solution.py:486
  459.9 19.0 %collective-permute-start.53 = (bf16[96,1536]{1,0:T(8,128)(2,1)S(1)}, bf16[96,1536]{1,0:T(8,128)(2,1)S(1)}, u32[]{:S(2)}, u32[]{:S(2)}) collective-permute-start(bf16[96,1536]{1,0:T(8,128)(2,1)S(1)} %collective-permute-done.52), channel_id=1, source_target_pairs={{0,8},{4,12},{8,16},{12,20},{16,24},{20,28},{24,0},{28,4},{1,9},{5... | collective-permute-start | bytes 884744 | tf_op jit(solution)/shard_map/ppermute | solution.py:486
  466.4 41.7 %collective-permute-start.69 = (bf16[192,768]{1,0:T(8,128)(2,1)S(1)}, bf16[192,768]{1,0:T(8,128)(2,1)S(1)}, u32[]{:S(2)}, u32[]{:S(2)}) collective-permute-start(bf16[192,768]{1,0:T(8,128)(2,1)S(1)} %collective-permute-done.68), channel_id=1, source_target_pairs={{0,8},{4,12},{8,16},{12,20},{16,24},{20,28},{24,0},{28,4},{1,9},{5... | collective-permute-start | bytes 884744 | tf_op jit(solution)/shard_map/ppermute | solution.py:486
  466.7 19.2 %collective-permute-start.35 = (bf16[4,48,384]{2,1,0:T(8,128)(2,1)S(1)}, bf16[4,48,384]{2,1,0:T(8,128)(2,1)S(1)}, u32[]{:S(2)}, u32[]{:S(2)}) collective-permute-start(bf16[4,48,384]{2,1,0:T(8,128)(2,1)S(1)} %get-tuple-element.194), channel_id=1, source_target_pairs={{0,24},{4,28},{8,0},{12,4},{16,8},{20,12},{24,16},{28,20},{1,25},{... | collective-permute-start | bytes 442376 | tf_op jit(solution)/shard_map/ppermute | solution.py:486
  470.6 35.9 %collective-permute-start.34 = (bf16[4,48,384]{2,1,0:T(8,128)(2,1)S(1)}, bf16[4,48,384]{2,1,0:T(8,128)(2,1)S(1)}, u32[]{:S(2)}, u32[]{:S(2)}) collective-permute-start(bf16[4,48,384]{2,1,0:T(8,128)(2,1)S(1)} %get-tuple-element.195), channel_id=1, source_target_pairs={{0,16},{4,20},{8,24},{12,28},{16,0},{20,4},{24,8},{28,12},{1,17},{... | collective-permute-start | bytes 442376 | tf_op jit(solution)/shard_map/ppermute | solution.py:486
  472.7 35.1 %collective-permute-start.33 = (bf16[4,48,384]{2,1,0:T(8,128)(2,1)S(1)}, bf16[4,48,384]{2,1,0:T(8,128)(2,1)S(1)}, u32[]{:S(2)}, u32[]{:S(2)}) collective-permute-start(bf16[4,48,384]{2,1,0:T(8,128)(2,1)S(1)} %get-tuple-element.193), channel_id=1, source_target_pairs={{0,8},{4,12},{8,16},{12,20},{16,24},{20,28},{24,0},{28,4},{1,9},{5... | collective-permute-start | bytes 442376 | tf_op jit(solution)/shard_map/ppermute | solution.py:486
  478.9 50.1 %collective-permute-start.77 = (bf16[2,192,768]{2,1,0:T(8,128)(2,1)S(1)}, bf16[2,192,768]{2,1,0:T(8,128)(2,1)S(1)}, u32[]{:S(2)}, u32[]{:S(2)}) collective-permute-start(bf16[2,192,768]{2,1,0:T(8,128)(2,1)S(1)} %collective-permute-done.76), channel_id=1, source_target_pairs={{0,8},{4,12},{8,16},{12,20},{16,24},{20,28},{24,0},{28,4},{1,9},{5... | collective-permute-start | bytes 1769480 | tf_op jit(solution)/shard_map/ppermute | solution.py:486
  485.9 115.2 %collective-permute-start.62 = (bf16[4,96,1536]{2,1,0:T(8,128)(2,1)S(1)}, bf16[4,96,1536]{2,1,0:T(8,128)(2,1)S(1)}, u32[]{:S(2)}, u32[]{:S(2)}) collective-permute-start(bf16[4,96,1536]{2,1,0:T(8,128)(2,1)S(1)} %bitcast_dynamic-update-slice_fusion.18), channel_id=1, source_target_pairs={{0,4},{4,0},{8,12},{12,8},{16,20},{20,16},{24,28},{28,24},{1,5},{5... | collective-permute-start | bytes 3538952 | tf_op jit(solution)/shard_map/ppermute | solution.py:492
  506.5 94.7 %collective-permute-start.54 = (bf16[4,96,1536]{2,1,0:T(8,128)(2,1)S(1)}, bf16[4,96,1536]{2,1,0:T(8,128)(2,1)S(1)}, u32[]{:S(2)}, u32[]{:S(2)}) collective-permute-start(bf16[4,96,1536]{2,1,0:T(8,128)(2,1)S(1)} %bitcast_dynamic-update-slice_fusion.22), channel_id=1, source_target_pairs={{0,4},{4,0},{8,12},{12,8},{16,20},{20,16},{24,28},{28,24},{1,5},{5... | collective-permute-start | bytes 3538952 | tf_op jit(solution)/shard_map/ppermute | solution.py:492
  508.1 68.7 %collective-permute-start.70 = (bf16[4,192,768]{2,1,0:T(8,128)(2,1)S(1)}, bf16[4,192,768]{2,1,0:T(8,128)(2,1)S(1)}, u32[]{:S(2)}, u32[]{:S(2)}) collective-permute-start(bf16[4,192,768]{2,1,0:T(8,128)(2,1)S(1)} %bitcast_dynamic-update-slice_fusion.14), channel_id=1, source_target_pairs={{0,4},{4,0},{8,12},{12,8},{16,20},{20,16},{24,28},{28,24},{1,5},{5... | collective-permute-start | bytes 3538952 | tf_op jit(solution)/shard_map/ppermute | solution.py:492
  527.7 46.8 %collective-permute-start.39 = (bf16[4,4,48,384]{3,2,1,0:T(8,128)(2,1)S(1)}, bf16[4,4,48,384]{3,2,1,0:T(8,128)(2,1)S(1)}, u32[]{:S(2)}, u32[]{:S(2)}) collective-permute-start(bf16[4,4,48,384]{3,2,1,0:T(8,128)(2,1)S(1)} %bitcast_dynamic-update-slice_fusion.38), channel_id=1, source_target_pairs={{0,4},{4,0},{8,12},{12,8},{16,20},{20,16},{24,28},{28,24},{1,5},{5... | collective-permute-start | bytes 1769480 | tf_op jit(solution)/shard_map/ppermute | solution.py:492
  529.1 47.7 %collective-permute-start.78 = (bf16[2,192,768]{2,1,0:T(8,128)(2,1)S(1)}, bf16[2,192,768]{2,1,0:T(8,128)(2,1)S(1)}, u32[]{:S(2)}, u32[]{:S(2)}) collective-permute-start(bf16[2,192,768]{2,1,0:T(8,128)(2,1)S(1)} %collective-permute-done.77), channel_id=1, source_target_pairs={{0,8},{4,12},{8,16},{12,20},{16,24},{20,28},{24,0},{28,4},{1,9},{5... | collective-permute-start | bytes 1769480 | tf_op jit(solution)/shard_map/ppermute | solution.py:486
  574.6 26.0 %collective-permute-start.40 = (bf16[1,2,4,4,48,384]{5,4,3,2,1,0:T(8,128)(2,1)S(1)}, bf16[1,2,4,4,48,384]{5,4,3,2,1,0:T(8,128)(2,1)S(1)}, u32[]{:S(2)}, u32[]{:S(2)}) collective-permute-start(bf16[1,2,4,4,48,384]{5,4,3,2,1,0:T(8,128)(2,1)S(1)} %bitcast.352), channel_id=1, source_target_pairs={{0,2},{1,3},{2,0},{3,1},{4,6},{5,7},{6,4},{7,5},{8,10},{9,11},{10,... | collective-permute-start | bytes 3538952 | tf_op jit(solution)/shard_map/ppermute | solution.py:497
  601.0 10.3 %collective-permute-start.41 = (bf16[2,2,4,4,48,384]{5,4,3,2,1,0:T(8,128)(2,1)S(1)}, bf16[2,2,4,4,48,384]{5,4,3,2,1,0:T(8,128)(2,1)S(1)}, u32[]{:S(2)}, u32[]{:S(2)}) collective-permute-start(bf16[2,2,4,4,48,384]{5,4,3,2,1,0:T(8,128)(2,1)S(1)} %maximum_select_fusion.2), channel_id=1, source_target_pairs={{0,1},{1,0},{2,3},{3,2},{4,5},{5,4},{6,7},{7,6},{8,9},{9,8},{10,11... | collective-permute-start | bytes 7077896 | tf_op jit(solution)/shard_map/ppermute | solution.py:497
  (72 other events, 668.5 us)

commit v3 on v2

--- a/solution.py
+++ b/solution.py
@@ -148,12 +148,12 @@
             o_refs[j][k] = o_ref[place_of(own_ref, j, k, team, rows, local), :]
 
 
-def attend_back_kernel(team, rows, local, block, unroll, own_ref, *refs):
+def attend_back_kernel(team, rows, local, block, unroll, experts, own_ref, *refs):
     pieces, refs = refs[:team], refs[team:]
     x_ref, wq_ref, wk_ref, wv_ref, wo_ref, low_ref = refs[:6]
-    q_ref, k_ref, v_ref, ot_ref, log_ref, gw_ref = refs[6:12]
-    gx_refs = refs[12 : 12 + team]
-    b_ref, g_ref, kt_ref, delta_ref, dqt_ref, d_ref, sum_ref = refs[12 + team :]
+    q_ref, k_ref, v_ref, ot_ref, log_ref = refs[6:11]
+    gx_refs, refs = refs[11 : 11 + team], refs[11 + team :]
+    gw_ref, b_ref, g_ref, kt_ref, delta_ref, dqt_ref, d_ref, sum_ref = refs
     length, width = x_ref.shape
     count = length // block
     scale = HEAD**-0.5
@@ -227,10 +227,14 @@
 
     each(count, unroll, spread)
 
-    grads = dot(x_ref[...], d_ref[...], TN)
-    for which in range(3):
-        gw_ref[which] = grads[:, which * PAIR : (which + 1) * PAIR].astype(LOW)
-    gw_ref[3] = dot(ot_ref[...].astype(LOW), b_ref[...]).T.astype(LOW)
+    grads = dot(x_ref[...], d_ref[...], TN).astype(LOW)
+    out_grads = dot(ot_ref[...].astype(LOW), b_ref[...]).T.astype(LOW)
+    cut = width // experts
+    for e in range(experts):
+        span = slice(e * cut, (e + 1) * cut)
+        for which in range(3):
+            gw_ref[e, which] = grads[span, which * PAIR : (which + 1) * PAIR]
+        gw_ref[e, 3] = out_grads[span]
 
     @pl.when(pair == pl.num_programs(0) - 1)
     def _():
@@ -288,7 +292,9 @@
     )(own, *pieces, gain[None], bias[None], weights, weights, weights, low)
 
 
-def attend_back(own, pieces, x, weights, out_weights, low, q, k, v, ot, logs_in, team, rows, pairs):
+def attend_back(
+    own, pieces, x, weights, out_weights, low, q, k, v, ot, logs_in, team, rows, pairs, experts
+):
     length, width = x.shape
     local = length // (team * rows)
     share = pairs * PAIR
@@ -298,7 +304,7 @@
     shape = jax.ShapeDtypeStruct
     out = pl.BlockSpec((rows, local, width), lambda p, own: (0, 0, 0))
     results = pl.pallas_call(
-        functools.partial(attend_back_kernel, team, rows, local, block, unroll),
+        functools.partial(attend_back_kernel, team, rows, local, block, unroll, experts),
         grid_spec=pltpu.PrefetchScalarGridSpec(
             num_scalar_prefetch=1,
             grid=(pairs,),
@@ -306,7 +312,8 @@
             + [fixed(length, width), weight(0), weight(1), weight(2)]
             + [pl.BlockSpec((PAIR, width), lambda p, own: (own[1] * pairs + p, 0))]
             + [fixed(1, length), columns(), columns(), columns(), across, logs],
-            out_specs=[pl.BlockSpec((4, width, PAIR), lambda p, own: (0, 0, p))] + [out] * team,
+            out_specs=[out] * team
+            + [pl.BlockSpec((experts, 4, width // experts, PAIR), lambda p, own: (0, 0, 0, p))],
             scratch_shapes=[
                 pltpu.VMEM((length, width), LOW),
                 pltpu.VMEM((length, PAIR), LOW),
@@ -317,7 +324,8 @@
                 pltpu.VMEM((length, width), FULL),
             ],
         ),
-        out_shape=[shape((4, width, share), LOW)] + [shape((rows, local, width), LOW)] * team,
+        out_shape=[shape((rows, local, width), LOW)] * team
+        + [shape((experts, 4, width // experts, share), LOW)],
         compiler_params=pltpu.CompilerParams(vmem_limit_bytes=VMEM_LIMIT),
         cost_estimate=pl.CostEstimate(
             flops=4 * length * width * 4 * share + 20 * length * length * share,
@@ -326,14 +334,14 @@
         ),
         name="attend_back",
     )(own, *pieces, x, weights, weights, weights, out_weights, low, q, k, v, ot, logs_in)
-    return results[0], results[1:]
+    return results[team], results[:team]
 
 
 GELU_SCALE = math.sqrt(2.0 / math.pi)
 GELU_CUBE = 0.044715
 
 
-def expert_kernel(count, first, last, *refs):
+def expert_kernel(count, first, last, own_ref, *refs):
     x_refs, refs = refs[:count], refs[count:]
     g_refs, refs = refs[:count], refs[count:]
     up_ref, down_ref, refs = refs[0], refs[1], refs[2:]
@@ -341,9 +349,7 @@
         y_in, gx_in, refs = refs[0], refs[1], refs[2:]
     gup_ref, gdown_ref, refs = refs[0], refs[1], refs[2:]
     if last:
-        y_outs, refs = refs[:count], refs[count:]
-        gx_outs, refs = refs[:count], refs[count:]
-        y_sum, gx_sum, refs = refs[0], refs[1], refs[2:]
+        y_out, gx_out, y_sum, gx_sum, refs = refs[0], refs[1], refs[2], refs[3], refs[4:]
     else:
         y_sum, gx_sum, refs = refs[0], refs[1], refs[2:]
     x_ref, g_ref = refs
@@ -385,47 +391,51 @@
         def _():
             for index in range(count):
                 span = pl.ds(index * size, size)
-                y_outs[index][...] = y_sum[span, :].astype(LOW)
-                gx_outs[index][...] = gx_sum[span, :].astype(LOW)
-
-
-def expert(xs, gs, up, down, part, parts, sums):
+                y_out[own_ref[2] ^ index] = y_sum[span, :].astype(LOW)
+                gx_out[own_ref[2] ^ index] = gx_sum[span, :].astype(LOW)
+
+
+def expert(own, xs, gs, up, down, part, parts, sums):
     count = len(xs)
     size, width = xs[0].shape
     hidden = up.shape[1] // parts
     block = math.gcd(hidden, 512)
     steps = hidden // block
     first, last = part == 0, part == parts - 1
-    rows = pl.BlockSpec((size, width), lambda f: (0, 0))
-    whole = pl.BlockSpec((count * size, width), lambda f: (0, 0))
+    rows = pl.BlockSpec((size, width), lambda f, own: (0, 0))
+    whole = pl.BlockSpec((count * size, width), lambda f, own: (0, 0))
+    every = pl.BlockSpec((count, size, width), lambda f, own: (0, 0, 0))
     shape = jax.ShapeDtypeStruct
     sum_shape = shape((count * size, width), FULL)
     in_specs = [rows] * (2 * count) + [
-        pl.BlockSpec((width, block), lambda f: (0, f + part * steps)),
-        pl.BlockSpec((block, width), lambda f: (f + part * steps, 0)),
+        pl.BlockSpec((width, block), lambda f, own: (0, f + part * steps)),
+        pl.BlockSpec((block, width), lambda f, own: (f + part * steps, 0)),
     ]
     out_specs = [
-        pl.BlockSpec((width, block), lambda f: (0, f)),
-        pl.BlockSpec((block, width), lambda f: (f, 0)),
+        pl.BlockSpec((width, block), lambda f, own: (0, f)),
+        pl.BlockSpec((block, width), lambda f, own: (f, 0)),
     ]
     out_shape = [shape((width, hidden), LOW), shape((hidden, width), LOW)]
     scratch = []
     if not first:
         in_specs += [whole] * 2
     if last:
-        out_specs += [rows] * (2 * count)
-        out_shape += [shape((size, width), LOW)] * (2 * count)
+        out_specs += [every] * 2
+        out_shape += [shape((count, size, width), LOW)] * 2
         scratch += [pltpu.VMEM(sum_shape.shape, FULL)] * 2
     else:
         out_specs += [whole] * 2
         out_shape += [sum_shape] * 2
     results = pl.pallas_call(
         functools.partial(expert_kernel, count, first, last),
-        grid=(steps,),
-        in_specs=in_specs,
-        out_specs=out_specs,
+        grid_spec=pltpu.PrefetchScalarGridSpec(
+            num_scalar_prefetch=1,
+            grid=(steps,),
+            in_specs=in_specs,
+            out_specs=out_specs,
+            scratch_shapes=scratch + [pltpu.VMEM((count * size, width), LOW)] * 2,
+        ),
         out_shape=out_shape,
-        scratch_shapes=scratch + [pltpu.VMEM((count * size, width), LOW)] * 2,
         compiler_params=pltpu.CompilerParams(vmem_limit_bytes=VMEM_LIMIT),
         cost_estimate=pl.CostEstimate(
             flops=12 * count * size * width * hidden,
@@ -433,8 +443,151 @@
             transcendentals=count * size * hidden,
         ),
         name="expert",
-    )(*xs, *gs, up, down, *sums)
+    )(own, *xs, *gs, up, down, *sums)
     return results[0], results[1], results[2:]
+
+
+def tie(values, others):
+    count, total = len(values), len(values) + len(others)
+    return pl.pallas_call(
+        lambda *refs: None,
+        in_specs=[pl.BlockSpec(memory_space=pl.ANY)] * total,
+        out_specs=[pl.BlockSpec(memory_space=pl.ANY)] * count,
+        out_shape=[jax.ShapeDtypeStruct(value.shape, value.dtype) for value in values],
+        input_output_aliases={index: index for index in range(count)},
+        name="tie",
+    )(*values, *others)
+
+
+def put_kernel(count, joined, place, own_ref, *refs):
+    out_ref = refs[count + joined]
+    size, cut, _ = refs[0].shape
+    for i in range(count):
+        for n in range(size):
+            first = pl.multiple_of(place(own_ref, i, n) * cut, cut)
+            out_ref[pl.ds(first, cut), :] = refs[i][n].astype(FULL)
+
+
+def put_chunk(own, parts, into, shape, block, place):
+    count, (size, cut, width) = len(parts), parts[0].shape
+    joined = [] if into is None else [into]
+    return pl.pallas_call(
+        functools.partial(put_kernel, count, len(joined), place),
+        grid_spec=pltpu.PrefetchScalarGridSpec(
+            num_scalar_prefetch=1,
+            grid=(1,),
+            in_specs=[pl.BlockSpec((size, cut, width), lambda s, own: (0, 0, 0))] * count
+            + [pl.BlockSpec(memory_space=pl.ANY)] * len(joined),
+            out_specs=pl.BlockSpec((count * size * cut, width), lambda s, own: block),
+        ),
+        out_shape=jax.ShapeDtypeStruct(shape, FULL),
+        input_output_aliases={1 + count: 0} if joined else {},
+        compiler_params=pltpu.CompilerParams(vmem_limit_bytes=VMEM_LIMIT),
+        cost_estimate=pl.CostEstimate(
+            flops=0, bytes_accessed=8 * count * size * cut * width, transcendentals=0
+        ),
+        name="put_chunk",
+    )(own, *parts, *joined)
+
+
+def place_kernel(team, rows, experts, own_ref, *refs):
+    parts, (qkv_ref, out_ref, hold_ref) = refs[: team * experts], refs[team * experts :]
+    cut, share = parts[0].shape[2:]
+    which = pl.program_id(0)
+
+    def rows_of(m, k):
+        index = (own_ref[2] ^ m) * rows + k
+        return pl.ds(pl.multiple_of(index * cut, cut), cut)
+
+    for j in range(team):
+        member = lax.rem(own_ref[1] + (team - j), team)
+        span = pl.ds(pl.multiple_of(member * share, share), share)
+
+        @pl.when(which < 3)
+        def _():
+            for m in range(experts):
+                for k in range(rows):
+                    part = parts[m * team + j][k, 0]
+                    qkv_ref[rows_of(m, k), span] = part.astype(FULL)
+
+        @pl.when(which == 3)
+        def _():
+            for m in range(experts):
+                for k in range(rows):
+                    part = parts[m * team + j][k, 0]
+                    hold_ref[rows_of(m, k), :] = part.astype(FULL)
+            out_ref[span, :] = hold_ref[...].T
+
+
+def place_weights(own, parts, team, rows, experts):
+    _, _, cut, share = parts[0].shape
+    width, padded = experts * rows * cut, team * share
+    return pl.pallas_call(
+        functools.partial(place_kernel, team, rows, experts),
+        grid_spec=pltpu.PrefetchScalarGridSpec(
+            num_scalar_prefetch=1,
+            grid=(4,),
+            in_specs=[pl.BlockSpec((rows, 1, cut, share), lambda w, own: (0, w, 0, 0))]
+            * (team * experts),
+            out_specs=[
+                pl.BlockSpec((width, padded), lambda w, own: (0, jnp.minimum(w, 2))),
+                pl.BlockSpec((padded, width), lambda w, own: (0, 0)),
+            ],
+            scratch_shapes=[pltpu.VMEM((width, share), FULL)],
+        ),
+        out_shape=[
+            jax.ShapeDtypeStruct((width, 3 * padded), FULL),
+            jax.ShapeDtypeStruct((padded, width), FULL),
+        ],
+        compiler_params=pltpu.CompilerParams(vmem_limit_bytes=VMEM_LIMIT),
+        cost_estimate=pl.CostEstimate(
+            flops=0, bytes_accessed=24 * width * padded, transcendentals=0
+        ),
+        name="place_weights",
+    )(own, *parts)
+
+
+def norm_back_kernel(team, own_ref, *refs):
+    parts, refs = refs[:team], refs[team:]
+    x_ref, more_ref, gain_ref, out_ref, sum_ref = refs
+    unit, inverse = standard(x_ref[0].astype(FULL))
+    grad = parts[0][0].astype(FULL)
+    for part in parts[1:]:
+        grad = grad + part[0].astype(FULL)
+    back, gain, bias = standard_back(grad, gain_ref[...], unit, inverse)
+    out_ref[0] = (back + more_ref[0].astype(FULL)).astype(LOW)
+
+    @pl.when(pl.program_id(0) == 0)
+    def _():
+        sum_ref[...] = jnp.zeros_like(sum_ref)
+
+    sum_ref[0:1, :] += gain[None]
+    sum_ref[1:2, :] += bias[None]
+
+
+def norm_back(own, parts, x, more, gain):
+    rows, local, width = x.shape
+    block = pl.BlockSpec((1, local, width), lambda k, own: (k, 0, 0))
+    home = lambda k, own: (lax.rem(own[0] + (rows - k), rows), 0, 0)
+    return pl.pallas_call(
+        functools.partial(norm_back_kernel, len(parts)),
+        grid_spec=pltpu.PrefetchScalarGridSpec(
+            num_scalar_prefetch=1,
+            grid=(rows,),
+            in_specs=[block] * (len(parts) + 2)
+            + [pl.BlockSpec((1, width), lambda k, own: (0, 0))],
+            out_specs=[
+                pl.BlockSpec((1, local, width), home),
+                pl.BlockSpec((8, width), lambda k, own: (0, 0)),
+            ],
+        ),
+        out_shape=[
+            jax.ShapeDtypeStruct(x.shape, LOW),
+            jax.ShapeDtypeStruct((8, width), FULL),
+        ],
+        cost_estimate=pl.CostEstimate(flops=0, bytes_accessed=40 * x.size, transcendentals=0),
+        name="norm_back",
+    )(own, *parts, x, more, gain[None])
 
 
 def add_low(a, b):
@@ -492,14 +645,17 @@
         return lax.ppermute(value, "seq", pattern)
 
     def swap(value, axis, m):
-        if m == 0:
+        if m == 0 or m >= lax.axis_size(axis):
             return value
         return lax.ppermute(value, axis, [(a, a ^ m) for a in range(lax.axis_size(axis))])
 
-    def home(pieces):
-        stacked = jnp.stack([row_send(piece, rows - k) for k, piece in enumerate(pieces)])
-        twice = jnp.concatenate([stacked, stacked], 0)
-        return lax.dynamic_slice_in_dim(twice, (rows - row) % rows, rows, 0)
+    across_rows = [[r * team + g for r in range(rows)] for g in range(team)]
+
+    def swap_rows(value):
+        return lax.all_to_all(value, "seq", 0, 0, tiled=True, axis_index_groups=across_rows)
+
+    def swap_experts(value):
+        return lax.all_to_all(value, "ex", 0, 0, tiled=True)
 
     center = (block_input - jnp.mean(block_input, -1, keepdims=True)).astype(LOW)
     owned_x = [row_send(pick(center, (row + k) % rows), k) for k in range(rows)]
@@ -507,7 +663,7 @@
 
     labels = jnp.pad(expert_ids.reshape(rows, 1, local), ((0, 0), (0, 15), (0, width - local)))
     carried = jnp.concatenate([grad_out.astype(LOW), labels.astype(LOW)], 1)
-    carried, pieces = lax.optimization_barrier((carried, pieces))
+    carried = tie([carried], [owned_x[1]])[0]
     owned_g = jnp.stack([row_send(pick(carried, (row + k) % rows), k) for k in range(rows)])
     grad_low = owned_g[:, :local]
     chosen = owned_g[:, local, :local].astype(jnp.int32)
@@ -522,11 +678,11 @@
         weights = weights.reshape(width, 3 * padded)
         out_weights = jnp.pad(w_attn_out, ((0, extra), (0, 0)))
 
-    own = jnp.stack([row, member]).astype(jnp.int32)
+    own = jnp.stack([row, member, mine]).astype(jnp.int32)
     results = attend(own, pieces, ln1_gain, ln1_bias, weights, lows, team, rows, pairs)
     full, q, k, v, ot, logs = results[:6]
     branch = 0.0
-    for j, part in enumerate(results[6:]):
+    for j, part in enumerate(tie(results[6:], [owned_g])):
         first = (member + team - j) % team * share
         weight = lax.dynamic_slice_in_dim(out_weights, first, share, 0)
         branch = branch + dot(team_send(part, j).reshape(owned, share), weight)
@@ -540,11 +696,14 @@
     onehot = (relative[..., None] == jnp.arange(experts, dtype=jnp.int32)).astype(jnp.int32)
     rank = jnp.cumsum(onehot, 1) - onehot
     target = relative * MOST + jnp.sum(rank * onehot, -1)
-    route = (
-        (target[:, None, :] == jnp.arange(experts * MOST, dtype=jnp.int32)[None, :, None])
-        .astype(LOW)
-        .reshape(rows, experts, MOST, local)
-    )
+    numbers = jnp.arange(experts * MOST, dtype=jnp.int32)[None, :, None]
+
+    def routes(target):
+        match = (target[:, None, :] == numbers).astype(LOW)
+        return match.reshape(rows, experts, MOST, local)
+
+    route = routes(target)
+    back_route = routes((target // MOST ^ mine) * MOST + target % MOST)
     named = (chosen[..., None] == jnp.arange(experts, dtype=jnp.int32)).astype(FULL)
     counts = jnp.sum(named, (0, 1))
 
@@ -555,11 +714,10 @@
         placed = placed.astype(LOW).reshape(experts, slots, width)
         return [swap(placed[m], "ex", m) for m in range(experts)]
 
-    def collect(parts):
-        returned = jnp.stack([swap(part, "ex", m) for m, part in enumerate(parts)])
+    def collect(returned):
         return jnp.einsum(
             "remt,ermd->rtd",
-            route,
+            back_route,
             returned.reshape(experts, rows, MOST, width),
             preferred_element_type=FULL,
         ).reshape(owned, width)
@@ -567,92 +725,204 @@
     grad_arrived = dispatch(grad_low)
     arrived = dispatch(normed_two)
 
-    def shared_sum(value, rows_first):
-        along_team = lambda v: team_send(v, 1)
-        along_rows = lambda v: row_send(v, 1)
-        cut = value.shape[0] // (team * rows)
-        if rows_first:
-            value = value.reshape((rows, team, cut) + value.shape[1:])
-            value = ring_scatter(value, rows, row, along_rows)
-            value = ring_scatter(value, team, member, along_team)
-            value = ring_gather(value, team, member, along_team)
-            value = ring_gather(value, rows, row, along_rows)
-        else:
-            value = value.reshape((team, rows, cut) + value.shape[1:])
-            value = ring_scatter(value, team, member, along_team)
-            value = ring_scatter(value, rows, row, along_rows)
-            value = ring_gather(value, rows, row, along_rows)
-            value = ring_gather(value, team, member, along_team)
-        return value.reshape((-1,) + value.shape[3:]).astype(FULL)
-
-    up_low, down_low, sums = expert(arrived, grad_arrived, w_in[0], w_down[0], 0, 2, ())
-    up_high, down_high, sums = expert(arrived, grad_arrived, w_in[0], w_down[0], 1, 2, sums)
-    produced, grad_rows = sums[:experts], sums[experts:]
-    grad_up = jnp.concatenate([shared_sum(up_low, False), shared_sum(up_high, False)], 1)
-    grad_down = jnp.concatenate([shared_sum(down_low, False), shared_sum(down_high, True)], 0)
-
+    hops = rows - 1
+
+    def along_team(value):
+        return team_send(value, 1)
+
+    def team_scatter(value):
+        return ring_scatter(value, team, member, along_team)
+
+    def team_gather(value):
+        return [team_send(value, j) for j in range(team)]
+
+    def cut_up(value, sizes):
+        return value.reshape(sizes + (value.shape[0] // seq,) + value.shape[1:])
+
+    def first_hop(value):
+        return row_send(pick(value, (row + rows - 1) % rows), 1)
+
+    def joined(came, value, step):
+        return add_low(came, pick(value, (row + 2 * rows - 2 - step) % rows))
+
+    def next_hop(came, value, step):
+        return row_send(joined(came, value, step), 1)
+
+    def sync(*values):
+        leaves, tree = jax.tree.flatten(values)
+        return jax.tree.unflatten(tree, tie(leaves, []))
+
+    def team_first(own_ref, i, n):
+        device = lax.rem(own_ref[1] + (team - i), team)
+        return device * rows + lax.rem(own_ref[0] + (rows - n), rows)
+
+    def rows_first(own_ref, i, n):
+        device = lax.rem(own_ref[1] + (team - n), team)
+        return lax.rem(own_ref[0] + (rows - i), rows) * team + device
+
+    up_shape, down_shape = w_in.shape[1:], w_down.shape[1:]
+
+    up_one, down_one, sums = expert(own, arrived, grad_arrived, w_in[0], w_down[0], 0, 2, ())
+    cut_a = cut_up(up_one, (team, rows))
+    middle_row = cut_a.shape[2] // 2
+    cut_z = cut_up(down_one, (rows, team))
+    first_a = team_scatter(cut_a[:, :, :middle_row])
+    z = first_hop(cut_z)
+    up_two, down_two, sums = expert(own, arrived, grad_arrived, w_in[0], w_down[0], 1, 2, sums)
+    produced, grad_rows = sums
+    rest_a = cut_a[:, :, middle_row:]
+    z, produced, grad_rows, rest_a = sync(z, produced, grad_rows, rest_a)
+
+    grad_rows = swap_experts(grad_rows)
+    z = next_hop(z, cut_z, 0)
+    rest_a = team_scatter(rest_a)
+    grad_rows, produced, first_a = sync(grad_rows, produced, first_a)
+
+    produced = swap_experts(produced)
     back_two, grad_gain_two, grad_bias_two = standard_back(
         collect(grad_rows), ln2_gain, unit_two, inverse_two
     )
     grad_branch = (back_two + grad_low.reshape(owned, width).astype(FULL)).astype(LOW)
     grad_branch = grad_branch.reshape(rows, local, width)
-    grad_weights, grad_full = attend_back(
-        own, [team_send(grad_branch, j) for j in range(team)], full, weights, out_weights, lows,
-        q, k, v, ot, logs, team, rows, pairs,
+    grad_branch, z = sync(grad_branch, z)
+
+    branches = [team_send(grad_branch, j) for j in range(team)]
+    z = next_hop(z, cut_z, 1)
+    half_a = jnp.concatenate([first_a, rest_a], 1)
+    half_a, up_two, down_two = sync(half_a, up_two, down_two)
+
+    a = first_hop(half_a)
+    half_b = team_scatter(cut_up(up_two, (team, rows)))
+    z, produced = sync(z, produced)
+
+    z = joined(z, cut_z, 2)
+    change = (branch + collect(produced)).astype(LOW).reshape(rows, local, width)
+    change = jnp.stack([change[(rows - n) % rows] for n in range(rows)] * 2)
+    change = lax.dynamic_slice_in_dim(change, (rows - row) % rows, rows, 0)
+    a, change = sync(a, change)
+
+    a = next_hop(a, half_a, 0)
+    a, branches, down_two, change = sync(a, branches, down_two, change)
+
+    a = next_hop(a, half_a, 1)
+    change = swap_rows(change)
+    half_c = team_scatter(cut_up(down_two, (team, rows)))
+    grads, grad_full = attend_back(
+        own, branches, full, weights, out_weights, lows, q, k, v, ot, logs,
+        team, rows, pairs, experts,
     )
-
-    change = (branch + collect(produced)).astype(LOW).reshape(rows, local, width)
-    block_output = block_input + home(list(change)).astype(FULL)
-
-    unit_one, inverse_one = standard(residual)
-    grad_normed_one = sum(
-        team_send(part, j).astype(FULL) for j, part in enumerate(grad_full)
-    ).reshape(owned, width)
-    back_one, grad_gain_one, grad_bias_one = standard_back(
-        grad_normed_one, ln1_gain, unit_one, inverse_one
+    half_b, a, z, grads, grad_full = sync(half_b, a, z, grads, grad_full)
+
+    grads = swap_experts(grads)
+    grad_full = [team_send(part, j) for j, part in enumerate(grad_full)]
+    b = first_hop(half_b)
+    a = joined(a, half_a, 2)
+    change, half_c, a, z = sync(change, half_c, a, z)
+
+    pieces_a = [a, row_send(a, 1)]
+    z = team_scatter(z)
+    block_output = block_input + change.astype(FULL)
+    b, block_output = sync(b, block_output)
+
+    b = next_hop(b, half_b, 0)
+    pieces_a = sync(pieces_a)[0]
+
+    pieces_a = pieces_a + [row_send(pieces_a[-1], 1)]
+    b, grads = sync(b, grads)
+
+    b = next_hop(b, half_b, 1)
+    cut = width // (experts * rows)
+    grads = jnp.sum(grads.astype(FULL), 0).astype(LOW).reshape(4, rows, cut, share)
+    grads = swap_rows(grads.swapaxes(0, 1))
+    pieces_a, grad_full = sync(pieces_a, grad_full)
+
+    pieces_a = pieces_a + [row_send(pieces_a[-1], 1)]
+    grad_change, norm_sums = norm_back(
+        own, grad_full, jnp.stack(owned_x), back_two.reshape(rows, local, width), ln1_gain
     )
-    grad_change = (back_two + back_one).astype(LOW).reshape(rows, local, width)
-    grad_input = grad_out + home(list(grad_change)).astype(FULL)
-
-    cut = width // (experts * rows)
-    bits = [1 << b for b in range(experts.bit_length() - 1)]
-    value = grad_weights.reshape(4, experts, rows, cut, share).swapaxes(0, 1)
-    for bit in bits:
-        halves = value.reshape((value.shape[0] // 2, 2) + value.shape[1:])
-        on = (mine // bit) % 2
-        keep = lax.dynamic_index_in_dim(halves, on, 1, keepdims=False)
-        give = lax.dynamic_index_in_dim(halves, 1 - on, 1, keepdims=False)
-        value = add_low(keep, swap(give, "ex", bit))
-    value = value[0].swapaxes(0, 1)
-    value = sum(row_send(pick(value, (row + k) % rows), k).astype(FULL) for k in range(rows)).astype(LOW)
-    out = jnp.zeros((rows,) + value.shape, LOW)
-    for k in range(rows):
-        out = lax.dynamic_update_index_in_dim(out, row_send(value, k), (row + rows - k) % rows, 0)
-    value = ring_gather(out, team, member, lambda v: team_send(v, 1))[None]
-    for bit in reversed(bits):
-        on = (mine // bit) % 2
-        other = swap(value, "ex", bit)
-        pair = jnp.where(on == 0, jnp.stack([value, other], 1), jnp.stack([other, value], 1))
-        value = pair.reshape((-1,) + pair.shape[2:])
-    value = value.reshape(experts, team, rows, 4, cut, share)
-    grad_qkv = jnp.transpose(value[:, :, :, :3], (0, 2, 4, 3, 1, 5)).reshape(width, 3, padded)
-    grad_qkv = grad_qkv[..., :width].reshape(width, 3 * width).astype(FULL)
-    grad_attn_out = jnp.transpose(value[:, :, :, 3], (1, 4, 0, 2, 3)).reshape(padded, width)
-    grad_attn_out = grad_attn_out[:width].astype(FULL)
-
+    b, z, grad_change, norm_sums = sync(b, z, grad_change, norm_sums)
+
+    b = joined(b, half_b, 2)
+    pieces_b = [b, row_send(b, 1)]
+    z = jnp.stack(team_gather(z))
     small = jnp.stack(
         [
-            grad_gain_one, grad_bias_one, grad_gain_two, grad_bias_two,
+            norm_sums[0], norm_sums[1], grad_gain_two, grad_bias_two,
             jnp.pad(counts, (0, width - experts)),
         ]
     )
-    for axis, size in (("ex", experts), ("seq", seq)):
-        for b in range(size.bit_length() - 1):
-            small = small + swap(small, axis, 1 << b)
+    small = small + swap(small, "ex", 1)
+    pieces_a, half_c = sync(pieces_a, half_c)
+
+    c = first_hop(half_c)
+    all_a = team_gather(jnp.stack(pieces_a))
+    pieces_b, grads = sync(pieces_b, grads)
+
+    pieces_b = pieces_b + [row_send(pieces_b[-1], 1)]
+    grads = jnp.sum(grads.astype(FULL), 0).astype(LOW)
+    grads = swap_rows(jnp.broadcast_to(grads[None], (rows,) + grads.shape))
+    c, small = sync(c, small)
+
+    c = next_hop(c, half_c, 0)
+    small = small + swap(small, "ex", 2)
+    pieces_b = sync(pieces_b)[0]
+
+    pieces_b = pieces_b + [row_send(pieces_b[-1], 1)]
+    c, z = sync(c, z)
+
+    c = next_hop(c, half_c, 1)
+    pieces_b, grads, all_a = sync(pieces_b, grads, all_a)
+
+    share_grads = team_gather(grads)
+    all_b = team_gather(jnp.stack(pieces_b))
+    pieces_z = [z, row_send(z, 1)]
+    grad_up = put_chunk(own, all_a, None, up_shape, (0, 0), team_first)
+    c, small, grad_up = sync(c, small, grad_up)
+
+    c = joined(c, half_c, 2)
+    pieces_c = [c, row_send(c, 1)]
+    small = small + swap(small, "seq", 1)
+    pieces_z = sync(pieces_z)[0]
+
+    pieces_z = pieces_z + [row_send(pieces_z[-1], 1)]
+    pieces_c, share_grads = sync(pieces_c, share_grads)
+
+    pieces_c = pieces_c + [row_send(pieces_c[-1], 1)]
+    far_grads = [swap(part, "ex", 2) for part in share_grads]
+    pieces_z, small, grad_change = sync(pieces_z, small, grad_change)
+
+    pieces_z = pieces_z + [row_send(pieces_z[-1], 1)]
+    small = small + swap(small, "seq", 2)
+    pieces_c, all_b, far_grads, share_grads = sync(pieces_c, all_b, far_grads, share_grads)
+
+    pieces_c = pieces_c + [row_send(pieces_c[-1], 1)]
+    near = [swap(part, "ex", 1) for part in share_grads]
+    far = [swap(part, "ex", 1) for part in far_grads]
+    grad_up = put_chunk(own, all_b, grad_up, up_shape, (0, 1), team_first)
+    pieces_z, small, grad_up = sync(pieces_z, small, grad_up)
+
+    grad_change = swap_rows(grad_change)
+    for bit in range(2, seq.bit_length() - 1):
+        small = small + swap(small, "seq", 1 << bit)
+    pieces_c, near, far, share_grads, far_grads = sync(
+        pieces_c, near, far, share_grads, far_grads
+    )
+
+    all_c = team_gather(jnp.stack(pieces_c))
+    parts = share_grads + near + far_grads + far
+    grad_qkv, grad_attn_out = place_weights(own, parts, team, rows, experts)
+    grad_down = put_chunk(own, pieces_z, None, down_shape, (0, 0), rows_first)
+    grad_input = grad_out + grad_change.astype(FULL)
+    all_c, grad_qkv, grad_input, grad_down = sync(all_c, grad_qkv, grad_input, grad_down)
+
+    if padded != width:
+        grad_qkv = grad_qkv.reshape(width, 3, padded)[..., :width].reshape(width, 3 * width)
+        grad_attn_out = grad_attn_out[:width]
+    grad_down = put_chunk(own, all_c, grad_down, down_shape, (1, 0), team_first)
     load = small[4, :experts] * (experts / (rows * length * experts))
     return (
-        block_output, grad_input, grad_qkv, grad_attn_out, small[0], small[1], small[2], small[3],
-        grad_up[None], grad_down[None], load,
+        block_output, grad_input, grad_qkv, grad_attn_out, small[0], small[1], small[2],
+        small[3], grad_up[None], grad_down[None], load,
     )
 
 

time: 650 us -> 490 us (0.75)
  waiting for transfers between devices: 339 us -> 154 us
  Pallas kernels: 90 us -> 125 us
  local copies, waits for them, and re-layouts: 55.2 us -> 40 us
    ppermute x16 -> x17, waiting for transfers between devices: 92.9 us -> 4.37 us  [team_send(): return lax.ppermute(value, 'seq', pattern)]
    ppermute x42 -> x30, waiting for transfers between devices: 184 us -> 99.3 us  [row_send(): return lax.ppermute(value, 'seq', pattern)]
    pallas_call x0 -> x36, Pallas kernels: none -> 33.6 us  [the longest x4 19.4 us: put_chunk(): pl.pallas_call(functools.partial(put_kernel, count, len(joined), place),...]
    all_to_all x0 -> x7, starting transfers between devices: none -> 29.5 us  [the longest x4 17.9 us: swap_rows(): lax.all_to_all(value, 'seq', 0, 0, tiled=True, axis_index_groups=across_r...]
    ppermute x21 -> x17, waiting for transfers between devices: 63.1 us -> 36.8 us  [swap(): lax.ppermute(value, axis, [(a, a ^ m) for a in range(lax.axis_size(axis))])]
    ppermute x42 -> x30, starting transfers between devices: 51.2 us -> 27.2 us  [row_send(): return lax.ppermute(value, 'seq', pattern)]
    convert_element_type x3 -> x0, local copies, waits for them, and re-layouts: 22.9 us -> none  [the longest x2 21.1 us: per_device(): grad_qkv = grad_qkv[..., :width].reshape(width, 3 * width).astype(FULL)]
    convert_element_type x14 -> x17, other arithmetic: 14.3 us -> 30.9 us  [add_low(): return (a.astype(FULL) + b.astype(FULL)).astype(LOW)]
  transfers between devices with their start and end apart: 79 -> 71, of which waited for: 38 -> 26; matrix products, arithmetic and copies ran while one was open for 12% -> 19% of each run, Pallas kernels for 4% -> 21%
where the time goes in v3:
time: 490 us; the launch traced here: 485 us
  waiting for transfers between devices  154 us (31%)
  Pallas kernels  125 us (26%)
  starting transfers between devices  91.5 us (19%)
  other arithmetic  63.4 us (13%)
  local copies, waits for them, and re-layouts  40 us (8%)
  matrix products  8.79 us (2%)
    ppermute x30, waiting for transfers between devices, row_send(): return lax.ppermute(value, 'seq', pattern)  99.3 us
    pallas_call x2, Pallas kernels, expert(): pl.pallas_call(functools.partial(expert_kernel, count, first, last), grid...  36.8 us
    ppermute x17, waiting for transfers between devices, swap(): lax.ppermute(value, axis, [(a, a ^ m) for a in range(lax.axis_size(axis))])  36.8 us
    convert_element_type x17, other arithmetic, add_low(): return (a.astype(FULL) + b.astype(FULL)).astype(LOW)  30.9 us
    pallas_call x1, Pallas kernels, attend_back(): pl.pallas_call(functools.partial(attend_back_kernel, team, rows, local, b...  28.2 us
    ppermute x30, starting transfers between devices, row_send(): return lax.ppermute(value, 'seq', pattern)  27.2 us
    pallas_call x1, Pallas kernels, attend(): pl.pallas_call(functools.partial(attend_kernel, team, rows, local, block,...  26.7 us
    ppermute x17, starting transfers between devices, team_send(): return lax.ppermute(value, 'seq', pattern)  19.9 us
  transfers between devices with their start and end apart: 71, of which 26 were waited for; matrix products, arithmetic and copies ran while one was open for 19% of the time, Pallas kernels for 21%

profile of v3, /device:TPU:0, one launch (start us, length us, event | category | flops | bytes accessed | tf_op | source)
XLA Modules:
  0.0 485.2 jit_solution(8068825936797999677)
XLA Ops:
  4.9 5.1 %collective-permute-start.2 = (bf16[128,768]{1,0:T(8,128)(2,1)S(1)}, bf16[128,768]{1,0:T(8,128)(2,1)S(1)}, u32[]{:S(2)}, u32[]{:S(2)}) collective-permute-start(bf16[128,768]{1,0:T(8,128)(2,1)S(1)} %get-tuple-element.317), channel_id=1, source_target_pairs={{0,24},{4,28},{8,0},{12,4},{16,8},{20,12},{24,16},{28,20},{1,25},{... | collective-permute-start | bytes 589832 | tf_op jit(solution)/shard_map/ppermute | solution.py:639
  16.8 9.8 %collective-permute-done.1.refs_2_ = bf16[128,768]{1,0:T(8,128)(2,1)S(1)} collective-permute-done((bf16[128,768]{1,0:T(8,128)(2,1)S(1)}, bf16[128,768]{1,0:T(8,128)(2,1)S(1)}, u32[]{:S(2)}, u32[]{:S(2)}) %collective-permute-start.1) | collective-permute-done | bytes 196640 | tf_op jit(solution)/shard_map/ppermute | solution.py:639
  31.1 2.0 collective-permute-start.8
  33.1 2.1 collective-permute-start.7
  37.5 26.7 %attend.1 = (bf16[1024,768]{1,0:T(8,128)(2,1)}, bf16[1024,384]{1,0:T(8,128)(2,1)}, bf16[1024,384]{1,0:T(8,128)(2,1)}, bf16[1024,384]{1,0:T(8,128)(2,1)}, f32[384...) custom-call(s32[3]{0:T(128)} %pad_add_fusion.own_ref, ...), custom_call_target="tpu_custom_call" | custom-call | flops 5033164800 | bytes 7864320 | tf_op jit(solution)/shard_map/attend/pallas_call | solution.py:268
  72.1 2.7 collective-permute-done.10
  81.1 3.6 collective-permute-done.16.refs_7_
  84.7 6.8 %collective-permute-done.12.refs_2_ = bf16[192,768]{1,0:T(8,128)(2,1)} collective-permute-done((bf16[192,768]{1,0:T(8,128)(2,1)S(1)}, bf16[192,768]{1,0:T(8,128)(2,1)}, u32[]{:S(2)}, u32[]{:S(2)}) %collective-permute-start.12) | collective-permute-done | bytes 294944 | tf_op jit(solution)/shard_map/ppermute | solution.py:650
  91.4 2.8 collective-permute-done.13.refs_3_
  94.2 17.7 %expert.2 = (bf16[768,1536]{1,0:T(8,128)(2,1)}, bf16[1536,768]{1,0:T(8,128)(2,1)}, f32[768,768]{1,0:T(8,128)}, f32[768,768]{1,0:T(8,128)}) custom-call(s32[3]{0:T(128)} %pad_add_fusion.own_ref, bf16[192,768]{1,0:T(8,128)(2,1)} %bitcast.244, bf16[192,768]{1,0:T(8,128)(2,1)} %collective-permute-done.11.refs_1_, ...), custom_call_target="tpu_custom_call" | custom-call | flops 10871635968 | bytes 14155776 | tf_op jit(solution)/shard_map/expert/pallas_call | solution.py:429
  113.1 3.0 fusion.61
  118.5 19.1 %expert.3 = (bf16[768,1536]{1,0:T(8,128)(2,1)}, bf16[1536,768]{1,0:T(8,128)(2,1)}, bf16[4,192,768]{2,1,0:T(8,128)(2,1)}, bf16[4,192,768]{2,1,0:T(8,128)(2,1)}) custom-call(s32[3]{0:T(128)} %pad_add_fusion.own_ref, bf16[192,768]{1,0:T(8,128)(2,1)} %bitcast.245, bf16[192,768]{1,0:T(8,128)(2,1)} %collective-permute-done.11.refs_1_, ...), custom_call_target="tpu_custom_call" | custom-call | flops 10871635968 | bytes 14155776 | tf_op jit(solution)/shard_map/expert/pallas_call | solution.py:429
  138.5 4.4 all-to-all-start
  145.3 2.0 fusion.11
  148.4 2.0 fusion.13.refs_2_
  150.4 8.4 %all-to-all-done.refs_0_ = bf16[4,192,768]{2,1,0:T(8,128)(2,1)} async-done(((bf16[4,192,768]{2,1,0:T(8,128)(2,1)}), bf16[4,192,768]{2,1,0:T(8,128)(2,1)}, u32[]{:S(2)}, u32[]{:S(2)}) %all-to-all-start) | async-done | bytes 1179680 | tf_op jit(solution)/shard_map/all_to_all | solution.py:658
  158.8 3.5 all-to-all-start.1
  162.4 2.4 bitcast_reduce_fusion
  166.0 2.0 fusion.4
  168.8 2.3 fusion.10
  178.1 11.6 %collective-permute-done.23.refs_0_ = bf16[2,192,768]{2,1,0:T(8,128)(2,1)S(1)} collective-permute-done((bf16[2,192,768]{2,1,0:T(8,128)(2,1)}, bf16[2,192,768]{2,1,0:T(8,128)(2,1)S(1)}, u32[]{:S(2)}, u32[]{:S(2)}) %collective-permute-start.23) | collective-permute-done | bytes 589856 | tf_op jit(solution)/shard_map/ppermute | solution.py:639
  191.6 1.9 fusion.14
  199.7 2.0 fusion.9.refs_2_
  201.7 6.0 %collective-permute-done.24.refs_0_ = bf16[96,1536]{1,0:T(8,128)(2,1)} collective-permute-done((bf16[96,1536]{1,0:T(8,128)(2,1)S(1)}, bf16[96,1536]{1,0:T(8,128)(2,1)}, u32[]{:S(2)}, u32[]{:S(2)}) %collective-permute-start.24) | collective-permute-done | bytes 294944 | tf_op jit(solution)/shard_map/ppermute | solution.py:639
  207.8 1.9 fusion.28
  209.7 4.2 all-to-all-start.2
  213.9 2.0 collective-permute-start.26
  218.5 28.2 %attend_back.1 = (bf16[4,128,768]{2,1,0:T(8,128)(2,1)}, bf16[4,128,768]{2,1,0:T(8,128)(2,1)}, bf16[4,4,192,384]{3,2,1,0:T(8,128)(2,1)}) custom-call(s32[3]{0:T(128)} %pad_add_fusion.own_ref, bf16[4,128,768]{2,1,0:T(8,128)(2,1)} %get-tuple-element.179.refs_0_, bf16[4,128,768]{2,1,0:T(8,128)(2,1)} %get-tuple-element.180.refs_1_, ...), custom_call_target="tpu_custom_call" | custom-call | flops 12884901888 | bytes 14155776 | tf_op jit(solution)/shard_map/attend_back/pallas_call | solution.py:306
  246.7 2.6 fusion.1.refs_0_
  252.9 3.6 all-to-all-start.3
  258.3 2.9 fusion.refs_1_
  262.7 2.9 convert_add_fusion.4.refs_1_
  265.6 7.1 %collective-permute-done.29.refs_1_ = bf16[96,1536]{1,0:T(8,128)(2,1)} collective-permute-done((bf16[96,1536]{1,0:T(8,128)(2,1)}, bf16[96,1536]{1,0:T(8,128)(2,1)}, u32[]{:S(2)}, u32[]{:S(2)}) %collective-permute-start.29) | collective-permute-done | bytes 294944 | tf_op jit(solution)/shard_map/ppermute | solution.py:639
  274.5 2.2 pad_maximum_fusion.5.refs_2_
  279.0 5.7 %collective-permute-done.30.refs_2_ = bf16[96,1536]{1,0:T(8,128)(2,1)} collective-permute-done((bf16[96,1536]{1,0:T(8,128)(2,1)}, bf16[96,1536]{1,0:T(8,128)(2,1)}, u32[]{:S(2)}, u32[]{:S(2)}) %collective-permute-start.30) | collective-permute-done | bytes 294944 | tf_op jit(solution)/shard_map/ppermute | solution.py:639
  284.7 6.3 %collective-permute-done.34.refs_0_ = bf16[96,1536]{1,0:T(8,128)(2,1)} collective-permute-done((bf16[96,1536]{1,0:T(8,128)(2,1)}, bf16[96,1536]{1,0:T(8,128)(2,1)}, u32[]{:S(2)}, u32[]{:S(2)}) %collective-permute-start.34) | collective-permute-done | bytes 294944 | tf_op jit(solution)/shard_map/ppermute | solution.py:639
  295.8 1.8 fusion.24.refs_1_
  297.6 5.5 %norm_back.1 = (bf16[4,128,768]{2,1,0:T(8,128)(2,1)}, f32[8,768]{1,0:T(8,128)}) custom-call(s32[3]{0:T(128)} %pad_add_fusion.own_ref, bf16[4,128,768]{2,1,0:T(8,128)(2,1)} %get-tuple-element.211.refs_0_, bf16[4,128,768]{2,1,0:T(8,128)(2,1)} %get-tuple-element.212.refs_1_, bf16[4,128,768]{2,1,0:T(8,128)(2,1)} %pad_maximum_fusion.5.refs_2_, ...), custom_call_target="tpu_custom_call" | custom-call | bytes 15728640 | tf_op jit(solution)/shard_map/norm_back/pallas_call | solution.py:572
  304.5 1.9 copy.164
  306.4 5.1 %all-to-all-start.4 = ((bf16[4,4,48,384]{3,2,1,0:T(8,128)(2,1)}), bf16[4,4,48,384]{3,2,1,0:T(8,128)(2,1)}, u32[]{:S(2)}, u32[]{:S(2)}) async-start(bf16[4,4,48,384]{3,2,1,0:T(8,128)(2,1)} %bitcast.210), calls=%async_computation.4 | async-start | bytes 1179648 | tf_op jit(solution)/shard_map/all_to_all | solution.py:655
  312.7 2.1 collective-permute-start.42
  321.7 10.4 %collective-permute-done.42.refs_1_ = bf16[96,1536]{1,0:T(8,128)(2,1)S(1)} collective-permute-done((bf16[96,1536]{1,0:T(8,128)(2,1)S(1)}, bf16[96,1536]{1,0:T(8,128)(2,1)S(1)}, u32[]{:S(2)}, u32[]{:S(2)}) %collective-permute-start.42) | collective-permute-done | bytes 294944 | tf_op jit(solution)/shard_map/ppermute | solution.py:639
  332.1 5.5 %all-to-all-done.4.refs_2_ = bf16[4,4,48,384]{3,2,1,0:T(8,128)(2,1)} async-done(((bf16[4,4,48,384]{3,2,1,0:T(8,128)(2,1)}), bf16[4,4,48,384]{3,2,1,0:T(8,128)(2,1)}, u32[]{:S(2)}, u32[]{:S(2)}) %all-to-all-start.4) | async-done | bytes 589856 | tf_op jit(solution)/shard_map/all_to_all | solution.py:655
  339.6 3.5 all-to-all-start.5
  345.2 2.0 collective-permute-start.43
  350.4 13.1 %collective-permute-done.43.refs_2_ = bf16[96,1536]{1,0:T(8,128)(2,1)S(1)} collective-permute-done((bf16[96,1536]{1,0:T(8,128)(2,1)S(1)}, bf16[96,1536]{1,0:T(8,128)(2,1)S(1)}, u32[]{:S(2)}, u32[]{:S(2)}) %collective-permute-start.43) | collective-permute-done | bytes 294944 | tf_op jit(solution)/shard_map/ppermute | solution.py:639
  364.2 1.9 pad_maximum_fusion.6.refs_1_
  369.8 3.2 collective-permute-done.44.refs_3_
  378.2 3.0 collective-permute-done.41
  381.8 4.8 put_chunk.4.refs_2_
  389.1 11.1 %collective-permute-done.46.refs_1_ = bf16[192,768]{1,0:T(8,128)(2,1)S(1)} collective-permute-done((bf16[192,768]{1,0:T(8,128)(2,1)S(1)}, bf16[192,768]{1,0:T(8,128)(2,1)S(1)}, u32[]{:S(2)}, u32[]{:S(2)}) %collective-permute-start.46) | collective-permute-done | bytes 294944 | tf_op jit(solution)/shard_map/ppermute | solution.py:639
  402.9 5.4 %collective-permute-done.58.refs_1_ = bf16[2,192,768]{2,1,0:T(8,128)(2,1)S(1)} collective-permute-done((bf16[2,192,768]{2,1,0:T(8,128)(2,1)S(1)}, bf16[2,192,768]{2,1,0:T(8,128)(2,1)S(1)}, u32[]{:S(2)}, u32[]{:S(2)}) %collective-permute-start.58) | collective-permute-done | bytes 589856 | tf_op jit(solution)/shard_map/ppermute | solution.py:639
  409.1 2.6 collective-permute-done.48.refs_2_
  413.3 4.0 collective-permute-done.51.refs_6_
  419.2 1.8 collective-permute-done.59.refs_2_
  422.3 5.2 %all-to-all-start.6 = ((bf16[4,128,768]{2,1,0:T(8,128)(2,1)}), bf16[4,128,768]{2,1,0:T(8,128)(2,1)}, u32[]{:S(2)}, u32[]{:S(2)}) async-start(bf16[4,128,768]{2,1,0:T(8,128)(2,1)} %get-tuple-element.269), calls=%async_computation.6 | async-start | bytes 1572864 | tf_op jit(solution)/shard_map/all_to_all | solution.py:655
  427.5 3.0 collective-permute-done.52.refs_3_
  435.4 16.6 %collective-permute-done.62 = f32[5,768]{1,0:T(8,128)S(1)} collective-permute-done((f32[5,768]{1,0:T(8,128)S(1)}, f32[5,768]{1,0:T(8,128)S(1)}, u32[]{:S(2)}, u32[]{:S(2)}) %collective-permute-start.62) | collective-permute-done | bytes 15392 | tf_op jit(solution)/shard_map/ppermute | solution.py:650
  452.6 4.8 put_chunk.5.refs_5_
  458.2 4.6 collective-permute-start.63
  462.8 4.9 %put_chunk.6.refs_4_ = f32[3072,768]{1,0:T(8,128)} custom-call(s32[3]{0:T(128)} %pad_add_fusion.own_ref, bf16[2,192,768]{2,1,0:T(8,128)(2,1)} %get-tuple-element.277.refs_0_, bf16[2,192,768]{2,1,0:T(8,128)(2,1)} %get-tuple-element.278.refs_1_, bf16[2,192,768]{2,1,0:T(8,128)(2,1)} %get-tuple-element.279.refs_2_, bf16[2,192,768]{2,1,0:T(8,128)(2,1)} %get-tuple-element.280.refs_3_), custom_call_target="tpu_custom_call" | custom-call | bytes 9437184 | tf_op jit(solution)/shard_map/put_chunk/pallas_call | solution.py:474
  468.9 2.4 convert_add_fusion.3.refs_3_
  471.3 8.7 %place_weights.1 = (f32[768,2304]{1,0:T(8,128)}, f32[768,768]{1,0:T(8,128)}) custom-call(s32[3]{0:T(128)} %pad_add_fusion.own_ref, bf16[4,4,48,384]{3,2,1,0:T(8,128)(2,1)} %get-tuple-element.255.refs_0_, bf16[4,4,48,384]{3,2,1,0:T(8,128)(2,1)} %get-tuple-element.256.refs_1_, bf16[4,4,48,384]{3,2,1,0:T(8,128)(2,1)} %get-tuple-element.257.refs_2_, ...), custom_call_target="tpu_custom_call" | custom-call | bytes 14155776 | tf_op jit(solution)/shard_map/place_weights/pallas_call | solution.py:525
  480.1 4.9 %put_chunk.7 = f32[3072,768]{1,0:T(8,128)} custom-call(s32[3]{0:T(128)} %pad_add_fusion.own_ref, bf16[4,192,768]{2,1,0:T(8,128)(2,1)} %get-tuple-element.286.refs_0_, bf16[4,192,768]{2,1,0:T(8,128)(2,1)} %get-tuple-element.287.refs_1_, f32[3072,768]{1,0:T(8,128)} %get-tuple-element.288.refs_2_), custom_call_target="tpu_custom_call", output_to_operand_aliasing={{}: (3, {})} | custom-call | bytes 9437184 | tf_op jit(solution)/shard_map/put_chunk/pallas_call | solution.py:474
  (380 shorter events, 119.9 us)
Async XLA Ops:
  4.9 11.0 %collective-permute-start.2 = (bf16[128,768]{1,0:T(8,128)(2,1)S(1)}, bf16[128,768]{1,0:T(8,128)(2,1)S(1)}, u32[]{:S(2)}, u32[]{:S(2)}) collective-permute-start(bf16[128,768]{1,0:T(8,128)(2,1)S(1)} %get-tuple-element.317), channel_id=1, source_target_pairs={{0,24},{4,28},{8,0},{12,4},{16,8},{20,12},{24,16},{28,20},{1,25},{... | collective-permute-start | bytes 589832 | tf_op jit(solution)/shard_map/ppermute | solution.py:639
  10.0 16.7 %collective-permute-start.1 = (bf16[128,768]{1,0:T(8,128)(2,1)S(1)}, bf16[128,768]{1,0:T(8,128)(2,1)S(1)}, u32[]{:S(2)}, u32[]{:S(2)}) collective-permute-start(bf16[128,768]{1,0:T(8,128)(2,1)S(1)} %get-tuple-element.318), channel_id=1, source_target_pairs={{0,16},{4,20},{8,24},{12,28},{16,0},{20,4},{24,8},{28,12},{1,17},{... | collective-permute-start | bytes 589832 | tf_op jit(solution)/shard_map/ppermute | solution.py:639
  10.0 18.2 %collective-permute-start = (bf16[128,768]{1,0:T(8,128)(2,1)S(1)}, bf16[128,768]{1,0:T(8,128)(2,1)S(1)}, u32[]{:S(2)}, u32[]{:S(2)}) collective-permute-start(bf16[128,768]{1,0:T(8,128)(2,1)S(1)} %get-tuple-element.319), channel_id=1, source_target_pairs={{0,8},{4,12},{8,16},{12,20},{16,24},{20,28},{24,0},{28,4},{1,9},{5... | collective-permute-start | bytes 589832 | tf_op jit(solution)/shard_map/ppermute | solution.py:639
  11.0 20.1 %collective-permute-start.3 = (bf16[128,768]{1,0:T(8,128)(2,1)S(1)}, bf16[128,768]{1,0:T(8,128)(2,1)S(1)}, u32[]{:S(2)}, u32[]{:S(2)}) collective-permute-start(bf16[128,768]{1,0:T(8,128)(2,1)S(1)} %bitcast.232), channel_id=1, source_target_pairs={{0,4},{4,0},{8,12},{12,8},{16,20},{20,16},{24,28},{28,24},{1,5},{5... | collective-permute-start | bytes 589832 | tf_op jit(solution)/shard_map/ppermute | solution.py:645
  15.9 17.2 %collective-permute-start.6 = (bf16[128,768]{1,0:T(8,128)(2,1)S(1)}, bf16[128,768]{1,0:T(8,128)(2,1)S(1)}, u32[]{:S(2)}, u32[]{:S(2)}) collective-permute-start(bf16[128,768]{1,0:T(8,128)(2,1)S(1)} %collective-permute-done.2.refs_3_), channel_id=1, source_target_pairs={{0,4},{4,0},{8,12},{12,8},{16,20},{20,16},{24,28},{28,24},{1,5},{5... | collective-permute-start | bytes 589832 | tf_op jit(solution)/shard_map/ppermute | solution.py:645
  30.7 33.5 %collective-permute-start.9 = (bf16[144,768]{1,0:T(8,128)(2,1)S(1)}, bf16[144,768]{1,0:T(8,128)(2,1)S(1)}, u32[]{:S(2)}, u32[]{:S(2)}) collective-permute-start(bf16[144,768]{1,0:T(8,128)(2,1)S(1)} %get-tuple-element.314), channel_id=1, source_target_pairs={{0,24},{4,28},{8,0},{12,4},{16,8},{20,12},{24,16},{28,20},{1,25},{... | collective-permute-start | bytes 663560 | tf_op jit(solution)/shard_map/ppermute | solution.py:639
  31.1 33.1 %collective-permute-start.8 = (bf16[144,768]{1,0:T(8,128)(2,1)S(1)}, bf16[144,768]{1,0:T(8,128)(2,1)S(1)}, u32[]{:S(2)}, u32[]{:S(2)}) collective-permute-start(bf16[144,768]{1,0:T(8,128)(2,1)S(1)} %get-tuple-element.315), channel_id=1, source_target_pairs={{0,16},{4,20},{8,24},{12,28},{16,0},{20,4},{24,8},{28,12},{1,17},{... | collective-permute-start | bytes 663560 | tf_op jit(solution)/shard_map/ppermute | solution.py:639
  33.1 31.1 %collective-permute-start.7 = (bf16[144,768]{1,0:T(8,128)(2,1)S(1)}, bf16[144,768]{1,0:T(8,128)(2,1)S(1)}, u32[]{:S(2)}, u32[]{:S(2)}) collective-permute-start(bf16[144,768]{1,0:T(8,128)(2,1)S(1)} %get-tuple-element.316), channel_id=1, source_target_pairs={{0,8},{4,12},{8,16},{12,20},{16,24},{20,28},{24,0},{28,4},{1,9},{5... | collective-permute-start | bytes 663560 | tf_op jit(solution)/shard_map/ppermute | solution.py:639
  69.3 11.1 %collective-permute-start.15 = (bf16[192,768]{1,0:T(8,128)(2,1)S(1)}, bf16[192,768]{1,0:T(8,128)(2,1)S(1)}, u32[]{:S(2)}, u32[]{:S(2)}) collective-permute-start(bf16[192,768]{1,0:T(8,128)(2,1)S(1)} %bitcast.251), channel_id=1, source_target_pairs={{0,2},{1,3},{2,0},{3,1},{4,6},{5,7},{6,4},{7,5},{8,10},{9,11},{10,... | collective-permute-start | bytes 884744 | tf_op jit(solution)/shard_map/ppermute | solution.py:650
  70.9 13.8 %collective-permute-start.16 = (bf16[192,768]{1,0:T(8,128)(2,1)S(1)}, bf16[192,768]{1,0:T(8,128)(2,1)}, u32[]{:S(2)}, u32[]{:S(2)}) collective-permute-start(bf16[192,768]{1,0:T(8,128)(2,1)S(1)} %bitcast.247), channel_id=1, source_target_pairs={{0,3},{1,2},{2,1},{3,0},{4,7},{5,6},{6,5},{7,4},{8,11},{9,10},{10,... | collective-permute-start | bytes 884744 | tf_op jit(solution)/shard_map/ppermute | solution.py:650
  70.9 13.8 %collective-permute-start.14 = (bf16[192,768]{1,0:T(8,128)(2,1)S(1)}, bf16[192,768]{1,0:T(8,128)(2,1)}, u32[]{:S(2)}, u32[]{:S(2)}) collective-permute-start(bf16[192,768]{1,0:T(8,128)(2,1)S(1)} %bitcast.246), channel_id=1, source_target_pairs={{0,1},{1,0},{2,3},{3,2},{4,5},{5,4},{6,7},{7,6},{8,9},{9,8},{10,11... | collective-permute-start | bytes 884744 | tf_op jit(solution)/shard_map/ppermute | solution.py:650
  78.9 12.5 %collective-permute-start.12 = (bf16[192,768]{1,0:T(8,128)(2,1)S(1)}, bf16[192,768]{1,0:T(8,128)(2,1)}, u32[]{:S(2)}, u32[]{:S(2)}) collective-permute-start(bf16[192,768]{1,0:T(8,128)(2,1)S(1)} %bitcast.250), channel_id=1, source_target_pairs={{0,2},{1,3},{2,0},{3,1},{4,6},{5,7},{6,4},{7,5},{8,10},{9,11},{10,... | collective-permute-start | bytes 884744 | tf_op jit(solution)/shard_map/ppermute | solution.py:650
  80.4 13.8 %collective-permute-start.13 = (bf16[192,768]{1,0:T(8,128)(2,1)S(1)}, bf16[192,768]{1,0:T(8,128)(2,1)}, u32[]{:S(2)}, u32[]{:S(2)}) collective-permute-start(bf16[192,768]{1,0:T(8,128)(2,1)S(1)} %bitcast.249), channel_id=1, source_target_pairs={{0,3},{1,2},{2,1},{3,0},{4,7},{5,6},{6,5},{7,4},{8,11},{9,10},{10,... | collective-permute-start | bytes 884744 | tf_op jit(solution)/shard_map/ppermute | solution.py:650
  80.4 13.8 %collective-permute-start.11 = (bf16[192,768]{1,0:T(8,128)(2,1)S(1)}, bf16[192,768]{1,0:T(8,128)(2,1)}, u32[]{:S(2)}, u32[]{:S(2)}) collective-permute-start(bf16[192,768]{1,0:T(8,128)(2,1)S(1)} %bitcast.248), channel_id=1, source_target_pairs={{0,1},{1,0},{2,3},{3,2},{4,5},{5,4},{6,7},{7,6},{8,9},{9,8},{10,11... | collective-permute-start | bytes 884744 | tf_op jit(solution)/shard_map/ppermute | solution.py:650
  113.1 24.6 %collective-permute-start.17 = (bf16[2,192,768]{2,1,0:T(8,128)(2,1)S(1)}, bf16[2,192,768]{2,1,0:T(8,128)(2,1)S(1)}, u32[]{:S(2)}, u32[]{:S(2)}) collective-permute-start(bf16[2,192,768]{2,1,0:T(8,128)(2,1)S(1)} %dynamic-slice_bitcast_fusion.4), channel_id=1, source_target_pairs={{0,8},{4,12},{8,16},{12,20},{16,24},{20,28},{24,0},{28,4},{1,9},{5... | collective-permute-start | bytes 1769480 | tf_op jit(solution)/shard_map/ppermute | solution.py:639
  118.0 30.4 %collective-permute-start.18 = (bf16[4,48,1536]{2,1,0:T(8,128)(2,1)}, bf16[4,48,1536]{2,1,0:T(8,128)(2,1)}, u32[]{:S(2)}, u32[]{:S(2)}) collective-permute-start(bf16[4,48,1536]{2,1,0:T(8,128)(2,1)} %dynamic-slice_bitcast_fusion.3), channel_id=1, source_target_pairs={{0,4},{4,0},{8,12},{12,8},{16,20},{20,16},{24,28},{28,24},{1,5},{5... | collective-permute-start | bytes 1769480 | tf_op jit(solution)/shard_map/ppermute | solution.py:645
  138.5 20.3 %all-to-all-start = ((bf16[4,192,768]{2,1,0:T(8,128)(2,1)}), bf16[4,192,768]{2,1,0:T(8,128)(2,1)}, u32[]{:S(2)}, u32[]{:S(2)}) async-start(bf16[4,192,768]{2,1,0:T(8,128)(2,1)} %get-tuple-element.160), calls=%async_computation | async-start | bytes 2359296 | tf_op jit(solution)/shard_map/all_to_all | solution.py:658
  143.8 28.8 %collective-permute-start.19 = (bf16[4,48,1536]{2,1,0:T(8,128)(2,1)}, bf16[4,48,1536]{2,1,0:T(8,128)(2,1)}, u32[]{:S(2)}, u32[]{:S(2)}) collective-permute-start(bf16[4,48,1536]{2,1,0:T(8,128)(2,1)} %dynamic-slice_bitcast_fusion.2), channel_id=1, source_target_pairs={{0,4},{4,0},{8,12},{12,8},{16,20},{20,16},{24,28},{28,24},{1,5},{5... | collective-permute-start | bytes 1769480 | tf_op jit(solution)/shard_map/ppermute | solution.py:645
  147.3 20.6 %collective-permute-start.22 = (bf16[2,192,768]{2,1,0:T(8,128)(2,1)}, bf16[2,192,768]{2,1,0:T(8,128)(2,1)S(1)}, u32[]{:S(2)}, u32[]{:S(2)}) collective-permute-start(bf16[2,192,768]{2,1,0:T(8,128)(2,1)} %fusion.11), channel_id=1, source_target_pairs={{0,8},{4,12},{8,16},{12,20},{16,24},{20,28},{24,0},{28,4},{1,9},{5... | collective-permute-start | bytes 1769480 | tf_op jit(solution)/shard_map/ppermute | solution.py:639
  158.8 30.9 %all-to-all-start.1 = ((bf16[4,192,768]{2,1,0:T(8,128)(2,1)}), bf16[4,192,768]{2,1,0:T(8,128)(2,1)S(1)}, u32[]{:S(2)}, u32[]{:S(2)}) async-start(bf16[4,192,768]{2,1,0:T(8,128)(2,1)} %get-tuple-element.171), calls=%async_computation.1 | async-start | bytes 2359296 | tf_op jit(solution)/shard_map/all_to_all | solution.py:658
  171.1 18.6 %collective-permute-start.23 = (bf16[2,192,768]{2,1,0:T(8,128)(2,1)}, bf16[2,192,768]{2,1,0:T(8,128)(2,1)S(1)}, u32[]{:S(2)}, u32[]{:S(2)}) collective-permute-start(bf16[2,192,768]{2,1,0:T(8,128)(2,1)} %fusion.10), channel_id=1, source_target_pairs={{0,8},{4,12},{8,16},{12,20},{16,24},{20,28},{24,0},{28,4},{1,9},{5... | collective-permute-start | bytes 1769480 | tf_op jit(solution)/shard_map/ppermute | solution.py:639
  176.6 19.3 %collective-permute-start.21 = (bf16[96,1536]{1,0:T(8,128)(2,1)}, bf16[96,1536]{1,0:T(8,128)(2,1)}, u32[]{:S(2)}, u32[]{:S(2)}) collective-permute-start(bf16[96,1536]{1,0:T(8,128)(2,1)} %dynamic-slice_bitcast_fusion.8), channel_id=1, source_target_pairs={{0,8},{4,12},{8,16},{12,20},{16,24},{20,28},{24,0},{28,4},{1,9},{5... | collective-permute-start | bytes 884744 | tf_op jit(solution)/shard_map/ppermute | solution.py:639
  177.1 24.6 %collective-permute-start.25 = (bf16[4,128,768]{2,1,0:T(8,128)(2,1)}, bf16[4,128,768]{2,1,0:T(8,128)(2,1)}, u32[]{:S(2)}, u32[]{:S(2)}) collective-permute-start(bf16[4,128,768]{2,1,0:T(8,128)(2,1)} %get-tuple-element.174.refs_1_), channel_id=1, source_target_pairs={{0,4},{4,0},{8,12},{12,8},{16,20},{20,16},{24,28},{28,24},{1,5},{5... | collective-permute-start | bytes 2359304 | tf_op jit(solution)/shard_map/ppermute | solution.py:645
  197.0 10.7 %collective-permute-start.24 = (bf16[96,1536]{1,0:T(8,128)(2,1)S(1)}, bf16[96,1536]{1,0:T(8,128)(2,1)}, u32[]{:S(2)}, u32[]{:S(2)}) collective-permute-start(bf16[96,1536]{1,0:T(8,128)(2,1)S(1)} %fusion.29), channel_id=1, source_target_pairs={{0,8},{4,12},{8,16},{12,20},{16,24},{20,28},{24,0},{28,4},{1,9},{5... | collective-permute-start | bytes 884744 | tf_op jit(solution)/shard_map/ppermute | solution.py:639
  198.2 48.5 %collective-permute-start.20 = (bf16[4,96,1536]{2,1,0:T(8,128)(2,1)}, bf16[4,96,1536]{2,1,0:T(8,128)(2,1)}, u32[]{:S(2)}, u32[]{:S(2)}) collective-permute-start(bf16[4,96,1536]{2,1,0:T(8,128)(2,1)} %dynamic-slice_bitcast_fusion.1), channel_id=1, source_target_pairs={{0,4},{4,0},{8,12},{12,8},{16,20},{20,16},{24,28},{28,24},{1,5},{5... | collective-permute-start | bytes 3538952 | tf_op jit(solution)/shard_map/ppermute | solution.py:645
  209.7 43.2 %all-to-all-start.2 = ((bf16[4,128,768]{2,1,0:T(8,128)(2,1)}), bf16[4,128,768]{2,1,0:T(8,128)(2,1)}, u32[]{:S(2)}, u32[]{:S(2)}) async-start(bf16[4,128,768]{2,1,0:T(8,128)(2,1)} %get-tuple-element.191), calls=%async_computation.2 | async-start | bytes 1572864 | tf_op jit(solution)/shard_map/all_to_all | solution.py:655
  213.9 35.4 %collective-permute-start.26 = (bf16[96,1536]{1,0:T(8,128)(2,1)}, bf16[96,1536]{1,0:T(8,128)(2,1)}, u32[]{:S(2)}, u32[]{:S(2)}) collective-permute-start(bf16[96,1536]{1,0:T(8,128)(2,1)} %fusion.28), channel_id=1, source_target_pairs={{0,8},{4,12},{8,16},{12,20},{16,24},{20,28},{24,0},{28,4},{1,9},{5... | collective-permute-start | bytes 884744 | tf_op jit(solution)/shard_map/ppermute | solution.py:639
  217.0 41.3 %collective-permute-start.28 = (bf16[4,192,768]{2,1,0:T(8,128)(2,1)}, bf16[4,192,768]{2,1,0:T(8,128)(2,1)}, u32[]{:S(2)}, u32[]{:S(2)}) collective-permute-start(bf16[4,192,768]{2,1,0:T(8,128)(2,1)} %dynamic-slice_bitcast_fusion), channel_id=1, source_target_pairs={{0,4},{4,0},{8,12},{12,8},{16,20},{20,16},{24,28},{28,24},{1,5},{5... | collective-permute-start | bytes 3538952 | tf_op jit(solution)/shard_map/ppermute | solution.py:645
  250.9 14.6 %collective-permute-start.27 = (bf16[96,1536]{1,0:T(8,128)(2,1)}, bf16[96,1536]{1,0:T(8,128)(2,1)}, u32[]{:S(2)}, u32[]{:S(2)}) collective-permute-start(bf16[96,1536]{1,0:T(8,128)(2,1)} %dynamic-slice_bitcast_fusion.7), channel_id=1, source_target_pairs={{0,8},{4,12},{8,16},{12,20},{16,24},{20,28},{24,0},{28,4},{1,9},{5... | collective-permute-start | bytes 884744 | tf_op jit(solution)/shard_map/ppermute | solution.py:639
  252.4 26.6 %collective-permute-start.31 = (bf16[4,128,768]{2,1,0:T(8,128)(2,1)}, bf16[4,128,768]{2,1,0:T(8,128)(2,1)}, u32[]{:S(2)}, u32[]{:S(2)}) collective-permute-start(bf16[4,128,768]{2,1,0:T(8,128)(2,1)} %get-tuple-element.201), channel_id=1, source_target_pairs={{0,4},{4,0},{8,12},{12,8},{16,20},{20,16},{24,28},{28,24},{1,5},{5... | collective-permute-start | bytes 2359304 | tf_op jit(solution)/shard_map/ppermute | solution.py:645
  252.9 38.2 %all-to-all-start.3 = ((bf16[4,4,192,384]{3,2,1,0:T(8,128)(2,1)}), bf16[4,4,192,384]{3,2,1,0:T(8,128)(2,1)S(1)}, u32[]{:S(2)}, u32[]{:S(2)}) async-start(bf16[4,4,192,384]{3,2,1,0:T(8,128)(2,1)} %get-tuple-element.208), calls=%async_computation.3 | async-start | bytes 4718592 | tf_op jit(solution)/shard_map/all_to_all | solution.py:658
  261.2 11.5 %collective-permute-start.29 = (bf16[96,1536]{1,0:T(8,128)(2,1)}, bf16[96,1536]{1,0:T(8,128)(2,1)}, u32[]{:S(2)}, u32[]{:S(2)}) collective-permute-start(bf16[96,1536]{1,0:T(8,128)(2,1)} %get-tuple-element.197.refs_0_), channel_id=1, source_target_pairs={{0,8},{4,12},{8,16},{12,20},{16,24},{20,28},{24,0},{28,4},{1,9},{5... | collective-permute-start | bytes 884744 | tf_op jit(solution)/shard_map/ppermute | solution.py:639
  272.7 12.0 %collective-permute-start.30 = (bf16[96,1536]{1,0:T(8,128)(2,1)}, bf16[96,1536]{1,0:T(8,128)(2,1)}, u32[]{:S(2)}, u32[]{:S(2)}) collective-permute-start(bf16[96,1536]{1,0:T(8,128)(2,1)} %get-tuple-element.199.refs_1_), channel_id=1, source_target_pairs={{0,8},{4,12},{8,16},{12,20},{16,24},{20,28},{24,0},{28,4},{1,9},{5... | collective-permute-start | bytes 884744 | tf_op jit(solution)/shard_map/ppermute | solution.py:639
  274.5 16.5 %collective-permute-start.34 = (bf16[96,1536]{1,0:T(8,128)(2,1)}, bf16[96,1536]{1,0:T(8,128)(2,1)}, u32[]{:S(2)}, u32[]{:S(2)}) collective-permute-start(bf16[96,1536]{1,0:T(8,128)(2,1)} %fusion.26), channel_id=1, source_target_pairs={{0,8},{4,12},{8,16},{12,20},{16,24},{20,28},{24,0},{28,4},{1,9},{5... | collective-permute-start | bytes 884744 | tf_op jit(solution)/shard_map/ppermute | solution.py:639
  277.5 18.3 %collective-permute-start.36 = (bf16[192,768]{1,0:T(8,128)(2,1)}, bf16[192,768]{1,0:T(8,128)(2,1)}, u32[]{:S(2)}, u32[]{:S(2)}) collective-permute-start(bf16[192,768]{1,0:T(8,128)(2,1)} %dynamic-slice_bitcast_fusion.5), channel_id=1, source_target_pairs={{0,4},{4,0},{8,12},{12,8},{16,20},{20,16},{24,28},{28,24},{1,5},{5... | collective-permute-start | bytes 884744 | tf_op jit(solution)/shard_map/ppermute | solution.py:645
  284.7 26.7 %collective-permute-start.32 = (bf16[96,1536]{1,0:T(8,128)(2,1)}, bf16[96,1536]{1,0:T(8,128)(2,1)}, u32[]{:S(2)}, u32[]{:S(2)}) collective-permute-start(bf16[96,1536]{1,0:T(8,128)(2,1)} %get-tuple-element.204.refs_2_), channel_id=1, source_target_pairs={{0,8},{4,12},{8,16},{12,20},{16,24},{20,28},{24,0},{28,4},{1,9},{5... | collective-permute-start | bytes 884744 | tf_op jit(solution)/shard_map/ppermute | solution.py:639
  294.2 17.3 %collective-permute-start.35 = (bf16[96,1536]{1,0:T(8,128)(2,1)}, bf16[96,1536]{1,0:T(8,128)(2,1)}, u32[]{:S(2)}, u32[]{:S(2)}) collective-permute-start(bf16[96,1536]{1,0:T(8,128)(2,1)} %fusion.25), channel_id=1, source_target_pairs={{0,8},{4,12},{8,16},{12,20},{16,24},{20,28},{24,0},{28,4},{1,9},{5... | collective-permute-start | bytes 884744 | tf_op jit(solution)/shard_map/ppermute | solution.py:639
  306.4 31.1 %all-to-all-start.4 = ((bf16[4,4,48,384]{3,2,1,0:T(8,128)(2,1)}), bf16[4,4,48,384]{3,2,1,0:T(8,128)(2,1)}, u32[]{:S(2)}, u32[]{:S(2)}) async-start(bf16[4,4,48,384]{3,2,1,0:T(8,128)(2,1)} %bitcast.210), calls=%async_computation.4 | async-start | bytes 1179648 | tf_op jit(solution)/shard_map/all_to_all | solution.py:655
  312.7 19.4 %collective-permute-start.42 = (bf16[96,1536]{1,0:T(8,128)(2,1)S(1)}, bf16[96,1536]{1,0:T(8,128)(2,1)S(1)}, u32[]{:S(2)}, u32[]{:S(2)}) collective-permute-start(bf16[96,1536]{1,0:T(8,128)(2,1)S(1)} %fusion.21.refs_0_), channel_id=1, source_target_pairs={{0,8},{4,12},{8,16},{12,20},{16,24},{20,28},{24,0},{28,4},{1,9},{5... | collective-permute-start | bytes 884744 | tf_op jit(solution)/shard_map/ppermute | solution.py:639
  316.1 53.7 %collective-permute-start.45 = (bf16[4,96,1536]{2,1,0:T(8,128)(2,1)S(1)}, bf16[4,96,1536]{2,1,0:T(8,128)(2,1)}, u32[]{:S(2)}, u32[]{:S(2)}) collective-permute-start(bf16[4,96,1536]{2,1,0:T(8,128)(2,1)S(1)} %pad_maximum_fusion.1.refs_5_), channel_id=1, source_target_pairs={{0,4},{4,0},{8,12},{12,8},{16,20},{20,16},{24,28},{28,24},{1,5},{5... | collective-permute-start | bytes 3538952 | tf_op jit(solution)/shard_map/ppermute | solution.py:645
  318.4 26.1 %collective-permute-start.33 = (bf16[192,768]{1,0:T(8,128)(2,1)}, bf16[192,768]{1,0:T(8,128)(2,1)S(1)}, u32[]{:S(2)}, u32[]{:S(2)}) collective-permute-start(bf16[192,768]{1,0:T(8,128)(2,1)} %dynamic-slice_bitcast_fusion.6), channel_id=1, source_target_pairs={{0,8},{4,12},{8,16},{12,20},{16,24},{20,28},{24,0},{28,4},{1,9},{5... | collective-permute-start | bytes 884744 | tf_op jit(solution)/shard_map/ppermute | solution.py:639
  321.2 21.9 %collective-permute-start.37 = (f32[5,768]{1,0:T(8,128)}, f32[5,768]{1,0:T(8,128)}, u32[]{:S(2)}, u32[]{:S(2)}) collective-permute-start(f32[5,768]{1,0:T(8,128)} %pad_maximum_fusion.7), channel_id=1, source_target_pairs={{0,1},{1,0},{2,3},{3,2},{4,5},{5,4},{6,7},{7,6},{8,9},{9,8},{10,11... | collective-permute-start | bytes 46088 | tf_op jit(solution)/shard_map/ppermute | solution.py:650
  321.2 43.0 %collective-permute-start.39 = (bf16[192,768]{1,0:T(8,128)(2,1)}, bf16[192,768]{1,0:T(8,128)(2,1)}, u32[]{:S(2)}, u32[]{:S(2)}) collective-permute-start(bf16[192,768]{1,0:T(8,128)(2,1)} %get-tuple-element.217), channel_id=1, source_target_pairs={{0,4},{4,0},{8,12},{12,8},{16,20},{20,16},{24,28},{28,24},{1,5},{5... | collective-permute-start | bytes 884744 | tf_op jit(solution)/shard_map/ppermute | solution.py:645
  339.6 33.4 %all-to-all-start.5 = ((bf16[4,4,48,384]{3,2,1,0:T(8,128)(2,1)}), bf16[4,4,48,384]{3,2,1,0:T(8,128)(2,1)S(1)}, u32[]{:S(2)}, u32[]{:S(2)}) async-start(bf16[4,4,48,384]{3,2,1,0:T(8,128)(2,1)} %broadcast_in_dim.15), calls=%async_computation.5 | async-start | bytes 1179648 | tf_op jit(solution)/shard_map/all_to_all | solution.py:655
  345.2 18.3 %collective-permute-start.43 = (bf16[96,1536]{1,0:T(8,128)(2,1)S(1)}, bf16[96,1536]{1,0:T(8,128)(2,1)S(1)}, u32[]{:S(2)}, u32[]{:S(2)}) collective-permute-start(bf16[96,1536]{1,0:T(8,128)(2,1)S(1)} %copy-done.35), channel_id=1, source_target_pairs={{0,8},{4,12},{8,16},{12,20},{16,24},{20,28},{24,0},{28,4},{1,9},{5... | collective-permute-start | bytes 884744 | tf_op jit(solution)/shard_map/ppermute | solution.py:639
  348.9 18.4 %collective-permute-start.38 = (bf16[192,768]{1,0:T(8,128)(2,1)}, bf16[192,768]{1,0:T(8,128)(2,1)}, u32[]{:S(2)}, u32[]{:S(2)}) collective-permute-start(bf16[192,768]{1,0:T(8,128)(2,1)} %fusion.23), channel_id=1, source_target_pairs={{0,8},{4,12},{8,16},{12,20},{16,24},{20,28},{24,0},{28,4},{1,9},{5... | collective-permute-start | bytes 884744 | tf_op jit(solution)/shard_map/ppermute | solution.py:639
  369.0 17.6 %collective-permute-start.40 = (bf16[192,768]{1,0:T(8,128)(2,1)}, bf16[192,768]{1,0:T(8,128)(2,1)S(1)}, u32[]{:S(2)}, u32[]{:S(2)}) collective-permute-start(bf16[192,768]{1,0:T(8,128)(2,1)} %fusion.22), channel_id=1, source_target_pairs={{0,8},{4,12},{8,16},{12,20},{16,24},{20,28},{24,0},{28,4},{1,9},{5... | collective-permute-start | bytes 884744 | tf_op jit(solution)/shard_map/ppermute | solution.py:639
  373.9 26.3 %collective-permute-start.47 = (bf16[4,4,48,384]{3,2,1,0:T(8,128)(2,1)}, bf16[4,4,48,384]{3,2,1,0:T(8,128)(2,1)}, u32[]{:S(2)}, u32[]{:S(2)}) collective-permute-start(bf16[4,4,48,384]{3,2,1,0:T(8,128)(2,1)} %get-tuple-element.235.refs_2_), channel_id=1, source_target_pairs={{0,4},{4,0},{8,12},{12,8},{16,20},{20,16},{24,28},{28,24},{1,5},{5... | collective-permute-start | bytes 1769480 | tf_op jit(solution)/shard_map/ppermute | solution.py:645
  376.8 36.4 %collective-permute-start.49 = (bf16[4,96,1536]{2,1,0:T(8,128)(2,1)S(1)}, bf16[4,96,1536]{2,1,0:T(8,128)(2,1)}, u32[]{:S(2)}, u32[]{:S(2)}) collective-permute-start(bf16[4,96,1536]{2,1,0:T(8,128)(2,1)S(1)} %pad_maximum_fusion.2.refs_3_), channel_id=1, source_target_pairs={{0,4},{4,0},{8,12},{12,8},{16,20},{20,16},{24,28},{28,24},{1,5},{5... | collective-permute-start | bytes 3538952 | tf_op jit(solution)/shard_map/ppermute | solution.py:645
  388.4 11.8 %collective-permute-start.46 = (bf16[192,768]{1,0:T(8,128)(2,1)S(1)}, bf16[192,768]{1,0:T(8,128)(2,1)S(1)}, u32[]{:S(2)}, u32[]{:S(2)}) collective-permute-start(bf16[192,768]{1,0:T(8,128)(2,1)S(1)} %fusion.20.refs_0_), channel_id=1, source_target_pairs={{0,8},{4,12},{8,16},{12,20},{16,24},{20,28},{24,0},{28,4},{1,9},{5... | collective-permute-start | bytes 884744 | tf_op jit(solution)/shard_map/ppermute | solution.py:639
  388.4 19.8 %collective-permute-start.58 = (bf16[2,192,768]{2,1,0:T(8,128)(2,1)S(1)}, bf16[2,192,768]{2,1,0:T(8,128)(2,1)S(1)}, u32[]{:S(2)}, u32[]{:S(2)}) collective-permute-start(bf16[2,192,768]{2,1,0:T(8,128)(2,1)S(1)} %copy-done.3), channel_id=1, source_target_pairs={{0,8},{4,12},{8,16},{12,20},{16,24},{20,28},{24,0},{28,4},{1,9},{5... | collective-permute-start | bytes 1769480 | tf_op jit(solution)/shard_map/ppermute | solution.py:639
  400.9 12.4 %collective-permute-start.50 = (bf16[4,4,48,384]{3,2,1,0:T(8,128)(2,1)}, bf16[4,4,48,384]{3,2,1,0:T(8,128)(2,1)S(1)}, u32[]{:S(2)}, u32[]{:S(2)}) collective-permute-start(bf16[4,4,48,384]{3,2,1,0:T(8,128)(2,1)} %get-tuple-element.242.refs_7_), channel_id=1, source_target_pairs={{0,2},{1,3},{2,0},{3,1},{4,6},{5,7},{6,4},{7,5},{8,10},{9,11},{10,... | collective-permute-start | bytes 1769480 | tf_op jit(solution)/shard_map/ppermute | solution.py:650
  401.7 15.6 %collective-permute-start.51 = (bf16[4,4,48,384]{3,2,1,0:T(8,128)(2,1)}, bf16[4,4,48,384]{3,2,1,0:T(8,128)(2,1)S(1)}, u32[]{:S(2)}, u32[]{:S(2)}) collective-permute-start(bf16[4,4,48,384]{3,2,1,0:T(8,128)(2,1)} %get-tuple-element.243.refs_8_), channel_id=1, source_target_pairs={{0,2},{1,3},{2,0},{3,1},{4,6},{5,7},{6,4},{7,5},{8,10},{9,11},{10,... | collective-permute-start | bytes 1769480 | tf_op jit(solution)/shard_map/ppermute | solution.py:650
  409.1 11.9 %collective-permute-start.59 = (bf16[2,192,768]{2,1,0:T(8,128)(2,1)}, bf16[2,192,768]{2,1,0:T(8,128)(2,1)S(1)}, u32[]{:S(2)}, u32[]{:S(2)}) collective-permute-start(bf16[2,192,768]{2,1,0:T(8,128)(2,1)} %get-tuple-element.266.refs_1_), channel_id=1, source_target_pairs={{0,8},{4,12},{8,16},{12,20},{16,24},{20,28},{24,0},{28,4},{1,9},{5... | collective-permute-start | bytes 1769480 | tf_op jit(solution)/shard_map/ppermute | solution.py:639
  418.1 12.4 %collective-permute-start.53 = (bf16[4,4,48,384]{3,2,1,0:T(8,128)(2,1)}, bf16[4,4,48,384]{3,2,1,0:T(8,128)(2,1)S(1)}, u32[]{:S(2)}, u32[]{:S(2)}) collective-permute-start(bf16[4,4,48,384]{3,2,1,0:T(8,128)(2,1)} %get-tuple-element.247.refs_8_), channel_id=1, source_target_pairs={{0,1},{1,0},{2,3},{3,2},{4,5},{5,4},{6,7},{7,6},{8,9},{9,8},{10,11... | collective-permute-start | bytes 1769480 | tf_op jit(solution)/shard_map/ppermute | solution.py:650
  418.1 12.4 %collective-permute-start.54 = (bf16[4,4,48,384]{3,2,1,0:T(8,128)(2,1)}, bf16[4,4,48,384]{3,2,1,0:T(8,128)(2,1)S(1)}, u32[]{:S(2)}, u32[]{:S(2)}) collective-permute-start(bf16[4,4,48,384]{3,2,1,0:T(8,128)(2,1)} %get-tuple-element.248.refs_9_), channel_id=1, source_target_pairs={{0,1},{1,0},{2,3},{3,2},{4,5},{5,4},{6,7},{7,6},{8,9},{9,8},{10,11... | collective-permute-start | bytes 1769480 | tf_op jit(solution)/shard_map/ppermute | solution.py:650
  418.6 12.0 %collective-permute-start.55 = (bf16[4,4,48,384]{3,2,1,0:T(8,128)(2,1)}, bf16[4,4,48,384]{3,2,1,0:T(8,128)(2,1)S(1)}, u32[]{:S(2)}, u32[]{:S(2)}) collective-permute-start(bf16[4,4,48,384]{3,2,1,0:T(8,128)(2,1)} %get-tuple-element.249.refs_10_), channel_id=1, source_target_pairs={{0,1},{1,0},{2,3},{3,2},{4,5},{5,4},{6,7},{7,6},{8,9},{9,8},{10,11... | collective-permute-start | bytes 1769480 | tf_op jit(solution)/shard_map/ppermute | solution.py:650
  418.6 12.0 %collective-permute-start.56 = (bf16[4,4,48,384]{3,2,1,0:T(8,128)(2,1)}, bf16[4,4,48,384]{3,2,1,0:T(8,128)(2,1)}, u32[]{:S(2)}, u32[]{:S(2)}) collective-permute-start(bf16[4,4,48,384]{3,2,1,0:T(8,128)(2,1)} %get-tuple-element.250.refs_11_), channel_id=1, source_target_pairs={{0,1},{1,0},{2,3},{3,2},{4,5},{5,4},{6,7},{7,6},{8,9},{9,8},{10,11... | collective-permute-start | bytes 1769480 | tf_op jit(solution)/shard_map/ppermute | solution.py:650
  421.0 9.6 %collective-permute-start.52 = (bf16[192,768]{1,0:T(8,128)(2,1)}, bf16[192,768]{1,0:T(8,128)(2,1)S(1)}, u32[]{:S(2)}, u32[]{:S(2)}) collective-permute-start(bf16[192,768]{1,0:T(8,128)(2,1)} %get-tuple-element.246.refs_2_), channel_id=1, source_target_pairs={{0,8},{4,12},{8,16},{12,20},{16,24},{20,28},{24,0},{28,4},{1,9},{5... | collective-permute-start | bytes 884744 | tf_op jit(solution)/shard_map/ppermute | solution.py:639
  422.3 46.5 %all-to-all-start.6 = ((bf16[4,128,768]{2,1,0:T(8,128)(2,1)}), bf16[4,128,768]{2,1,0:T(8,128)(2,1)}, u32[]{:S(2)}, u32[]{:S(2)}) async-start(bf16[4,128,768]{2,1,0:T(8,128)(2,1)} %get-tuple-element.269), calls=%async_computation.6 | async-start | bytes 1572864 | tf_op jit(solution)/shard_map/all_to_all | solution.py:655
  430.5 26.8 %collective-permute-start.61 = (bf16[2,192,768]{2,1,0:T(8,128)(2,1)S(1)}, bf16[2,192,768]{2,1,0:T(8,128)(2,1)S(1)}, u32[]{:S(2)}, u32[]{:S(2)}) collective-permute-start(bf16[2,192,768]{2,1,0:T(8,128)(2,1)S(1)} %copy-done.29), channel_id=1, source_target_pairs={{0,8},{4,12},{8,16},{12,20},{16,24},{20,28},{24,0},{28,4},{1,9},{5... | collective-permute-start | bytes 1769480 | tf_op jit(solution)/shard_map/ppermute | solution.py:639
  433.3 46.7 %collective-permute-start.57 = (bf16[4,192,768]{2,1,0:T(8,128)(2,1)S(1)}, bf16[4,192,768]{2,1,0:T(8,128)(2,1)}, u32[]{:S(2)}, u32[]{:S(2)}) collective-permute-start(bf16[4,192,768]{2,1,0:T(8,128)(2,1)S(1)} %pad_maximum_fusion.3.refs_0_), channel_id=1, source_target_pairs={{0,4},{4,0},{8,12},{12,8},{16,20},{20,16},{24,28},{28,24},{1,5},{5... | collective-permute-start | bytes 3538952 | tf_op jit(solution)/shard_map/ppermute | solution.py:645
  434.9 17.0 %collective-permute-start.62 = (f32[5,768]{1,0:T(8,128)S(1)}, f32[5,768]{1,0:T(8,128)S(1)}, u32[]{:S(2)}, u32[]{:S(2)}) collective-permute-start(f32[5,768]{1,0:T(8,128)S(1)} %copy-done.63), channel_id=1, source_target_pairs={{0,8},{4,12},{8,0},{12,4},{16,24},{20,28},{24,16},{28,20},{1,9},{5... | collective-permute-start | bytes 46088 | tf_op jit(solution)/shard_map/ppermute | solution.py:650
  458.2 9.5 %collective-permute-start.63 = (f32[5,768]{1,0:T(8,128)}, f32[5,768]{1,0:T(8,128)S(1)}, u32[]{:S(2)}, u32[]{:S(2)}) collective-permute-start(f32[5,768]{1,0:T(8,128)} %get-tuple-element.284), channel_id=1, source_target_pairs={{0,16},{4,20},{8,24},{12,28},{16,0},{20,4},{24,8},{28,12},{1,17},{... | collective-permute-start | bytes 46088 | tf_op jit(solution)/shard_map/ppermute | solution.py:650
  (88 other events, 473.5 us)
